TPU v7x, 512 devices: a whole 4x8x8 slice. The times are simulated.
512 devices in a mesh: gx: 32 (over y, x), yz: 16 (over z, core).
Axes of the slice: x: 4, y: 8, z: 8, core: 2. Of those that a mesh axis runs over, the one named last changes fastest.
Arguments:
- right_side: float32 [32, 16, 80, 768], P('gx', 'yz'), may hold values from -750 to 750
- face_table: int32 [32, 16, 4, 512], P('gx', 'yz'), may hold values from 0 to 1023, as said below
- send_faces: int32 [32, 16, 2, 128], P('gx', 'yz'), may hold values from 0 to 767, as said below
- stabilize: float32 [32, 16, 512], P('gx', 'yz'), may hold values from 3 to 6
- coupling: float32 [32, 16, 512], P('gx', 'yz'), may hold values from 0.5 to 2
- inverse: float32 [2, 192, 192], replicated, may hold values from -0.4375 to 0.4375
- lifting: float32 [2, 320, 192], replicated, may hold values from -0.3125 to 0.3125
- trace_block: float32 [2, 320, 320], replicated, may hold values from -0.3125 to 0.3125
Outputs:
- solution: float32 [32, 16, 80, 768], P('gx', 'yz')
Inputs may be any that keep to these rules, and one draw needn't show every extreme that they name: `face_table`: on each device every local face 0 to 1023 appears exactly twice. Local faces below 768 are the device's own, the next 128 are the faces in row 0 of send_faces of the previous device along gx, in that order, and the last 128 those in row 1 of the previous device along yz. `send_faces`: on each device the 256 entries are distinct.
All inputs are finite; a program needn't handle non-finite values.
Results may differ from a plain program's by a relative error of at most 0.003.
Values sent between devices are 32-bit elements; how exact they have to be, the bound alone decides.
No kernel may reach another device: no remote copies, remote signals or barrier semaphores. Data moves between devices by JAX's collectives and lax.ppermute only.
A program may use at most 64 MiB of HBM per device.

v0:
```python
import jax
import jax.numpy as jnp
from jax import lax
from jax.sharding import PartitionSpec as P

ITERS = 4


EPSILON = 1e-06


def passed_along(value, axis, steps):
    count = lax.axis_size(axis)
    pairs = [(source, (source + steps) % count) for source in range(count)]
    return lax.ppermute(value, axis, pairs)


def element_apply(extended, element_faces, penalty, scaling, inverse, lifting, trace_block):
    trace_dofs = extended.shape[0]
    elements = element_faces.shape[1]
    shapes = lifting.shape[0]
    group = elements // shapes
    gathered = extended[:, element_faces].reshape(trace_dofs * 4, shapes, group)
    penalty_grid = penalty.reshape(shapes, group)
    scaling_grid = scaling.reshape(shapes, group)
    interior = jnp.einsum("kji,jkn->ikn", lifting, gathered, precision=lax.Precision.HIGHEST)
    solved = (
        jnp.einsum("kmi,mkn->ikn", inverse, interior, precision=lax.Precision.HIGHEST)
        / scaling_grid
    )
    result = penalty_grid * gathered + jnp.einsum(
        "kji,jkn->ikn", trace_block, gathered, precision=lax.Precision.HIGHEST
    )
    result = result - jnp.einsum("kji,ikn->jkn", lifting, solved, precision=lax.Precision.HIGHEST)
    result = result.reshape(trace_dofs, 4, elements)
    return jnp.zeros(extended.shape, jnp.float32).at[:, element_faces].add(result)


def least_squares(hessenberg, target):
    breadth = hessenberg.shape[1]
    unit_columns = []
    triangle = {}
    for k in range(breadth):
        column = hessenberg[:, k]
        for i in range(k):
            triangle[i, k] = jnp.sum(unit_columns[i] * column)
            column = column - triangle[i, k] * unit_columns[i]
        triangle[k, k] = jnp.sqrt(jnp.sum(column * column))
        unit_columns.append(column / triangle[k, k])
    projected = [jnp.sum(vector * target) for vector in unit_columns]
    outcome = [None] * breadth
    for k in reversed(range(breadth)):
        running = projected[k]
        for i in range(k + 1, breadth):
            running = running - triangle[k, i] * outcome[i]
        outcome[k] = running / triangle[k, k]
    return outcome


def send_upward(slab_part, section_part):
    return (passed_along(slab_part, "gx", 1), passed_along(section_part, "yz", 1))


def send_downward(slab_part, section_part):
    return (passed_along(slab_part, "gx", -1), passed_along(section_part, "yz", -1))


def per_device(
    right_side, face_table, send_faces, stabilize, coupling, inverse, lifting, trace_block
):
    source = right_side[0, 0]
    element_faces = face_table[0, 0]
    send_lists = send_faces[0, 0]
    penalty = stabilize[0, 0]
    scaling = coupling[0, 0]
    own_count = source.shape[1]
    shared = send_lists.shape[1]

    def local_dot(first, second):
        return jnp.sum(first * second)

    def global_squares(vector):
        return lax.psum(local_dot(vector, vector), ("gx", "yz"))

    initial_norm = jnp.sqrt(global_squares(source) + EPSILON)
    krylov = [source / initial_norm]
    hessenberg = jnp.zeros((ITERS + 1, ITERS), jnp.float32)
    for j in range(ITERS):
        operator_vector = krylov[j]
        slab_ghost, section_ghost = send_upward(
            operator_vector[:, send_lists[0]], operator_vector[:, send_lists[1]]
        )
        summed = element_apply(
            jnp.concatenate([operator_vector, slab_ghost, section_ghost], axis=1),
            element_faces,
            penalty,
            scaling,
            inverse,
            lifting,
            trace_block,
        )
        from_slab, from_section = send_downward(
            summed[:, own_count : own_count + shared], summed[:, own_count + shared :]
        )
        fresh = (
            summed[:, :own_count]
            .at[:, send_lists[0]]
            .add(from_slab)
            .at[:, send_lists[1]]
            .add(from_section)
        )
        collected = []
        for i in range(j + 1):
            projection = lax.psum(local_dot(krylov[i], fresh), ("gx", "yz"))
            fresh = fresh - projection * krylov[i]
            collected.append(projection)
        products = jnp.stack(collected)
        subdiag = jnp.sqrt(global_squares(fresh) + EPSILON)
        hessenberg = hessenberg.at[: j + 1, j].set(products).at[j + 1, j].set(subdiag)
        krylov.append(fresh / subdiag)
    target = jnp.zeros((ITERS + 1,), jnp.float32).at[0].set(initial_norm)
    combine = least_squares(hessenberg, target)
    solution = combine[0] * krylov[0]
    for j in range(1, ITERS):
        solution = solution + combine[j] * krylov[j]
    return solution[None, None]


def solution(mesh):
    return jax.shard_map(
        per_device,
        mesh=mesh,
        in_specs=(
            P("gx", "yz", None, None),
            P("gx", "yz", None, None),
            P("gx", "yz", None, None),
            P("gx", "yz", None),
            P("gx", "yz", None),
            P(),
            P(),
            P(),
        ),
        out_specs=P("gx", "yz", None, None),
        check_vma=False,
    )
```

profile of v0, /device:TPU:1, one launch (start us, length us, event | category | flops | bytes accessed | tf_op | source)
XLA Modules:
  0.0 1726.8 jit_solution(5703982664234155574)
XLA Ops:
  0.0 1.7 multiply_reduce_fusion.14
  1.9 106.1 %psum.105 = f32[]{:T(128)} all-reduce(f32[]{:T(128)} %multiply_reduce_fusion.14), channel_id=1, replica_groups=mesh['gx'=32,'yz'=16] {'gx','yz'}, use_global_device_ids=true, to_apply=%region_1.0 | all-reduce | flops 1 | bytes 8 | tf_op jit(solution)/shard_map/psum | solution.py:83
  110.6 2.5 collective-permute-start
  117.1 1.8 collective-permute-done
  119.0 7.6 gather_fusion.2
  130.9 2.0 fusion.4
  137.6 12.0 scatter_custom_fusion
  149.6 4.3 collective-permute-start.2
  154.0 2.8 collective-permute-start.3
  156.8 2.0 scatter_custom_fusion.1
  161.0 98.5 %psum.106 = f32[]{:T(128)} all-reduce(f32[]{:T(128)} %multiply_reduce_fusion.13), channel_id=1, replica_groups=mesh['gx'=32,'yz'=16] {'gx','yz'}, use_global_device_ids=true, to_apply=%region_6.0 | all-reduce | flops 1 | bytes 8 | tf_op jit(solution)/shard_map/psum | solution.py:114
  260.8 93.8 %psum.107 = f32[]{:T(128)} all-reduce(f32[]{:T(128)} %multiply_reduce_fusion.12), channel_id=1, replica_groups=mesh['gx'=32,'yz'=16] {'gx','yz'}, use_global_device_ids=true, to_apply=%region_8.0 | all-reduce | flops 1 | bytes 8 | tf_op jit(solution)/shard_map/psum | solution.py:83
  357.2 3.7 collective-permute-start.4
  362.0 3.6 collective-permute-done.4
  365.6 7.6 gather_fusion.5
  373.2 2.4 copy.22
  378.9 2.0 fusion.5
  385.1 2.4 copy.46
  387.6 11.9 scatter_custom_fusion.3
  399.5 2.7 collective-permute-start.6
  402.2 3.8 collective-permute-start.7
  410.9 97.2 %psum.108 = f32[]{:T(128)} all-reduce(f32[]{:T(128)} %multiply_reduce_fusion.11), channel_id=1, replica_groups=mesh['gx'=32,'yz'=16] {'gx','yz'}, use_global_device_ids=true, to_apply=%region_14.0 | all-reduce | flops 1 | bytes 8 | tf_op jit(solution)/shard_map/psum | solution.py:114
  510.2 94.8 %psum.109 = f32[]{:T(128)} all-reduce(f32[]{:T(128)} %multiply_reduce_fusion.10), channel_id=1, replica_groups=mesh['gx'=32,'yz'=16] {'gx','yz'}, use_global_device_ids=true, to_apply=%region_16.0 | all-reduce | flops 1 | bytes 8 | tf_op jit(solution)/shard_map/psum | solution.py:114
  605.0 2.0 multiply_reduce_fusion.9
  607.0 95.4 %psum.110 = f32[]{:T(128)} all-reduce(f32[]{:T(128)} %get-tuple-element.135), channel_id=1, replica_groups=mesh['gx'=32,'yz'=16] {'gx','yz'}, use_global_device_ids=true, to_apply=%region_18.0 | all-reduce | flops 1 | bytes 8 | tf_op jit(solution)/shard_map/psum | solution.py:83
  704.6 2.7 collective-permute-start.8
  707.4 2.3 collective-permute-start.9
  710.4 2.6 collective-permute-done.8
  714.0 7.6 gather_fusion.8
  721.6 2.4 copy.28
  724.0 1.6 reshape.401
  727.2 2.0 fusion.6
  733.5 2.4 copy.47
  735.9 11.9 scatter_custom_fusion.6
  747.9 1.8 collective-permute-start.11
  749.7 4.3 collective-permute-start.10
  759.6 98.9 %psum.111 = f32[]{:T(128)} all-reduce(f32[]{:T(128)} %multiply_reduce_fusion.8), channel_id=1, replica_groups=mesh['gx'=32,'yz'=16] {'gx','yz'}, use_global_device_ids=true, to_apply=%region_24.0 | all-reduce | flops 1 | bytes 8 | tf_op jit(solution)/shard_map/psum | solution.py:114
  860.4 94.8 %psum.112 = f32[]{:T(128)} all-reduce(f32[]{:T(128)} %multiply_reduce_fusion.7), channel_id=1, replica_groups=mesh['gx'=32,'yz'=16] {'gx','yz'}, use_global_device_ids=true, to_apply=%region_26.0 | all-reduce | flops 1 | bytes 8 | tf_op jit(solution)/shard_map/psum | solution.py:114
  955.2 2.0 multiply_reduce_fusion.6
  957.2 95.6 %psum.113 = f32[]{:T(128)} all-reduce(f32[]{:T(128)} %get-tuple-element.133), channel_id=1, replica_groups=mesh['gx'=32,'yz'=16] {'gx','yz'}, use_global_device_ids=true, to_apply=%region_28.0 | all-reduce | flops 1 | bytes 8 | tf_op jit(solution)/shard_map/psum | solution.py:114
  1054.8 95.4 %psum.114 = f32[]{:T(128)} all-reduce(f32[]{:T(128)} %multiply_reduce_fusion.5), channel_id=1, replica_groups=mesh['gx'=32,'yz'=16] {'gx','yz'}, use_global_device_ids=true, to_apply=%region_30.0 | all-reduce | flops 1 | bytes 8 | tf_op jit(solution)/shard_map/psum | solution.py:83
  1153.0 3.7 collective-permute-start.12
  1156.7 2.3 collective-permute-start.13
  1162.4 7.6 gather_fusion.11
  1170.0 2.4 copy.34
  1172.4 1.6 reshape.407
  1175.6 2.0 fusion.7
  1182.4 11.9 scatter_custom_fusion.9
  1194.4 1.8 collective-permute-start.15
  1196.2 4.3 collective-permute-start.14
  1200.5 3.2 broadcast_select_fusion.2
  1209.1 95.9 %psum.115 = f32[]{:T(128)} all-reduce(f32[]{:T(128)} %multiply_reduce_fusion.4), channel_id=1, replica_groups=mesh['gx'=32,'yz'=16] {'gx','yz'}, use_global_device_ids=true, to_apply=%region_36.0 | all-reduce | flops 1 | bytes 8 | tf_op jit(solution)/shard_map/psum | solution.py:114
  1306.4 3.7 broadcast_select_fusion.1
  1310.1 94.9 %psum.116 = f32[]{:T(128)} all-reduce(f32[]{:T(128)} %multiply_reduce_fusion.3), channel_id=1, replica_groups=mesh['gx'=32,'yz'=16] {'gx','yz'}, use_global_device_ids=true, to_apply=%region_38.0 | all-reduce | flops 1 | bytes 8 | tf_op jit(solution)/shard_map/psum | solution.py:114
  1405.0 2.0 multiply_reduce_fusion.2
  1407.1 95.6 %psum.117 = f32[]{:T(128)} all-reduce(f32[]{:T(128)} %get-tuple-element.131), channel_id=1, replica_groups=mesh['gx'=32,'yz'=16] {'gx','yz'}, use_global_device_ids=true, to_apply=%region_40.0 | all-reduce | flops 1 | bytes 8 | tf_op jit(solution)/shard_map/psum | solution.py:114
  1505.3 95.8 %psum.118 = f32[]{:T(128)} all-reduce(f32[]{:T(128)} %multiply_reduce_fusion.1), channel_id=1, replica_groups=mesh['gx'=32,'yz'=16] {'gx','yz'}, use_global_device_ids=true, to_apply=%region_42.0 | all-reduce | flops 1 | bytes 8 | tf_op jit(solution)/shard_map/psum | solution.py:114
  1601.1 2.0 multiply_reduce_fusion
  1603.2 95.8 %psum.119 = f32[]{:T(128)} all-reduce(f32[]{:T(128)} %multiply_reduce_fusion), channel_id=1, replica_groups=mesh['gx'=32,'yz'=16] {'gx','yz'}, use_global_device_ids=true, to_apply=%region_44.0 | all-reduce | flops 1 | bytes 8 | tf_op jit(solution)/shard_map/psum | solution.py:83
  1699.8 4.4 broadcast_select_fusion
  1709.8 2.0 multiply_reduce_fusion.20
  1711.8 1.9 multiply_reduce_fusion.17
  1714.4 1.9 multiply_reduce_fusion.21
  1716.3 1.8 multiply_reduce_fusion.15
  (169 shorter events, 81.5 us)
Async XLA Ops:
  0.0 130.8 %copy-start = (f32[2,320,320]{2,1,0:T(8,128)S(1)}, f32[2,320,320]{2,1,0:T(8,128)}, u32[]{:S(2)}) copy-start(f32[2,320,320]{2,1,0:T(8,128)} %param.33) | copy-start | bytes 2457604
  0.0 1.7 copy-start.7
  108.7 0.7 copy-start.20
  109.4 0.6 copy-start.17
  109.4 0.6 copy-start.18
  109.9 3.2 copy-start.9
  110.6 8.3 collective-permute-start
  113.1 1.4 copy-start.10
  113.8 5.2 collective-permute-start.1
  114.5 0.7 copy-start.11
  114.5 23.1 %copy-start.8 = (s32[1,4,4,128]{3,1,2,0:T(4,128)}, s32[1,4,4,128]{3,1,2,0:T(4,128)S(1)}, u32[]{:S(2)}) copy-start(s32[1,4,4,128]{3,1,2,0:T(4,128)S(1)} %copy.49) | copy-start | bytes 24580
  115.8 0.7 copy-start.12
  117.1 15.7 copy-start.13
  128.2 1.1 copy-start.1
  130.8 2.0 copy-start.21
  149.6 7.1 collective-permute-start.2
  154.0 4.8 collective-permute-start.3
  357.2 8.3 collective-permute-start.4
  360.9 4.6 collective-permute-start.5
  378.8 2.0 copy-start.14
  378.8 2.0 copy-start.22
  399.5 2.7 copy-start.6
  399.5 7.5 collective-permute-start.6
  402.2 6.3 collective-permute-start.7
  508.1 1.5 copy-start.26
  703.2 9.8 copy-start.4
  704.6 5.1 copy-start.25
  704.6 8.3 collective-permute-start.8
  707.4 5.6 collective-permute-start.9
  727.2 2.0 copy-start.15
  727.2 2.0 copy-start.23
  747.9 6.2 copy-start.5
  747.9 9.4 collective-permute-start.11
  749.7 6.0 collective-permute-start.10
  1151.6 9.8 copy-start.2
  1153.0 6.0 copy-start.19
  1153.0 8.3 collective-permute-start.12
  1156.7 4.6 collective-permute-start.13
  1175.6 2.0 copy-start.16
  1175.6 2.0 copy-start.24
  1194.4 12.3 collective-permute-start.15
  1196.2 8.9 collective-permute-start.14
  1405.0 97.6 %copy-start.3 = (f32[80,768]{0,1:T(8,128)S(1)}, f32[80,768]{0,1:T(8,128)}, u32[]{:S(2)}) copy-start(f32[80,768]{0,1:T(8,128)} %copy-done.2) | copy-start | bytes 737284
where the time goes:
time: 1740 us; the launch traced here: 1730 us
  blocking collectives  1450 us (83%)
  other arithmetic  111 us (6%)
  local copies, waits for them, and re-layouts  77.5 us (4%)
  starting transfers between devices  44.8 us (3%)
  matrix products  23.1 us (1%)
    psum x10, blocking collectives, per_device(): projection = lax.psum(local_dot(krylov[i], fresh), ('gx', 'yz'))  962 us
    psum x5, blocking collectives, global_squares(): return lax.psum(local_dot(vector, vector), ('gx', 'yz'))  487 us
    scatter-add x4, other arithmetic, element_apply(): jnp.zeros(extended.shape, jnp.float32).at[:, element_faces].add(result)  47.8 us
    ppermute x16, starting transfers between devices, passed_along(): return lax.ppermute(value, axis, pairs)  44.8 us
    gather x8, local copies, waits for them, and re-layouts, element_apply(): gathered = extended[:, element_faces].reshape(trace_dofs * 4, shapes, group)  39.3 us
  transfers between devices with their start and end apart: 16, of which 4 were waited for; matrix products, arithmetic and copies ran while one was open for 1% of the time, Pallas kernels for 0%

commit v1 on v0

v1 whole, which is shorter than its diff:
```python
import functools

import jax
import jax.numpy as jnp
from jax import lax
from jax.experimental import pallas as pl
from jax.experimental.pallas import tpu as pltpu
from jax.sharding import PartitionSpec as P

ITERS = 4
EPSILON = 1e-06
SHIFT = 12.0
NORM_ROOM = 1024.0
F32 = jnp.float32
BF16 = jnp.bfloat16
PAIRS = [(i, j) for j in range(ITERS + 1) for i in range(j + 1)]
VMEM_BYTES = 40 * 1024 * 1024


def halves(value):
    high = value.astype(BF16)
    return high, (value - high.astype(F32)).astype(BF16)


def stacked(value):
    return jnp.concatenate(halves(value), axis=0)


def folded(value):
    half = value.shape[0] // 2
    return value[:half] + value[half:]


def dot(first, second):
    return jnp.dot(first, second, preferred_element_type=F32)


def dot_last(first, second, precision=None):
    return lax.dot_general(
        first, second, (((1,), (1,)), ((), ())), preferred_element_type=F32, precision=precision
    )


def first_kernel(source_ref, send_ref, pick_ref, slab_ref, section_ref):
    owned = source_ref.shape[1]
    shared = send_ref.shape[1]
    faces = lax.broadcasted_iota(jnp.int32, (owned, shared), 0)
    for row in range(2):
        pick_ref[:, row * shared : (row + 1) * shared] = jnp.where(
            faces == send_ref[row : row + 1, :], 1.0, 0.0
        ).astype(BF16)
    sent = folded(dot(stacked(source_ref[...]), pick_ref[...]))
    slab_ref[...] = sent[:, :shared]
    section_ref[...] = sent[:, shared:]


def prepare_kernel(
    table_ref, inverse_ref, lifting_ref, block_ref, select_ref, weight_ref, scale_ref
):
    faces = select_ref.shape[0]
    elements = table_ref.shape[1]
    trace = block_ref.shape[1]
    shapes = block_ref.shape[0]
    dofs = trace // 4
    ids = lax.broadcasted_iota(jnp.int32, (faces, elements), 0)
    for k in range(4):
        select_ref[:, k * elements : (k + 1) * elements] = jnp.where(
            ids == table_ref[k : k + 1, :], 1.0, 0.0
        ).astype(BF16)
    place = lax.broadcasted_iota(jnp.int32, (trace, trace), 0)
    k = sum(jnp.where(place >= m * dofs, 1, 0) for m in range(1, 4))
    order = jnp.where(
        lax.broadcasted_iota(jnp.int32, (trace, trace), 1) == (place - k * dofs) * 4 + k, 1.0, 0.0
    )
    highest = lax.Precision.HIGHEST
    block_bound = jnp.zeros((1, 1), F32)
    inner_bound = jnp.zeros((1, 1), F32)
    for t in range(shapes):
        lifted = jnp.dot(order, lifting_ref[t], preferred_element_type=F32, precision=highest)
        inner = dot_last(dot_last(lifted, inverse_ref[t], highest), lifted, highest)
        block = dot_last(dot_last(order, block_ref[t], highest), order, highest)
        block_bound = jnp.maximum(block_bound, jnp.sum(block * block, keepdims=True))
        inner_bound = jnp.maximum(inner_bound, jnp.sum(inner * inner, keepdims=True))
        high, low = halves(jnp.concatenate([block, inner], axis=0))
        weight_ref[t] = jnp.concatenate([high, high, low], axis=1)
    bound = 4.0 * (6.0 + jnp.sqrt(block_bound) + 2.0 * jnp.sqrt(inner_bound)) + SHIFT
    scale_ref[...] = jnp.broadcast_to(
        jnp.maximum(1.0, bound * (1.0 / NORM_ROOM)), scale_ref.shape
    )


def inner_products(vectors, last, gram_ref, first_row):
    for i, vector in enumerate(vectors):
        gram_ref[first_row + i : first_row + i + 1, :] = lane_sums(vector * last)


def lane_sums(product):
    total = product[:, :128]
    for start in range(128, product.shape[1], 128):
        total = total + product[:, start : start + 128]
    return jnp.sum(total, axis=0, keepdims=True)


def apply_kernel(first, final, earlier, *refs):
    refs = list(refs)
    own_ref = refs.pop(0)
    ghosts = [refs.pop(0) for _ in range(2)]
    if not first:
        down = [refs.pop(0) for _ in range(2)]
        back = [refs.pop(0) for _ in range(2)]
    vectors = [refs.pop(0) for _ in range(earlier)]
    select_ref, weight_ref, pick_ref, stabilize_ref, coupling_ref, scale_ref = refs[:6]
    refs = refs[6:]
    if not first:
        vector_ref = refs.pop(0)
    gram_ref = refs.pop(0)
    part_ref = refs.pop(0)
    down_out = [refs.pop(0) for _ in range(2)]
    if not final:
        up_out = [refs.pop(0) for _ in range(2)]
    wide_ref, result_ref = refs

    dofs, owned = own_ref.shape
    shared = ghosts[0].shape[1]
    shapes = weight_ref.shape[0]
    elements = stabilize_ref.shape[1]
    group = elements // shapes
    trace = 4 * dofs

    if first:
        vector = own_ref[...]
        ghost = jnp.concatenate([ref[...] for ref in ghosts], axis=1)
    else:
        received = jnp.concatenate([ref[...] for ref in back], axis=1)
        vector = own_ref[...] + folded(dot_last(stacked(received), pick_ref[...]))
        vector_ref[...] = vector
        ghost = jnp.concatenate([a[...] + b[...] for a, b in zip(ghosts, down)], axis=1)
    extended = jnp.concatenate([vector, ghost], axis=1)
    wide_ref[...] = stacked(extended)

    for t in range(shapes):
        columns = slice(t * group, (t + 1) * group)
        picked = []
        for k in range(4):
            start = k * elements + t * group
            picked.append(dot(wide_ref[...], select_ref[:, start : start + group]))
        high = jnp.concatenate([p[:dofs] for p in picked], axis=0)
        low = jnp.concatenate([p[dofs:] for p in picked], axis=0)
        high16, low16 = high.astype(BF16), low.astype(BF16)
        product = dot(weight_ref[t], jnp.concatenate([high16, low16, high16], axis=0))
        result = (
            stabilize_ref[:, columns] * (high + low)
            + product[:trace]
            - product[trace:] / coupling_ref[:, columns]
        )
        for k in range(4):
            start = k * elements + t * group
            result_ref[:, start : start + group] = stacked(result[k * dofs : (k + 1) * dofs])
    inner_products([ref[...] for ref in vectors] + [vector], vector, gram_ref, 0)
    gram_ref[earlier + 1 :, :] = jnp.zeros((8 - earlier - 1, 128), F32)
    shrink = 1.0 / scale_ref[:, :1]
    summed = folded(dot_last(result_ref[...], select_ref[...])) * shrink
    part = summed[:, :owned] - (SHIFT * shrink) * vector
    part_ref[...] = part
    for i in range(2):
        down_out[i][...] = summed[:, owned + i * shared : owned + (i + 1) * shared]
    if not final:
        sent = folded(dot(stacked(part), pick_ref[...]))
        for i in range(2):
            up_out[i][...] = sent[:, i * shared : (i + 1) * shared]


def last_kernel(*refs):
    own_ref, slab_ref, section_ref = refs[:3]
    vectors = refs[3 : 3 + ITERS]
    grams = refs[3 + ITERS : 3 + 2 * ITERS]
    pick_ref, row_ref, sums_ref = refs[3 + 2 * ITERS :]
    received = jnp.concatenate([slab_ref[...], section_ref[...]], axis=1)
    vector = own_ref[...] + folded(dot_last(stacked(received), pick_ref[...]))
    sums_ref[...] = jnp.zeros(sums_ref.shape, F32)
    for j in range(ITERS):
        start = j * (j + 1) // 2
        sums_ref[start : start + j + 1, :] = grams[j][: j + 1, :]
    inner_products([ref[...] for ref in vectors] + [vector], vector, sums_ref, ITERS * (ITERS + 1) // 2)
    totals = jnp.sum(sums_ref[...], axis=1, keepdims=True)
    count = sums_ref.shape[0]
    diagonal = lax.broadcasted_iota(jnp.int32, (count, 128), 0) == lax.broadcasted_iota(
        jnp.int32, (count, 128), 1
    )
    row = jnp.sum(jnp.where(diagonal, totals, 0.0), axis=0, keepdims=True)
    row_ref[...] = jnp.broadcast_to(row, row_ref.shape)


def least_squares(hessenberg, target):
    breadth = len(hessenberg)
    height = len(target)
    unit_columns = []
    triangle = {}
    for k in range(breadth):
        column = list(hessenberg[k])
        for i in range(k):
            triangle[i, k] = sum(unit_columns[i][r] * column[r] for r in range(height))
            column = [column[r] - triangle[i, k] * unit_columns[i][r] for r in range(height)]
        triangle[k, k] = jnp.sqrt(sum(c * c for c in column))
        unit_columns.append([c / triangle[k, k] for c in column])
    projected = [sum(v[r] * target[r] for r in range(height)) for v in unit_columns]
    outcome = [None] * breadth
    for k in reversed(range(breadth)):
        running = projected[k]
        for i in range(k + 1, breadth):
            running = running - triangle[k, i] * outcome[i]
        outcome[k] = running / triangle[k, k]
    return outcome


def coefficients(gram, scale):
    size = ITERS + 1
    zero = jnp.zeros_like(scale)

    def inner(a, b):
        total = zero
        for i in range(size):
            for j in range(size):
                if a[i] is not None and b[j] is not None:
                    total = total + a[i] * b[j] * gram[i][j]
        return total

    def plus(a, factor, b):
        out = []
        for x, y in zip(a, b):
            if y is None:
                out.append(x)
            else:
                out.append(factor * y if x is None else x + factor * y)
        return out

    initial_norm = jnp.sqrt(gram[0][0] + EPSILON)
    krylov = [[1.0 / initial_norm] + [None] * ITERS]
    columns = []
    for j in range(ITERS):
        shifted = [None] + [scale * c if c is not None else None for c in krylov[j][:-1]]
        fresh = plus(shifted, SHIFT, krylov[j])
        products = [inner(vector, fresh) for vector in krylov]
        for value, vector in zip(products, krylov):
            fresh = plus(fresh, -value, vector)
        subdiag = jnp.sqrt(jnp.maximum(inner(fresh, fresh), 0.0) + EPSILON)
        columns.append(products + [subdiag] + [zero] * (ITERS - 1 - j))
        krylov.append([c / subdiag if c is not None else None for c in fresh])
    combine = least_squares(columns, [initial_norm] + [zero] * ITERS)
    total = [None] * size
    for y, vector in zip(combine, krylov):
        total = plus(total, y, vector)
    return total[:ITERS]


def solve_kernel(rows_ref, scale_ref, *refs):
    vectors = refs[:ITERS]
    out_ref = refs[ITERS]
    sums = jnp.sum(rows_ref[...], axis=0, keepdims=True)
    gram = [[None] * (ITERS + 1) for _ in range(ITERS + 1)]
    for p, (i, j) in enumerate(PAIRS):
        gram[i][j] = gram[j][i] = sums[:, p : p + 1]
    weights = coefficients(gram, scale_ref[:, :1])
    total = weights[0] * vectors[0][...]
    for weight, ref in zip(weights[1:], vectors[1:]):
        total = total + weight * ref[...]
    out_ref[...] = total


def passed_along(value, axis, steps):
    count = lax.axis_size(axis)
    pairs = [(source, (source + steps) % count) for source in range(count)]
    return lax.ppermute(value, axis, pairs)


def shape(*dims, dtype=F32):
    return jax.ShapeDtypeStruct(dims, dtype)


def call(kernel, out_shape, *args, scratch=(), flops=0, name=None):
    return pl.pallas_call(
        kernel,
        out_shape=out_shape,
        in_specs=[pl.BlockSpec(memory_space=pltpu.VMEM)] * len(args),
        out_specs=jax.tree.map(lambda _: pl.BlockSpec(memory_space=pltpu.VMEM), out_shape),
        scratch_shapes=list(scratch),
        cost_estimate=pl.CostEstimate(flops=flops, bytes_accessed=4 * 1024 * 1024, transcendentals=0),
        compiler_params=pltpu.CompilerParams(vmem_limit_bytes=VMEM_BYTES),
        name=name,
    )(*args)


def per_device(
    right_side, face_table, send_faces, stabilize, coupling, inverse, lifting, trace_block
):
    source = right_side[0, 0]
    table = face_table[0, 0]
    send_lists = send_faces[0, 0]
    penalty = stabilize[0]
    scaling = coupling[0]
    dofs, owned = source.shape
    elements = table.shape[1]
    shared = send_lists.shape[1]
    faces = owned + 2 * shared
    shapes, trace, _ = lifting.shape
    devices = lax.axis_size("gx") * lax.axis_size("yz")
    part = shape(dofs, shared)

    pick, slab, section = call(
        first_kernel, (shape(owned, 2 * shared, dtype=BF16), part, part), source, send_lists, name="first"
    )
    ghosts = [passed_along(slab, "gx", 1), passed_along(section, "yz", 1)]
    select, weights, scale = call(
        prepare_kernel,
        (
            shape(faces, 4 * elements, dtype=BF16),
            shape(shapes, 2 * trace, 3 * trace, dtype=BF16),
            shape(1, 128),
        ),
        table,
        inverse,
        lifting,
        trace_block,
        flops=2 * 10**9,
        name="prepare",
    )
    vectors = [source]
    grams = []
    own, exchanged = source, ghosts
    for j in range(ITERS):
        final = j == ITERS - 1
        outs = [shape(8, 128), shape(dofs, owned), part, part]
        if j:
            outs = [shape(dofs, owned)] + outs
        if not final:
            outs = outs + [part, part]
        earlier = vectors[:j] if j else []
        results = call(
            functools.partial(apply_kernel, j == 0, final, len(earlier)),
            tuple(outs),
            own,
            *exchanged,
            *earlier,
            select,
            weights,
            pick,
            penalty,
            scaling,
            scale,
            scratch=[pltpu.VMEM((2 * dofs, faces), BF16), pltpu.VMEM((2 * dofs, 4 * elements), BF16)],
            flops=2 * 10**9,
            name=f"apply{j}",
        )
        results = list(results)
        if j:
            vectors.append(results.pop(0))
        grams.append(results.pop(0))
        own = results.pop(0)
        down = [results.pop(0) for _ in range(2)]
        back = [passed_along(down[0], "gx", -1), passed_along(down[1], "yz", -1)]
        if final:
            exchanged = back
        else:
            up = [passed_along(results.pop(0), "gx", 1), passed_along(results.pop(0), "yz", 1)]
            exchanged = up + down + back
    rows = call(
        last_kernel, shape(devices, 128), own, *exchanged, *vectors, *grams, pick, scratch=[pltpu.VMEM((16, 128), F32)],
        name="last",
    )
    rows = lax.all_to_all(rows.reshape(devices, 1, 128), ("gx", "yz"), 0, 0).reshape(devices, 128)
    solution = call(solve_kernel, shape(dofs, owned), rows, scale, *vectors, name="solve")
    return solution[None, None]


def solution(mesh):
    return jax.shard_map(
        per_device,
        mesh=mesh,
        in_specs=(
            P("gx", "yz", None, None),
            P("gx", "yz", None, None),
            P("gx", "yz", None, None),
            P("gx", "yz", None),
            P("gx", "yz", None),
            P(),
            P(),
            P(),
        ),
        out_specs=P("gx", "yz", None, None),
        check_vma=False,
    )
```

time: 1740 us -> 125 us (0.07)
  blocking collectives: 1450 us -> 34.3 us
  other arithmetic: 111 us -> 0 us
  local copies, waits for them, and re-layouts: 77.5 us -> 5.84 us
  Pallas kernels: 0 us -> 27.2 us
  matrix products: 23.1 us -> 0 us
    psum x15 -> x0, blocking collectives: 1450 us -> none  [the longest x10 962 us: per_device(): projection = lax.psum(local_dot(krylov[i], fresh), ('gx', 'yz'))]
    scatter-add x12 -> x0, other arithmetic: 60.6 us -> none  [the longest x4 47.8 us: element_apply(): jnp.zeros(extended.shape, jnp.float32).at[:, element_faces].add(result)]
    gather x16 -> x0, local copies, waits for them, and re-layouts: 44.8 us -> none  [the longest x8 39.3 us: element_apply(): gathered = extended[:, element_faces].reshape(trace_dofs * 4, shapes, group)]
    all_to_all x0 -> x1, blocking collectives: none -> 34.3 us  [per_device(): lax.all_to_all(rows.reshape(devices, 1, 128), ('gx', 'yz'), 0, 0)]
    reduce_sum x23 -> x0, other arithmetic: 31.6 us -> none  [the longest x15 20.8 us: local_dot(): return jnp.sum(first * second)]
    pallas_call x0 -> x8, Pallas kernels: none -> 27.2 us  [call(): pl.pallas_call(kernel, out_shape=out_shape, in_specs=[pl.BlockSpec(memory...]
    dot_general x16 -> x0, matrix products: 23.1 us -> none  [the longest x4 8.01 us: element_apply(): jnp.einsum('kji,jkn->ikn', trace_block, gathered, precision=lax.Precision...]
  transfers between devices with their start and end apart: 16 -> 16, of which waited for: 4 -> 4; matrix products, arithmetic and copies ran while one was open for 1% -> 1% of each run, Pallas kernels for 0% -> 8%
where the time goes in v1:
time: 125 us; the launch traced here: 124 us
  starting transfers between devices  51.8 us (41%)
  blocking collectives  34.3 us (27%)
  Pallas kernels  27.2 us (22%)
  local copies, waits for them, and re-layouts  5.84 us (5%)
  waiting for transfers between devices  4.92 us (4%)
    ppermute x16, starting transfers between devices, passed_along(): return lax.ppermute(value, axis, pairs)  51.8 us
    all_to_all x1, blocking collectives, per_device(): lax.all_to_all(rows.reshape(devices, 1, 128), ('gx', 'yz'), 0, 0)  34.3 us
    pallas_call x8, Pallas kernels, call(): pl.pallas_call(kernel, out_shape=out_shape, in_specs=[pl.BlockSpec(memory...  27.2 us
    unnamed x17, local copies, waits for them, and re-layouts  5.84 us
    ppermute x16, waiting for transfers between devices, passed_along(): return lax.ppermute(value, axis, pairs)  4.92 us
  transfers between devices with their start and end apart: 16, of which 4 were waited for; matrix products, arithmetic and copies ran while one was open for 1% of the time, Pallas kernels for 8%

profile of v1, /device:TPU:1, one launch (start us, length us, event | category | flops | bytes accessed | tf_op | source)
XLA Modules:
  0.0 124.2 jit_solution(14971556118709059337)
XLA Ops:
  0.0 0.0 copy-start
  0.0 0.9 copy-done
  0.9 0.0 copy-start.4
  0.9 0.7 copy-done.4
  1.6 0.3 first.1
  1.9 3.9 %collective-permute-start = (f32[80,128]{1,0:T(8,128)S(1)}, f32[80,128]{1,0:T(8,128)S(1)}, u32[]{:S(2)}, u32[]{:S(2)}) collective-permute-start(f32[80,128]{1,0:T(8,128)S(1)} %get-tuple-element.36), channel_id=1, source_target_pairs={{0,16},{16,32},{32,48},{48,64},{64,80},{80,96},{96,112},{112,128},... | collective-permute-start | bytes 122888 | tf_op jit(solution)/shard_map/ppermute | solution.py:273
  5.9 0.0 copy-start.1
  5.9 0.0 copy-start.2
  5.9 0.0 copy-start.3
  5.9 2.9 %collective-permute-start.1 = (f32[80,128]{1,0:T(8,128)S(1)}, f32[80,128]{1,0:T(8,128)S(1)}, u32[]{:S(2)}, u32[]{:S(2)}) collective-permute-start(f32[80,128]{1,0:T(8,128)S(1)} %get-tuple-element.37), channel_id=1, source_target_pairs={{0,1},{1,2},{2,3},{3,4},{4,5},{5,6},{6,7},{7,8},{8,9},{9,10},{10,1... | collective-permute-start | bytes 122888 | tf_op jit(solution)/shard_map/ppermute | solution.py:273
  8.9 1.3 %copy.10.lifting_ref = f32[2,320,192]{2,1,0:T(8,128)S(1)} copy(f32[2,320,192]{1,2,0:T(8,128)} %param.14) | data formatting | bytes 983040 | tf_op args[6]
  10.2 0.0 copy-start.5
  10.2 1.2 copy-done.5
  11.4 0.0 copy-start.6
  11.4 1.0 copy-done.6
  12.4 0.0 copy-start.7
  12.4 0.7 copy-done.7
  13.1 10.0 %prepare.1 = (bf16[1024,2048]{1,0:T(8,128)(2,1)S(1)}, bf16[2,640,960]{2,1,0:T(8,128)(2,1)S(1)}, f32[1,128]{1,0:T(1,128)S(1)}) custom-call(s32[4,512]{1,0:T(4,128)S(1)} %bitcast.28, f32[2,192,192]{2,1,0:T(8,128)S(1)} %copy-done.6, f32[2,320,192]{2,1,0:T(8,128)S(1)} %copy.10.lifting_ref, f32[2,320,320]{2,1,0:T(8,128)S(1)} %copy-done.5), custom_call_target="tpu_custom_call" | custom-call | flops 2000000000 | bytes 4194304 | tf_op jit(solution)/shard_map/prepare/pallas_call | solution.py:281
  23.1 0.0 collective-permute-done.refs_1_
  23.1 0.0 collective-permute-done.1.refs_2_
  23.2 0.0 copy-done.1
  23.2 0.0 copy-done.2
  23.2 0.0 copy-done.3
  23.2 3.5 %apply0.1 = (f32[8,128]{1,0:T(8,128)S(1)}, f32[80,768]{1,0:T(8,128)S(1)}, f32[80,128]{1,0:T(8,128)S(1)}, f32[80,128]{1,0:T(8,128)S(1)}, f32[80,128]{1,0:T(8,128)S(1)}, /*index=5*/f32[80,128]{1,0:T(8,128)S(1)}) custom-call(f32[80,768]{1,0:T(8,128)S(1)} %bitcast.11, f32[80,128]{1,0:T(8,128)S(1)} %collective-permute-done.refs_1_, ...), custom_call_target="tpu_custom_call" | custom-call | flops 2000000000 | bytes 4194304 | tf_op jit(solution)/shard_map/apply0/pallas_call | solution.py:281
  26.7 3.1 %collective-permute-start.2 = (f32[80,128]{1,0:T(8,128)S(1)}, f32[80,128]{1,0:T(8,128)S(1)}, u32[]{:S(2)}, u32[]{:S(2)}) collective-permute-start(f32[80,128]{1,0:T(8,128)S(1)} %get-tuple-element.43), channel_id=1, source_target_pairs={{0,16},{16,32},{32,48},{48,64},{64,80},{80,96},{96,112},{112,128},... | collective-permute-start | bytes 122888 | tf_op jit(solution)/shard_map/ppermute | solution.py:273
  29.9 0.4 collective-permute-start.3
  30.3 5.6 %collective-permute-start.4 = (f32[80,128]{1,0:T(8,128)S(1)}, f32[80,128]{1,0:T(8,128)S(1)}, u32[]{:S(2)}, u32[]{:S(2)}) collective-permute-start(f32[80,128]{1,0:T(8,128)S(1)} %get-tuple-element.45.refs_3_), channel_id=1, source_target_pairs={{0,496},{16,0},{32,16},{48,32},{64,48},{80,64},{96,80},{112,96},{1... | collective-permute-start | bytes 122888 | tf_op jit(solution)/shard_map/ppermute | solution.py:273
  35.9 2.3 %collective-permute-start.5 = (f32[80,128]{1,0:T(8,128)S(1)}, f32[80,128]{1,0:T(8,128)S(1)}, u32[]{:S(2)}, u32[]{:S(2)}) collective-permute-start(f32[80,128]{1,0:T(8,128)S(1)} %get-tuple-element.46.refs_4_), channel_id=1, source_target_pairs={{0,15},{1,0},{2,1},{3,2},{4,3},{5,4},{6,5},{7,6},{8,7},{9,8},{10,9... | collective-permute-start | bytes 122888 | tf_op jit(solution)/shard_map/ppermute | solution.py:273
  38.2 0.0 collective-permute-done.2.refs_1_
  38.2 0.0 collective-permute-done.3.refs_2_
  38.2 0.0 collective-permute-done.4.refs_5_
  38.2 1.9 %collective-permute-done.5.refs_6_ = f32[80,128]{1,0:T(8,128)S(1)} collective-permute-done((f32[80,128]{1,0:T(8,128)S(1)}, f32[80,128]{1,0:T(8,128)S(1)}, u32[]{:S(2)}, u32[]{:S(2)}) %collective-permute-start.5) | collective-permute-done | bytes 40992 | tf_op jit(solution)/shard_map/ppermute | solution.py:273
  40.0 3.9 %apply1.1 = (f32[80,768]{1,0:T(8,128)S(1)}, f32[8,128]{1,0:T(8,128)S(1)}, f32[80,768]{1,0:T(8,128)S(1)}, f32[80,128]{1,0:T(8,128)S(1)}, f32[80,128]{1,0:T(8,128)...) custom-call(f32[80,768]{1,0:T(8,128)S(1)} %get-tuple-element.42.refs_0_, ...), custom_call_target="tpu_custom_call" | custom-call | flops 2000000000 | bytes 4194304 | tf_op jit(solution)/shard_map/apply1/pallas_call | solution.py:281
  43.9 1.9 %collective-permute-start.6 = (f32[80,128]{1,0:T(8,128)S(1)}, f32[80,128]{1,0:T(8,128)S(1)}, u32[]{:S(2)}, u32[]{:S(2)}) collective-permute-start(f32[80,128]{1,0:T(8,128)S(1)} %get-tuple-element.48), channel_id=1, source_target_pairs={{0,16},{16,32},{32,48},{48,64},{64,80},{80,96},{96,112},{112,128},... | collective-permute-start | bytes 122888 | tf_op jit(solution)/shard_map/ppermute | solution.py:273
  45.9 0.0 collective-permute-start.7
  45.9 7.0 %collective-permute-start.8 = (f32[80,128]{1,0:T(8,128)S(1)}, f32[80,128]{1,0:T(8,128)S(1)}, u32[]{:S(2)}, u32[]{:S(2)}) collective-permute-start(f32[80,128]{1,0:T(8,128)S(1)} %get-tuple-element.50.refs_3_), channel_id=1, source_target_pairs={{0,496},{16,0},{32,16},{48,32},{64,48},{80,64},{96,80},{112,96},{1... | collective-permute-start | bytes 122888 | tf_op jit(solution)/shard_map/ppermute | solution.py:273
  52.9 3.8 %collective-permute-start.9 = (f32[80,128]{1,0:T(8,128)S(1)}, f32[80,128]{1,0:T(8,128)S(1)}, u32[]{:S(2)}, u32[]{:S(2)}) collective-permute-start(f32[80,128]{1,0:T(8,128)S(1)} %get-tuple-element.51.refs_4_), channel_id=1, source_target_pairs={{0,15},{1,0},{2,1},{3,2},{4,3},{5,4},{6,5},{7,6},{8,7},{9,8},{10,9... | collective-permute-start | bytes 122888 | tf_op jit(solution)/shard_map/ppermute | solution.py:273
  56.7 0.0 collective-permute-done.6.refs_1_
  56.7 0.0 collective-permute-done.7.refs_2_
  56.7 0.0 collective-permute-done.8.refs_5_
  56.7 0.9 collective-permute-done.9.refs_6_
  57.6 3.9 %apply2.1 = (f32[80,768]{1,0:T(8,128)S(1)}, f32[8,128]{1,0:T(8,128)S(1)}, f32[80,768]{1,0:T(8,128)S(1)}, f32[80,128]{1,0:T(8,128)S(1)}, f32[80,128]{1,0:T(8,128)...) custom-call(f32[80,768]{1,0:T(8,128)S(1)} %get-tuple-element.47.refs_0_, ...), custom_call_target="tpu_custom_call" | custom-call | flops 2000000000 | bytes 4194304 | tf_op jit(solution)/shard_map/apply2/pallas_call | solution.py:281
  61.4 1.9 %collective-permute-start.10 = (f32[80,128]{1,0:T(8,128)S(1)}, f32[80,128]{1,0:T(8,128)S(1)}, u32[]{:S(2)}, u32[]{:S(2)}) collective-permute-start(f32[80,128]{1,0:T(8,128)S(1)} %get-tuple-element.54), channel_id=1, source_target_pairs={{0,16},{16,32},{32,48},{48,64},{64,80},{80,96},{96,112},{112,128},... | collective-permute-start | bytes 122888 | tf_op jit(solution)/shard_map/ppermute | solution.py:273
  63.4 0.0 collective-permute-start.11
  63.4 6.7 %collective-permute-start.12 = (f32[80,128]{1,0:T(8,128)S(1)}, f32[80,128]{1,0:T(8,128)S(1)}, u32[]{:S(2)}, u32[]{:S(2)}) collective-permute-start(f32[80,128]{1,0:T(8,128)S(1)} %get-tuple-element.56.refs_3_), channel_id=1, source_target_pairs={{0,496},{16,0},{32,16},{48,32},{64,48},{80,64},{96,80},{112,96},{1... | collective-permute-start | bytes 122888 | tf_op jit(solution)/shard_map/ppermute | solution.py:273
  70.1 4.0 %collective-permute-start.13 = (f32[80,128]{1,0:T(8,128)S(1)}, f32[80,128]{1,0:T(8,128)S(1)}, u32[]{:S(2)}, u32[]{:S(2)}) collective-permute-start(f32[80,128]{1,0:T(8,128)S(1)} %get-tuple-element.57.refs_4_), channel_id=1, source_target_pairs={{0,15},{1,0},{2,1},{3,2},{4,3},{5,4},{6,5},{7,6},{8,7},{9,8},{10,9... | collective-permute-start | bytes 122888 | tf_op jit(solution)/shard_map/ppermute | solution.py:273
  74.1 0.0 collective-permute-done.10.refs_1_
  74.1 0.0 collective-permute-done.11.refs_2_
  74.1 0.0 collective-permute-done.12.refs_5_
  74.1 1.1 collective-permute-done.13.refs_6_
  75.2 3.9 %apply3.1 = (f32[80,768]{1,0:T(8,128)S(1)}, f32[8,128]{1,0:T(8,128)S(1)}, f32[80,768]{1,0:T(8,128)S(1)}, f32[80,128]{1,0:T(8,128)S(1)}, f32[80,128]{1,0:T(8,128)S(1)}) custom-call(f32[80,768]{1,0:T(8,128)S(1)} %get-tuple-element.53.refs_0_, f32[80,128]{1,0:T(8,128)S(1)} %collective-permute-done.10.refs_1_, f32[80,128]{1,0:T(8,128)S(1)} %collective-permute-done.11.refs_2_, ...), custom_call_target="tpu_custom_call" | custom-call | flops 2000000000 | bytes 4194304 | tf_op jit(solution)/shard_map/apply3/pallas_call | solution.py:281
  79.1 3.0 %collective-permute-start.14 = (f32[80,128]{1,0:T(8,128)S(1)}, f32[80,128]{1,0:T(8,128)S(1)}, u32[]{:S(2)}, u32[]{:S(2)}) collective-permute-start(f32[80,128]{1,0:T(8,128)S(1)} %get-tuple-element.60), channel_id=1, source_target_pairs={{0,496},{16,0},{32,16},{48,32},{64,48},{80,64},{96,80},{112,96},{1... | collective-permute-start | bytes 122888 | tf_op jit(solution)/shard_map/ppermute | solution.py:273
  82.0 5.2 %collective-permute-start.15 = (f32[80,128]{1,0:T(8,128)S(1)}, f32[80,128]{1,0:T(8,128)S(1)}, u32[]{:S(2)}, u32[]{:S(2)}) collective-permute-start(f32[80,128]{1,0:T(8,128)S(1)} %get-tuple-element.61), channel_id=1, source_target_pairs={{0,15},{1,0},{2,1},{3,2},{4,3},{5,4},{6,5},{7,6},{8,7},{9,8},{10,9... | collective-permute-start | bytes 122888 | tf_op jit(solution)/shard_map/ppermute | solution.py:273
  87.2 0.0 collective-permute-done.14.refs_1_
  87.2 1.1 collective-permute-done.15.refs_2_
  88.3 0.4 last.1
  88.8 34.3 %all_to_all.5 = f32[512,1,128]{2,1,0:T(1,128)S(1)} all-to-all(f32[512,1,128]{2,1,0:T(1,128)S(1)} %bitcast.17), channel_id=1, replica_groups=mesh['gx'=32,'yz'=16] {'gx','yz'}, dimensions={0} | all-to-all | bytes 524288 | tf_op jit(solution)/shard_map/all_to_all | solution.py:370
  123.0 1.2 solve.1
Async XLA Ops:
  0.0 0.9 copy-start
  0.9 0.7 copy-start.4
  1.9 21.2 %collective-permute-start = (f32[80,128]{1,0:T(8,128)S(1)}, f32[80,128]{1,0:T(8,128)S(1)}, u32[]{:S(2)}, u32[]{:S(2)}) collective-permute-start(f32[80,128]{1,0:T(8,128)S(1)} %get-tuple-element.36), channel_id=1, source_target_pairs={{0,16},{16,32},{32,48},{48,64},{64,80},{80,96},{96,112},{112,128},... | collective-permute-start | bytes 122888 | tf_op jit(solution)/shard_map/ppermute | solution.py:273
  5.9 17.3 %copy-start.1 = (f32[1,1,80,768]{3,2,1,0:T(8,128)S(1)}, f32[1,1,80,768]{3,2,1,0:T(8,128)}, u32[]{:S(2)}) copy-start(f32[1,1,80,768]{3,2,1,0:T(8,128)} %param.8) | copy-start | bytes 737284
  5.9 17.3 %copy-start.2 = (f32[1,1,512]{2,1,0:T(1,128)S(1)}, f32[1,1,512]{2,1,0:T(1,128)}, u32[]{:S(2)}) copy-start(f32[1,1,512]{2,1,0:T(1,128)} %param.11) | copy-start | bytes 6148
  5.9 17.3 %copy-start.3 = (f32[1,1,512]{2,1,0:T(1,128)S(1)}, f32[1,1,512]{2,1,0:T(1,128)}, u32[]{:S(2)}) copy-start(f32[1,1,512]{2,1,0:T(1,128)} %param.12) | copy-start | bytes 6148
  5.9 17.2 %collective-permute-start.1 = (f32[80,128]{1,0:T(8,128)S(1)}, f32[80,128]{1,0:T(8,128)S(1)}, u32[]{:S(2)}, u32[]{:S(2)}) collective-permute-start(f32[80,128]{1,0:T(8,128)S(1)} %get-tuple-element.37), channel_id=1, source_target_pairs={{0,1},{1,2},{2,3},{3,4},{4,5},{5,6},{6,7},{7,8},{8,9},{9,10},{10,1... | collective-permute-start | bytes 122888 | tf_op jit(solution)/shard_map/ppermute | solution.py:273
  10.2 1.2 copy-start.5
  11.4 1.0 copy-start.6
  12.4 0.7 copy-start.7
  26.7 11.4 %collective-permute-start.2 = (f32[80,128]{1,0:T(8,128)S(1)}, f32[80,128]{1,0:T(8,128)S(1)}, u32[]{:S(2)}, u32[]{:S(2)}) collective-permute-start(f32[80,128]{1,0:T(8,128)S(1)} %get-tuple-element.43), channel_id=1, source_target_pairs={{0,16},{16,32},{32,48},{48,64},{64,80},{80,96},{96,112},{112,128},... | collective-permute-start | bytes 122888 | tf_op jit(solution)/shard_map/ppermute | solution.py:273
  29.9 8.3 %collective-permute-start.3 = (f32[80,128]{1,0:T(8,128)S(1)}, f32[80,128]{1,0:T(8,128)S(1)}, u32[]{:S(2)}, u32[]{:S(2)}) collective-permute-start(f32[80,128]{1,0:T(8,128)S(1)} %get-tuple-element.44), channel_id=1, source_target_pairs={{0,1},{1,2},{2,3},{3,4},{4,5},{5,6},{6,7},{7,8},{8,9},{9,10},{10,1... | collective-permute-start | bytes 122888 | tf_op jit(solution)/shard_map/ppermute | solution.py:273
  30.3 7.9 %collective-permute-start.4 = (f32[80,128]{1,0:T(8,128)S(1)}, f32[80,128]{1,0:T(8,128)S(1)}, u32[]{:S(2)}, u32[]{:S(2)}) collective-permute-start(f32[80,128]{1,0:T(8,128)S(1)} %get-tuple-element.45.refs_3_), channel_id=1, source_target_pairs={{0,496},{16,0},{32,16},{48,32},{64,48},{80,64},{96,80},{112,96},{1... | collective-permute-start | bytes 122888 | tf_op jit(solution)/shard_map/ppermute | solution.py:273
  35.9 4.1 %collective-permute-start.5 = (f32[80,128]{1,0:T(8,128)S(1)}, f32[80,128]{1,0:T(8,128)S(1)}, u32[]{:S(2)}, u32[]{:S(2)}) collective-permute-start(f32[80,128]{1,0:T(8,128)S(1)} %get-tuple-element.46.refs_4_), channel_id=1, source_target_pairs={{0,15},{1,0},{2,1},{3,2},{4,3},{5,4},{6,5},{7,6},{8,7},{9,8},{10,9... | collective-permute-start | bytes 122888 | tf_op jit(solution)/shard_map/ppermute | solution.py:273
  43.9 12.8 %collective-permute-start.6 = (f32[80,128]{1,0:T(8,128)S(1)}, f32[80,128]{1,0:T(8,128)S(1)}, u32[]{:S(2)}, u32[]{:S(2)}) collective-permute-start(f32[80,128]{1,0:T(8,128)S(1)} %get-tuple-element.48), channel_id=1, source_target_pairs={{0,16},{16,32},{32,48},{48,64},{64,80},{80,96},{96,112},{112,128},... | collective-permute-start | bytes 122888 | tf_op jit(solution)/shard_map/ppermute | solution.py:273
  45.9 10.8 %collective-permute-start.7 = (f32[80,128]{1,0:T(8,128)S(1)}, f32[80,128]{1,0:T(8,128)S(1)}, u32[]{:S(2)}, u32[]{:S(2)}) collective-permute-start(f32[80,128]{1,0:T(8,128)S(1)} %get-tuple-element.49), channel_id=1, source_target_pairs={{0,1},{1,2},{2,3},{3,4},{4,5},{5,6},{6,7},{7,8},{8,9},{9,10},{10,1... | collective-permute-start | bytes 122888 | tf_op jit(solution)/shard_map/ppermute | solution.py:273
  45.9 10.8 %collective-permute-start.8 = (f32[80,128]{1,0:T(8,128)S(1)}, f32[80,128]{1,0:T(8,128)S(1)}, u32[]{:S(2)}, u32[]{:S(2)}) collective-permute-start(f32[80,128]{1,0:T(8,128)S(1)} %get-tuple-element.50.refs_3_), channel_id=1, source_target_pairs={{0,496},{16,0},{32,16},{48,32},{64,48},{80,64},{96,80},{112,96},{1... | collective-permute-start | bytes 122888 | tf_op jit(solution)/shard_map/ppermute | solution.py:273
  52.9 4.6 %collective-permute-start.9 = (f32[80,128]{1,0:T(8,128)S(1)}, f32[80,128]{1,0:T(8,128)S(1)}, u32[]{:S(2)}, u32[]{:S(2)}) collective-permute-start(f32[80,128]{1,0:T(8,128)S(1)} %get-tuple-element.51.refs_4_), channel_id=1, source_target_pairs={{0,15},{1,0},{2,1},{3,2},{4,3},{5,4},{6,5},{7,6},{8,7},{9,8},{10,9... | collective-permute-start | bytes 122888 | tf_op jit(solution)/shard_map/ppermute | solution.py:273
  61.4 12.7 %collective-permute-start.10 = (f32[80,128]{1,0:T(8,128)S(1)}, f32[80,128]{1,0:T(8,128)S(1)}, u32[]{:S(2)}, u32[]{:S(2)}) collective-permute-start(f32[80,128]{1,0:T(8,128)S(1)} %get-tuple-element.54), channel_id=1, source_target_pairs={{0,16},{16,32},{32,48},{48,64},{64,80},{80,96},{96,112},{112,128},... | collective-permute-start | bytes 122888 | tf_op jit(solution)/shard_map/ppermute | solution.py:273
  63.4 10.8 %collective-permute-start.11 = (f32[80,128]{1,0:T(8,128)S(1)}, f32[80,128]{1,0:T(8,128)S(1)}, u32[]{:S(2)}, u32[]{:S(2)}) collective-permute-start(f32[80,128]{1,0:T(8,128)S(1)} %get-tuple-element.55), channel_id=1, source_target_pairs={{0,1},{1,2},{2,3},{3,4},{4,5},{5,6},{6,7},{7,8},{8,9},{9,10},{10,1... | collective-permute-start | bytes 122888 | tf_op jit(solution)/shard_map/ppermute | solution.py:273
  63.4 10.7 %collective-permute-start.12 = (f32[80,128]{1,0:T(8,128)S(1)}, f32[80,128]{1,0:T(8,128)S(1)}, u32[]{:S(2)}, u32[]{:S(2)}) collective-permute-start(f32[80,128]{1,0:T(8,128)S(1)} %get-tuple-element.56.refs_3_), channel_id=1, source_target_pairs={{0,496},{16,0},{32,16},{48,32},{64,48},{80,64},{96,80},{112,96},{1... | collective-permute-start | bytes 122888 | tf_op jit(solution)/shard_map/ppermute | solution.py:273
  70.1 5.1 %collective-permute-start.13 = (f32[80,128]{1,0:T(8,128)S(1)}, f32[80,128]{1,0:T(8,128)S(1)}, u32[]{:S(2)}, u32[]{:S(2)}) collective-permute-start(f32[80,128]{1,0:T(8,128)S(1)} %get-tuple-element.57.refs_4_), channel_id=1, source_target_pairs={{0,15},{1,0},{2,1},{3,2},{4,3},{5,4},{6,5},{7,6},{8,7},{9,8},{10,9... | collective-permute-start | bytes 122888 | tf_op jit(solution)/shard_map/ppermute | solution.py:273
  79.1 8.1 %collective-permute-start.14 = (f32[80,128]{1,0:T(8,128)S(1)}, f32[80,128]{1,0:T(8,128)S(1)}, u32[]{:S(2)}, u32[]{:S(2)}) collective-permute-start(f32[80,128]{1,0:T(8,128)S(1)} %get-tuple-element.60), channel_id=1, source_target_pairs={{0,496},{16,0},{32,16},{48,32},{64,48},{80,64},{96,80},{112,96},{1... | collective-permute-start | bytes 122888 | tf_op jit(solution)/shard_map/ppermute | solution.py:273
  82.0 6.3 %collective-permute-start.15 = (f32[80,128]{1,0:T(8,128)S(1)}, f32[80,128]{1,0:T(8,128)S(1)}, u32[]{:S(2)}, u32[]{:S(2)}) collective-permute-start(f32[80,128]{1,0:T(8,128)S(1)} %get-tuple-element.61), channel_id=1, source_target_pairs={{0,15},{1,0},{2,1},{3,2},{4,3},{5,4},{6,5},{7,6},{8,7},{9,8},{10,9... | collective-permute-start | bytes 122888 | tf_op jit(solution)/shard_map/ppermute | solution.py:273

commit v2 on v1

--- a/solution.py
+++ b/solution.py
@@ -13,8 +13,9 @@
 NORM_ROOM = 1024.0
 F32 = jnp.float32
 BF16 = jnp.bfloat16
+STARTS = ("gx later", "gx first", "yz up", "yz down")
 PAIRS = [(i, j) for j in range(ITERS + 1) for i in range(j + 1)]
-VMEM_BYTES = 40 * 1024 * 1024
+VMEM_BYTES = 20 * 1024 * 1024
 
 
 def halves(value):
@@ -41,47 +42,81 @@
     )
 
 
-def first_kernel(source_ref, send_ref, pick_ref, slab_ref, section_ref):
+def fetched(sources, targets, semaphores):
+    copies = [
+        pltpu.make_async_copy(source, target, semaphores.at[k])
+        for k, (source, target) in enumerate(zip(sources, targets))
+    ]
+    for copy in copies:
+        copy.start()
+    return [copy.wait for copy in copies]
+
+
+def first_kernel(source_hbm, send_hbm, pick_ref, slab_ref, section_ref, source_ref, send_ref, semaphores):
+    have_source, have_send = fetched((source_hbm, send_hbm), (source_ref, send_ref), semaphores)
     owned = source_ref.shape[1]
     shared = send_ref.shape[1]
     faces = lax.broadcasted_iota(jnp.int32, (owned, shared), 0)
+    have_send()
     for row in range(2):
         pick_ref[:, row * shared : (row + 1) * shared] = jnp.where(
             faces == send_ref[row : row + 1, :], 1.0, 0.0
         ).astype(BF16)
+    have_source()
     sent = folded(dot(stacked(source_ref[...]), pick_ref[...]))
     slab_ref[...] = sent[:, :shared]
     section_ref[...] = sent[:, shared:]
 
 
+def three_pass(first, second):
+    return dot_last(first[0], second[0]) + (dot_last(first[0], second[1]) + dot_last(first[1], second[0]))
+
+
 def prepare_kernel(
-    table_ref, inverse_ref, lifting_ref, block_ref, select_ref, weight_ref, scale_ref
+    table_hbm, inverse_hbm, lifting_hbm, block_hbm, select_ref, weight_ref, scale_ref,
+    table_ref, inverse_ref, lifting_ref, block_ref, semaphores,
 ):
+    have_table, have_inverse, have_lifting, have_block = fetched(
+        (table_hbm, inverse_hbm, lifting_hbm, block_hbm),
+        (table_ref, inverse_ref, lifting_ref, block_ref),
+        semaphores,
+    )
     faces = select_ref.shape[0]
     elements = table_ref.shape[1]
     trace = block_ref.shape[1]
     shapes = block_ref.shape[0]
     dofs = trace // 4
-    ids = lax.broadcasted_iota(jnp.int32, (faces, elements), 0)
-    for k in range(4):
-        select_ref[:, k * elements : (k + 1) * elements] = jnp.where(
-            ids == table_ref[k : k + 1, :], 1.0, 0.0
-        ).astype(BF16)
     place = lax.broadcasted_iota(jnp.int32, (trace, trace), 0)
     k = sum(jnp.where(place >= m * dofs, 1, 0) for m in range(1, 4))
     order = jnp.where(
         lax.broadcasted_iota(jnp.int32, (trace, trace), 1) == (place - k * dofs) * 4 + k, 1.0, 0.0
-    )
-    highest = lax.Precision.HIGHEST
+    ).astype(BF16)
+    have_table()
+    group = elements // shapes
+    ids = lax.broadcasted_iota(jnp.int32, (faces, group), 0)
+    for t in range(shapes):
+        for k in range(4):
+            start = (t * 4 + k) * group
+            select_ref[:, start : start + group] = jnp.where(
+                ids == table_ref[k : k + 1, t * group : (t + 1) * group], 1.0, 0.0
+            ).astype(BF16)
     block_bound = jnp.zeros((1, 1), F32)
     inner_bound = jnp.zeros((1, 1), F32)
+    have_inverse()
+    have_lifting()
+    have_block()
     for t in range(shapes):
-        lifted = jnp.dot(order, lifting_ref[t], preferred_element_type=F32, precision=highest)
-        inner = dot_last(dot_last(lifted, inverse_ref[t], highest), lifted, highest)
-        block = dot_last(dot_last(order, block_ref[t], highest), order, highest)
-        block_bound = jnp.maximum(block_bound, jnp.sum(block * block, keepdims=True))
+        lifted = [dot_last(order, part).astype(BF16) for part in halves(lifting_ref[t])]
+        half = three_pass(lifted, halves(inverse_ref[t]))
+        inner = three_pass(halves(half), lifted)
+        turned = [dot_last(order, part).astype(BF16) for part in halves(block_ref[t])]
+        block = [dot_last(part, order) for part in turned]
+        square = block[0] + block[1]
+        block_bound = jnp.maximum(block_bound, jnp.sum(square * square, keepdims=True))
         inner_bound = jnp.maximum(inner_bound, jnp.sum(inner * inner, keepdims=True))
-        high, low = halves(jnp.concatenate([block, inner], axis=0))
+        inner_high, inner_low = halves(inner)
+        high = jnp.concatenate([block[0].astype(BF16), inner_high], axis=0)
+        low = jnp.concatenate([block[1].astype(BF16), inner_low], axis=0)
         weight_ref[t] = jnp.concatenate([high, high, low], axis=1)
     bound = 4.0 * (6.0 + jnp.sqrt(block_bound) + 2.0 * jnp.sqrt(inner_bound)) + SHIFT
     scale_ref[...] = jnp.broadcast_to(
@@ -104,24 +139,26 @@
 def apply_kernel(first, final, earlier, *refs):
     refs = list(refs)
     own_ref = refs.pop(0)
-    ghosts = [refs.pop(0) for _ in range(2)]
-    if not first:
+    if first:
+        ghosts = [refs.pop(0) for _ in range(2)]
+    else:
+        got = [refs.pop(0) for _ in range(4)]
         down = [refs.pop(0) for _ in range(2)]
-        back = [refs.pop(0) for _ in range(2)]
     vectors = [refs.pop(0) for _ in range(earlier)]
-    select_ref, weight_ref, pick_ref, stabilize_ref, coupling_ref, scale_ref = refs[:6]
-    refs = refs[6:]
+    select_ref, weight_ref, pick_ref, stabilize_ref, coupling_ref, scale_ref, odd_ref = refs[:7]
+    refs = refs[7:]
     if not first:
         vector_ref = refs.pop(0)
     gram_ref = refs.pop(0)
     part_ref = refs.pop(0)
     down_out = [refs.pop(0) for _ in range(2)]
     if not final:
-        up_out = [refs.pop(0) for _ in range(2)]
-    wide_ref, result_ref = refs
+        message = [refs.pop(0) for _ in range(4)]
+    (wide_ref,) = refs
+    odd = odd_ref[...] != 0
 
     dofs, owned = own_ref.shape
-    shared = ghosts[0].shape[1]
+    shared = pick_ref.shape[1] // 2
     shapes = weight_ref.shape[0]
     elements = stabilize_ref.shape[1]
     group = elements // shapes
@@ -131,19 +168,21 @@
         vector = own_ref[...]
         ghost = jnp.concatenate([ref[...] for ref in ghosts], axis=1)
     else:
-        received = jnp.concatenate([ref[...] for ref in back], axis=1)
+        parts = dict(zip(STARTS, [ref[...] for ref in got]))
+        back = [jnp.where(odd, parts["gx later"], parts["gx first"]), parts["yz down"]]
+        up = [jnp.where(odd, parts["gx first"], parts["gx later"]), parts["yz up"]]
+        received = jnp.concatenate(back, axis=1)
         vector = own_ref[...] + folded(dot_last(stacked(received), pick_ref[...]))
         vector_ref[...] = vector
-        ghost = jnp.concatenate([a[...] + b[...] for a, b in zip(ghosts, down)], axis=1)
+        ghost = jnp.concatenate([a + b[...] for a, b in zip(up, down)], axis=1)
     extended = jnp.concatenate([vector, ghost], axis=1)
     wide_ref[...] = stacked(extended)
 
+    everything = dot(wide_ref[...], select_ref[...])
+    results = []
     for t in range(shapes):
         columns = slice(t * group, (t + 1) * group)
-        picked = []
-        for k in range(4):
-            start = k * elements + t * group
-            picked.append(dot(wide_ref[...], select_ref[:, start : start + group]))
+        picked = [everything[:, (t * 4 + k) * group : (t * 4 + k + 1) * group] for k in range(4)]
         high = jnp.concatenate([p[:dofs] for p in picked], axis=0)
         low = jnp.concatenate([p[dofs:] for p in picked], axis=0)
         high16, low16 = high.astype(BF16), low.astype(BF16)
@@ -153,21 +192,27 @@
             + product[:trace]
             - product[trace:] / coupling_ref[:, columns]
         )
-        for k in range(4):
-            start = k * elements + t * group
-            result_ref[:, start : start + group] = stacked(result[k * dofs : (k + 1) * dofs])
+        results += [stacked(result[k * dofs : (k + 1) * dofs]) for k in range(4)]
     inner_products([ref[...] for ref in vectors] + [vector], vector, gram_ref, 0)
     gram_ref[earlier + 1 :, :] = jnp.zeros((8 - earlier - 1, 128), F32)
     shrink = 1.0 / scale_ref[:, :1]
-    summed = folded(dot_last(result_ref[...], select_ref[...])) * shrink
+    summed = folded(dot_last(jnp.concatenate(results, axis=1), select_ref[...])) * shrink
     part = summed[:, :owned] - (SHIFT * shrink) * vector
     part_ref[...] = part
     for i in range(2):
         down_out[i][...] = summed[:, owned + i * shared : owned + (i + 1) * shared]
     if not final:
         sent = folded(dot(stacked(part), pick_ref[...]))
-        for i in range(2):
-            up_out[i][...] = sent[:, i * shared : (i + 1) * shared]
+        up, up_section = sent[:, :shared], sent[:, shared:]
+        down, down_section = summed[:, owned : owned + shared], summed[:, owned + shared :]
+        parts = {
+            "gx later": jnp.where(odd, up, down),
+            "gx first": jnp.where(odd, down, up),
+            "yz up": up_section,
+            "yz down": down_section,
+        }
+        for name, ref in zip(STARTS, message):
+            ref[...] = parts[name]
 
 
 def last_kernel(*refs):
@@ -253,6 +298,11 @@
     return total[:ITERS]
 
 
+def add_kernel(rows_ref, out_ref):
+    total = jnp.sum(rows_ref[...], axis=0, keepdims=True)
+    out_ref[...] = jnp.broadcast_to(total, out_ref.shape)
+
+
 def solve_kernel(rows_ref, scale_ref, *refs):
     vectors = refs[:ITERS]
     out_ref = refs[ITERS]
@@ -273,15 +323,32 @@
     return lax.ppermute(value, axis, pairs)
 
 
+def exchange(value, name):
+    axis, kind = name.split()
+    if kind in ("up", "down"):
+        return passed_along(value, axis, 1 if kind == "up" else -1)
+    count = lax.axis_size(axis)
+    ahead = 1 if kind == "later" else 0
+    pairs = [(i, (i + (1 if i % 2 == ahead else -1)) % count) for i in range(count)]
+    return lax.ppermute(value, axis, pairs)
+
+
+def every(row, axis):
+    count = row.shape[0]
+    return lax.all_to_all(row.reshape(count, 1, 128), axis, 0, 0).reshape(count, 128)
+
+
 def shape(*dims, dtype=F32):
     return jax.ShapeDtypeStruct(dims, dtype)
 
 
-def call(kernel, out_shape, *args, scratch=(), flops=0, name=None):
+def call(kernel, out_shape, *args, scratch=(), flops=0, name=None, space=pltpu.VMEM):
+    if space == pltpu.HBM:
+        args = [pltpu.with_memory_space_constraint(arg, space) for arg in args]
     return pl.pallas_call(
         kernel,
         out_shape=out_shape,
-        in_specs=[pl.BlockSpec(memory_space=pltpu.VMEM)] * len(args),
+        in_specs=[pl.BlockSpec(memory_space=space)] * len(args),
         out_specs=jax.tree.map(lambda _: pl.BlockSpec(memory_space=pltpu.VMEM), out_shape),
         scratch_shapes=list(scratch),
         cost_estimate=pl.CostEstimate(flops=flops, bytes_accessed=4 * 1024 * 1024, transcendentals=0),
@@ -303,13 +370,23 @@
     shared = send_lists.shape[1]
     faces = owned + 2 * shared
     shapes, trace, _ = lifting.shape
-    devices = lax.axis_size("gx") * lax.axis_size("yz")
     part = shape(dofs, shared)
 
     pick, slab, section = call(
-        first_kernel, (shape(owned, 2 * shared, dtype=BF16), part, part), source, send_lists, name="first"
+        first_kernel,
+        (shape(owned, 2 * shared, dtype=BF16), part, part),
+        source,
+        send_lists,
+        scratch=[
+            pltpu.VMEM(source.shape, F32),
+            pltpu.VMEM(send_lists.shape, jnp.int32),
+            pltpu.SemaphoreType.DMA((2,)),
+        ],
+        name="first",
+        space=pltpu.HBM,
     )
     ghosts = [passed_along(slab, "gx", 1), passed_along(section, "yz", 1)]
+    turned = jnp.swapaxes(lifting, 1, 2)
     select, weights, scale = call(
         prepare_kernel,
         (
@@ -319,11 +396,20 @@
         ),
         table,
         inverse,
-        lifting,
+        turned,
         trace_block,
+        scratch=[
+            pltpu.VMEM(table.shape, jnp.int32),
+            pltpu.VMEM(inverse.shape, F32),
+            pltpu.VMEM(turned.shape, F32),
+            pltpu.VMEM(trace_block.shape, F32),
+            pltpu.SemaphoreType.DMA((4,)),
+        ],
         flops=2 * 10**9,
         name="prepare",
-    )
+        space=pltpu.HBM,
+    )
+    odd = jnp.full((1, 128), lax.axis_index("gx") % 2, jnp.int32)
     vectors = [source]
     grams = []
     own, exchanged = source, ghosts
@@ -333,7 +419,7 @@
         if j:
             outs = [shape(dofs, owned)] + outs
         if not final:
-            outs = outs + [part, part]
+            outs = outs + [part] * 4
         earlier = vectors[:j] if j else []
         results = call(
             functools.partial(apply_kernel, j == 0, final, len(earlier)),
@@ -347,7 +433,8 @@
             penalty,
             scaling,
             scale,
-            scratch=[pltpu.VMEM((2 * dofs, faces), BF16), pltpu.VMEM((2 * dofs, 4 * elements), BF16)],
+            odd,
+            scratch=[pltpu.VMEM((2 * dofs, faces), BF16)],
             flops=2 * 10**9,
             name=f"apply{j}",
         )
@@ -357,18 +444,24 @@
         grams.append(results.pop(0))
         own = results.pop(0)
         down = [results.pop(0) for _ in range(2)]
-        back = [passed_along(down[0], "gx", -1), passed_along(down[1], "yz", -1)]
         if final:
-            exchanged = back
+            exchanged = [passed_along(down[0], "gx", -1), passed_along(down[1], "yz", -1)]
         else:
-            up = [passed_along(results.pop(0), "gx", 1), passed_along(results.pop(0), "yz", 1)]
-            exchanged = up + down + back
+            exchanged = [exchange(results.pop(0), name) for name in STARTS] + down
+    gx, yz = lax.axis_size("gx"), lax.axis_size("yz")
     rows = call(
-        last_kernel, shape(devices, 128), own, *exchanged, *vectors, *grams, pick, scratch=[pltpu.VMEM((16, 128), F32)],
+        last_kernel,
+        shape(yz, 128),
+        own,
+        *exchanged,
+        *vectors,
+        *grams,
+        pick,
+        scratch=[pltpu.VMEM((16, 128), F32)],
         name="last",
     )
-    rows = lax.all_to_all(rows.reshape(devices, 1, 128), ("gx", "yz"), 0, 0).reshape(devices, 128)
-    solution = call(solve_kernel, shape(dofs, owned), rows, scale, *vectors, name="solve")
+    rows = call(add_kernel, shape(gx, 128), every(rows, "yz"), name="add")
+    solution = call(solve_kernel, shape(dofs, owned), every(rows, "gx"), scale, *vectors, name="solve")
     return solution[None, None]
 
 

time: 125 us -> 108 us (0.86)
  Pallas kernels: 27.2 us -> 20.5 us
  starting transfers between devices: 51.8 us -> 47 us
  blocking collectives: 34.3 us -> 32 us
  local copies, waits for them, and re-layouts: 5.84 us -> 4.12 us
  waiting for transfers between devices: 4.92 us -> 3.48 us
    ppermute x16 -> x10, starting transfers between devices: 51.8 us -> 26.1 us  [passed_along(): return lax.ppermute(value, axis, pairs)]
    ppermute x0 -> x6, starting transfers between devices: none -> 20.9 us  [exchange(): return lax.ppermute(value, axis, pairs)]
    pallas_call x8 -> x9, Pallas kernels: 27.2 us -> 20.5 us  [call(): pl.pallas_call(kernel, out_shape=out_shape, in_specs=[pl.BlockSpec(memory...]
    all_to_all x1 -> x2, blocking collectives: 34.3 us -> 32 us  [every(): lax.all_to_all(row.reshape(count, 1, 128), axis, 0, 0).reshape(count, 128)]
    unnamed x17 -> x10, local copies, waits for them, and re-layouts: 5.84 us -> 4.12 us
    ppermute x16 -> x10, waiting for transfers between devices: 4.92 us -> 3.47 us  [passed_along(): return lax.ppermute(value, axis, pairs)]
  transfers between devices with their start and end apart: 16 -> 16, of which waited for: 4 -> 7; matrix products, arithmetic and copies ran while one was open for 1% -> 0% of each run, Pallas kernels for 8% -> 5%
where the time goes in v2:
time: 108 us; the launch traced here: 107 us
  starting transfers between devices  47 us (44%)
  blocking collectives  32 us (30%)
  Pallas kernels  20.5 us (19%)
  local copies, waits for them, and re-layouts  4.12 us (4%)
  waiting for transfers between devices  3.48 us (3%)
    all_to_all x2, blocking collectives, every(): lax.all_to_all(row.reshape(count, 1, 128), axis, 0, 0).reshape(count, 128)  32 us
    ppermute x10, starting transfers between devices, passed_along(): return lax.ppermute(value, axis, pairs)  26.1 us
    ppermute x6, starting transfers between devices, exchange(): return lax.ppermute(value, axis, pairs)  20.9 us
    pallas_call x9, Pallas kernels, call(): pl.pallas_call(kernel, out_shape=out_shape, in_specs=[pl.BlockSpec(memory...  20.5 us
    unnamed x10, local copies, waits for them, and re-layouts  4.12 us
    ppermute x10, waiting for transfers between devices, passed_along(): return lax.ppermute(value, axis, pairs)  3.47 us
  transfers between devices with their start and end apart: 16, of which 7 were waited for; matrix products, arithmetic and copies ran while one was open for 0% of the time, Pallas kernels for 5%

profile of v2, /device:TPU:1, one launch (start us, length us, event | category | flops | bytes accessed | tf_op | source)
XLA Modules:
  0.0 107.3 jit_solution(10791545887032099270)
XLA Ops:
  0.0 0.0 copy-start.2
  0.0 0.0 copy-start.4
  0.0 0.0 copy-start.3
  0.0 1.3 %first.1 = (bf16[768,256]{1,0:T(8,128)(2,1)S(1)}, f32[80,128]{1,0:T(8,128)S(1)}, f32[80,128]{1,0:T(8,128)S(1)}) custom-call(f32[80,768]{1,0:T(8,128)} %bitcast.15, s32[2,128]{1,0:T(2,128)} %bitcast.34), custom_call_target="tpu_custom_call" | custom-call | bytes 4194304 | tf_op jit(solution)/shard_map/first/pallas_call | solution.py:348
  1.3 3.9 %collective-permute-start = (f32[80,128]{1,0:T(8,128)S(1)}, f32[80,128]{1,0:T(8,128)S(1)}, u32[]{:S(2)}, u32[]{:S(2)}) collective-permute-start(f32[80,128]{1,0:T(8,128)S(1)} %get-tuple-element.42), channel_id=1, source_target_pairs={{0,16},{16,32},{32,48},{48,64},{64,80},{80,96},{96,112},{112,128},... | collective-permute-start | bytes 122888 | tf_op jit(solution)/shard_map/ppermute | solution.py:323
  5.2 2.9 %collective-permute-start.1 = (f32[80,128]{1,0:T(8,128)S(1)}, f32[80,128]{1,0:T(8,128)S(1)}, u32[]{:S(2)}, u32[]{:S(2)}) collective-permute-start(f32[80,128]{1,0:T(8,128)S(1)} %get-tuple-element.43), channel_id=1, source_target_pairs={{0,1},{1,2},{2,3},{3,4},{4,5},{5,6},{6,7},{7,8},{8,9},{9,10},{10,1... | collective-permute-start | bytes 122888 | tf_op jit(solution)/shard_map/ppermute | solution.py:323
  8.2 5.1 %prepare.1 = (bf16[1024,2048]{1,0:T(8,128)(2,1)S(1)}, bf16[2,640,960]{2,1,0:T(8,128)(2,1)S(1)}, f32[1,128]{1,0:T(1,128)S(1)}) custom-call(s32[4,512]{1,0:T(4,128)} %bitcast.36, f32[2,192,192]{2,1,0:T(8,128)} %inverse_hbm.1, f32[2,192,320]{2,1,0:T(8,128)} %bitcast.35, f32[2,320,320]{2,1,0:T(8,128)} %block_hbm.1), custom_call_target="tpu_custom_call" | custom-call | flops 2000000000 | bytes 4194304 | tf_op jit(solution)/shard_map/prepare/pallas_call | solution.py:348
  13.3 0.0 copy-start
  13.3 1.9 %copy-done = bf16[1024,2048]{1,0:T(8,128)(2,1)} copy-done((bf16[1024,2048]{1,0:T(8,128)(2,1)}, bf16[1024,2048]{1,0:T(8,128)(2,1)S(1)}, u32[]{:S(2)}) %copy-start) | copy-done | bytes 4194328
  15.2 0.0 collective-permute-done.refs_1_
  15.2 0.0 collective-permute-done.1.refs_2_
  15.2 0.0 copy-done.2
  15.2 0.0 copy-done.4
  15.2 0.0 copy-done.3
  15.2 0.0 copy-start.1
  15.2 2.2 %copy-done.1 = bf16[1024,2048]{1,0:T(8,128)(2,1)S(1)} copy-done((bf16[1024,2048]{1,0:T(8,128)(2,1)S(1)}, bf16[1024,2048]{1,0:T(8,128)(2,1)}, u32[]{:S(2)}) %copy-start.1) | copy-done | bytes 4194328
  17.4 2.9 %apply0.1 = (f32[8,128]{1,0:T(8,128)S(1)}, f32[80,768]{1,0:T(8,128)S(1)}, f32[80,128]{1,0:T(8,128)S(1)}, f32[80,128]{1,0:T(8,128)S(1)}, f32[80,128]{1,0:T(8,128)...) custom-call(f32[80,768]{1,0:T(8,128)S(1)} %bitcast.16, ...), custom_call_target="tpu_custom_call" | custom-call | flops 2000000000 | bytes 4194304 | tf_op jit(solution)/shard_map/apply0/pallas_call | solution.py:348
  20.3 5.8 %collective-permute-start.2 = (f32[80,128]{1,0:T(8,128)S(1)}, f32[80,128]{1,0:T(8,128)S(1)}, u32[]{:S(2)}, u32[]{:S(2)}) collective-permute-start(f32[80,128]{1,0:T(8,128)S(1)} %get-tuple-element.49), channel_id=1, source_target_pairs={{0,496},{16,32},{32,16},{48,64},{64,48},{80,96},{96,80},{112,128},... | collective-permute-start | bytes 122888 | tf_op jit(solution)/shard_map/ppermute | solution.py:333
  26.1 1.9 %collective-permute-start.3 = (f32[80,128]{1,0:T(8,128)S(1)}, f32[80,128]{1,0:T(8,128)S(1)}, u32[]{:S(2)}, u32[]{:S(2)}) collective-permute-start(f32[80,128]{1,0:T(8,128)S(1)} %get-tuple-element.50), channel_id=1, source_target_pairs={{0,16},{16,0},{32,48},{48,32},{64,80},{80,64},{96,112},{112,96},{1... | collective-permute-start | bytes 122888 | tf_op jit(solution)/shard_map/ppermute | solution.py:333
  28.0 0.3 collective-permute-start.4
  28.3 3.1 %collective-permute-start.5 = (f32[80,128]{1,0:T(8,128)S(1)}, f32[80,128]{1,0:T(8,128)S(1)}, u32[]{:S(2)}, u32[]{:S(2)}) collective-permute-start(f32[80,128]{1,0:T(8,128)S(1)} %get-tuple-element.52), channel_id=1, source_target_pairs={{0,15},{1,0},{2,1},{3,2},{4,3},{5,4},{6,5},{7,6},{8,7},{9,8},{10,9... | collective-permute-start | bytes 122888 | tf_op jit(solution)/shard_map/ppermute | solution.py:323
  31.4 0.0 collective-permute-done.2.refs_1_
  31.4 0.0 collective-permute-done.3.refs_2_
  31.5 0.7 collective-permute-done.4.refs_3_
  32.1 0.2 collective-permute-done.5.refs_4_
  32.3 3.2 %apply1.1 = (f32[80,768]{1,0:T(8,128)S(1)}, f32[8,128]{1,0:T(8,128)S(1)}, f32[80,768]{1,0:T(8,128)S(1)}, f32[80,128]{1,0:T(8,128)S(1)}, f32[80,128]{1,0:T(8,128)...) custom-call(f32[80,768]{1,0:T(8,128)S(1)} %get-tuple-element.48.refs_0_, ...), custom_call_target="tpu_custom_call" | custom-call | flops 2000000000 | bytes 4194304 | tf_op jit(solution)/shard_map/apply1/pallas_call | solution.py:348
  35.6 4.4 %collective-permute-start.6 = (f32[80,128]{1,0:T(8,128)S(1)}, f32[80,128]{1,0:T(8,128)S(1)}, u32[]{:S(2)}, u32[]{:S(2)}) collective-permute-start(f32[80,128]{1,0:T(8,128)S(1)} %get-tuple-element.56), channel_id=1, source_target_pairs={{0,496},{16,32},{32,16},{48,64},{64,48},{80,96},{96,80},{112,128},... | collective-permute-start | bytes 122888 | tf_op jit(solution)/shard_map/ppermute | solution.py:333
  39.9 1.9 %collective-permute-start.7 = (f32[80,128]{1,0:T(8,128)S(1)}, f32[80,128]{1,0:T(8,128)S(1)}, u32[]{:S(2)}, u32[]{:S(2)}) collective-permute-start(f32[80,128]{1,0:T(8,128)S(1)} %get-tuple-element.57), channel_id=1, source_target_pairs={{0,16},{16,0},{32,48},{48,32},{64,80},{80,64},{96,112},{112,96},{1... | collective-permute-start | bytes 122888 | tf_op jit(solution)/shard_map/ppermute | solution.py:333
  41.9 0.0 collective-permute-start.8
  41.9 3.8 %collective-permute-start.9 = (f32[80,128]{1,0:T(8,128)S(1)}, f32[80,128]{1,0:T(8,128)S(1)}, u32[]{:S(2)}, u32[]{:S(2)}) collective-permute-start(f32[80,128]{1,0:T(8,128)S(1)} %get-tuple-element.59), channel_id=1, source_target_pairs={{0,15},{1,0},{2,1},{3,2},{4,3},{5,4},{6,5},{7,6},{8,7},{9,8},{10,9... | collective-permute-start | bytes 122888 | tf_op jit(solution)/shard_map/ppermute | solution.py:323
  45.7 0.0 collective-permute-done.6.refs_1_
  45.7 0.0 collective-permute-done.7.refs_2_
  45.7 0.7 collective-permute-done.8.refs_3_
  46.3 0.2 collective-permute-done.9.refs_4_
  46.5 3.3 %apply2.1 = (f32[80,768]{1,0:T(8,128)S(1)}, f32[8,128]{1,0:T(8,128)S(1)}, f32[80,768]{1,0:T(8,128)S(1)}, f32[80,128]{1,0:T(8,128)S(1)}, f32[80,128]{1,0:T(8,128)...) custom-call(f32[80,768]{1,0:T(8,128)S(1)} %get-tuple-element.55.refs_0_, ...), custom_call_target="tpu_custom_call" | custom-call | flops 2000000000 | bytes 4194304 | tf_op jit(solution)/shard_map/apply2/pallas_call | solution.py:348
  49.8 4.8 %collective-permute-start.10 = (f32[80,128]{1,0:T(8,128)S(1)}, f32[80,128]{1,0:T(8,128)S(1)}, u32[]{:S(2)}, u32[]{:S(2)}) collective-permute-start(f32[80,128]{1,0:T(8,128)S(1)} %get-tuple-element.64), channel_id=1, source_target_pairs={{0,496},{16,32},{32,16},{48,64},{64,48},{80,96},{96,80},{112,128},... | collective-permute-start | bytes 122888 | tf_op jit(solution)/shard_map/ppermute | solution.py:333
  54.6 2.1 %collective-permute-start.11 = (f32[80,128]{1,0:T(8,128)S(1)}, f32[80,128]{1,0:T(8,128)S(1)}, u32[]{:S(2)}, u32[]{:S(2)}) collective-permute-start(f32[80,128]{1,0:T(8,128)S(1)} %get-tuple-element.65), channel_id=1, source_target_pairs={{0,16},{16,0},{32,48},{48,32},{64,80},{80,64},{96,112},{112,96},{1... | collective-permute-start | bytes 122888 | tf_op jit(solution)/shard_map/ppermute | solution.py:333
  56.7 0.0 collective-permute-start.12
  56.7 4.0 %collective-permute-start.13 = (f32[80,128]{1,0:T(8,128)S(1)}, f32[80,128]{1,0:T(8,128)S(1)}, u32[]{:S(2)}, u32[]{:S(2)}) collective-permute-start(f32[80,128]{1,0:T(8,128)S(1)} %get-tuple-element.67), channel_id=1, source_target_pairs={{0,15},{1,0},{2,1},{3,2},{4,3},{5,4},{6,5},{7,6},{8,7},{9,8},{10,9... | collective-permute-start | bytes 122888 | tf_op jit(solution)/shard_map/ppermute | solution.py:323
  60.7 0.0 collective-permute-done.10.refs_1_
  60.7 0.0 collective-permute-done.11.refs_2_
  60.7 0.7 collective-permute-done.12.refs_3_
  61.4 0.2 collective-permute-done.13.refs_4_
  61.6 3.2 %apply3.1 = (f32[80,768]{1,0:T(8,128)S(1)}, f32[8,128]{1,0:T(8,128)S(1)}, f32[80,768]{1,0:T(8,128)S(1)}, f32[80,128]{1,0:T(8,128)S(1)}, f32[80,128]{1,0:T(8,128)S(1)}) custom-call(f32[80,768]{1,0:T(8,128)S(1)} %get-tuple-element.63.refs_0_, f32[80,128]{1,0:T(8,128)S(1)} %collective-permute-done.10.refs_1_, f32[80,128]{1,0:T(8,128)S(1)} %collective-permute-done.11.refs_2_, ...), custom_call_target="tpu_custom_call" | custom-call | flops 2000000000 | bytes 4194304 | tf_op jit(solution)/shard_map/apply3/pallas_call | solution.py:348
  64.8 3.9 %collective-permute-start.14 = (f32[80,128]{1,0:T(8,128)S(1)}, f32[80,128]{1,0:T(8,128)S(1)}, u32[]{:S(2)}, u32[]{:S(2)}) collective-permute-start(f32[80,128]{1,0:T(8,128)S(1)} %get-tuple-element.72), channel_id=1, source_target_pairs={{0,496},{16,0},{32,16},{48,32},{64,48},{80,64},{96,80},{112,96},{1... | collective-permute-start | bytes 122888 | tf_op jit(solution)/shard_map/ppermute | solution.py:323
  68.8 4.0 %collective-permute-start.15 = (f32[80,128]{1,0:T(8,128)S(1)}, f32[80,128]{1,0:T(8,128)S(1)}, u32[]{:S(2)}, u32[]{:S(2)}) collective-permute-start(f32[80,128]{1,0:T(8,128)S(1)} %get-tuple-element.73), channel_id=1, source_target_pairs={{0,15},{1,0},{2,1},{3,2},{4,3},{5,4},{6,5},{7,6},{8,7},{9,8},{10,9... | collective-permute-start | bytes 122888 | tf_op jit(solution)/shard_map/ppermute | solution.py:323
  72.8 0.0 collective-permute-done.14.refs_1_
  72.8 0.9 collective-permute-done.15.refs_2_
  73.7 0.4 last.1
  74.1 16.2 %all_to_all.10 = f32[16,1,128]{2,1,0:T(1,128)S(1)} all-to-all(f32[16,1,128]{2,1,0:T(1,128)S(1)} %bitcast.24), channel_id=1, replica_groups=mesh['gx'=32,'yz'=16] {'yz'}, dimensions={0} | all-to-all | bytes 16384 | tf_op jit(solution)/shard_map/all_to_all | solution.py:338
  90.3 15.9 %all_to_all.11 = f32[32,1,128]{2,1,0:T(1,128)S(1)} all-to-all(f32[32,1,128]{2,1,0:T(1,128)S(1)} %bitcast.23), channel_id=1, replica_groups=mesh['gx'=32,'yz'=16] {'gx'}, dimensions={0} | all-to-all | bytes 32768 | tf_op jit(solution)/shard_map/all_to_all | solution.py:338
  106.2 1.2 %solve.1 = f32[80,768]{1,0:T(8,128)} custom-call(f32[32,128]{1,0:T(8,128)S(1)} %bitcast.22, f32[1,128]{1,0:T(1,128)S(1)} %get-tuple-element.47.refs_8_.refs_13_.refs_14_.refs_15_.scale_ref, f32[80,768]{1,0:T(8,128)S(1)} %bitcast.21, f32[80,768]{1,0:T(8,128)S(1)} %get-tuple-element.62.refs_8_.refs_4_.refs_1_, ...), custom_call_target="tpu_custom_call" | custom-call | bytes 4194304 | tf_op jit(solution)/shard_map/solve/pallas_call | solution.py:348
  (2 shorter events, 0.0 us)
Async XLA Ops:
  0.0 15.2 %copy-start.2 = (f32[1,1,80,768]{3,2,1,0:T(8,128)S(1)}, f32[1,1,80,768]{3,2,1,0:T(8,128)}, u32[]{:S(2)}) copy-start(f32[1,1,80,768]{3,2,1,0:T(8,128)} %param.8) | copy-start | bytes 737284
  0.0 15.2 %copy-start.4 = (f32[1,1,512]{2,1,0:T(1,128)S(1)}, f32[1,1,512]{2,1,0:T(1,128)}, u32[]{:S(2)}) copy-start(f32[1,1,512]{2,1,0:T(1,128)} %param.12) | copy-start | bytes 6148
  0.0 15.2 %copy-start.3 = (f32[1,1,512]{2,1,0:T(1,128)S(1)}, f32[1,1,512]{2,1,0:T(1,128)}, u32[]{:S(2)}) copy-start(f32[1,1,512]{2,1,0:T(1,128)} %param.11) | copy-start | bytes 6148
  1.3 13.9 %collective-permute-start = (f32[80,128]{1,0:T(8,128)S(1)}, f32[80,128]{1,0:T(8,128)S(1)}, u32[]{:S(2)}, u32[]{:S(2)}) collective-permute-start(f32[80,128]{1,0:T(8,128)S(1)} %get-tuple-element.42), channel_id=1, source_target_pairs={{0,16},{16,32},{32,48},{48,64},{64,80},{80,96},{96,112},{112,128},... | collective-permute-start | bytes 122888 | tf_op jit(solution)/shard_map/ppermute | solution.py:323
  5.2 10.0 %collective-permute-start.1 = (f32[80,128]{1,0:T(8,128)S(1)}, f32[80,128]{1,0:T(8,128)S(1)}, u32[]{:S(2)}, u32[]{:S(2)}) collective-permute-start(f32[80,128]{1,0:T(8,128)S(1)} %get-tuple-element.43), channel_id=1, source_target_pairs={{0,1},{1,2},{2,3},{3,4},{4,5},{5,6},{6,7},{7,8},{8,9},{9,10},{10,1... | collective-permute-start | bytes 122888 | tf_op jit(solution)/shard_map/ppermute | solution.py:323
  13.3 1.9 %copy-start = (bf16[1024,2048]{1,0:T(8,128)(2,1)}, bf16[1024,2048]{1,0:T(8,128)(2,1)S(1)}, u32[]{:S(2)}) copy-start(bf16[1024,2048]{1,0:T(8,128)(2,1)S(1)} %get-tuple-element.44.refs_3_.refs_8_.refs_9_.refs_10_) | copy-start | bytes 12582916
  15.2 2.2 %copy-start.1 = (bf16[1024,2048]{1,0:T(8,128)(2,1)S(1)}, bf16[1024,2048]{1,0:T(8,128)(2,1)}, u32[]{:S(2)}) copy-start(bf16[1024,2048]{1,0:T(8,128)(2,1)} %copy-done) | copy-start | bytes 12582916
  20.3 11.2 %collective-permute-start.2 = (f32[80,128]{1,0:T(8,128)S(1)}, f32[80,128]{1,0:T(8,128)S(1)}, u32[]{:S(2)}, u32[]{:S(2)}) collective-permute-start(f32[80,128]{1,0:T(8,128)S(1)} %get-tuple-element.49), channel_id=1, source_target_pairs={{0,496},{16,32},{32,16},{48,64},{64,48},{80,96},{96,80},{112,128},... | collective-permute-start | bytes 122888 | tf_op jit(solution)/shard_map/ppermute | solution.py:333
  26.1 5.3 %collective-permute-start.3 = (f32[80,128]{1,0:T(8,128)S(1)}, f32[80,128]{1,0:T(8,128)S(1)}, u32[]{:S(2)}, u32[]{:S(2)}) collective-permute-start(f32[80,128]{1,0:T(8,128)S(1)} %get-tuple-element.50), channel_id=1, source_target_pairs={{0,16},{16,0},{32,48},{48,32},{64,80},{80,64},{96,112},{112,96},{1... | collective-permute-start | bytes 122888 | tf_op jit(solution)/shard_map/ppermute | solution.py:333
  28.0 4.1 %collective-permute-start.4 = (f32[80,128]{1,0:T(8,128)S(1)}, f32[80,128]{1,0:T(8,128)S(1)}, u32[]{:S(2)}, u32[]{:S(2)}) collective-permute-start(f32[80,128]{1,0:T(8,128)S(1)} %get-tuple-element.51), channel_id=1, source_target_pairs={{0,1},{1,2},{2,3},{3,4},{4,5},{5,6},{6,7},{7,8},{8,9},{9,10},{10,1... | collective-permute-start | bytes 122888 | tf_op jit(solution)/shard_map/ppermute | solution.py:323
  28.3 4.0 %collective-permute-start.5 = (f32[80,128]{1,0:T(8,128)S(1)}, f32[80,128]{1,0:T(8,128)S(1)}, u32[]{:S(2)}, u32[]{:S(2)}) collective-permute-start(f32[80,128]{1,0:T(8,128)S(1)} %get-tuple-element.52), channel_id=1, source_target_pairs={{0,15},{1,0},{2,1},{3,2},{4,3},{5,4},{6,5},{7,6},{8,7},{9,8},{10,9... | collective-permute-start | bytes 122888 | tf_op jit(solution)/shard_map/ppermute | solution.py:323
  35.6 10.1 %collective-permute-start.6 = (f32[80,128]{1,0:T(8,128)S(1)}, f32[80,128]{1,0:T(8,128)S(1)}, u32[]{:S(2)}, u32[]{:S(2)}) collective-permute-start(f32[80,128]{1,0:T(8,128)S(1)} %get-tuple-element.56), channel_id=1, source_target_pairs={{0,496},{16,32},{32,16},{48,64},{64,48},{80,96},{96,80},{112,128},... | collective-permute-start | bytes 122888 | tf_op jit(solution)/shard_map/ppermute | solution.py:333
  39.9 5.7 %collective-permute-start.7 = (f32[80,128]{1,0:T(8,128)S(1)}, f32[80,128]{1,0:T(8,128)S(1)}, u32[]{:S(2)}, u32[]{:S(2)}) collective-permute-start(f32[80,128]{1,0:T(8,128)S(1)} %get-tuple-element.57), channel_id=1, source_target_pairs={{0,16},{16,0},{32,48},{48,32},{64,80},{80,64},{96,112},{112,96},{1... | collective-permute-start | bytes 122888 | tf_op jit(solution)/shard_map/ppermute | solution.py:333
  41.9 4.5 %collective-permute-start.8 = (f32[80,128]{1,0:T(8,128)S(1)}, f32[80,128]{1,0:T(8,128)S(1)}, u32[]{:S(2)}, u32[]{:S(2)}) collective-permute-start(f32[80,128]{1,0:T(8,128)S(1)} %get-tuple-element.58), channel_id=1, source_target_pairs={{0,1},{1,2},{2,3},{3,4},{4,5},{5,6},{6,7},{7,8},{8,9},{9,10},{10,1... | collective-permute-start | bytes 122888 | tf_op jit(solution)/shard_map/ppermute | solution.py:323
  41.9 4.6 %collective-permute-start.9 = (f32[80,128]{1,0:T(8,128)S(1)}, f32[80,128]{1,0:T(8,128)S(1)}, u32[]{:S(2)}, u32[]{:S(2)}) collective-permute-start(f32[80,128]{1,0:T(8,128)S(1)} %get-tuple-element.59), channel_id=1, source_target_pairs={{0,15},{1,0},{2,1},{3,2},{4,3},{5,4},{6,5},{7,6},{8,7},{9,8},{10,9... | collective-permute-start | bytes 122888 | tf_op jit(solution)/shard_map/ppermute | solution.py:323
  49.8 11.0 %collective-permute-start.10 = (f32[80,128]{1,0:T(8,128)S(1)}, f32[80,128]{1,0:T(8,128)S(1)}, u32[]{:S(2)}, u32[]{:S(2)}) collective-permute-start(f32[80,128]{1,0:T(8,128)S(1)} %get-tuple-element.64), channel_id=1, source_target_pairs={{0,496},{16,32},{32,16},{48,64},{64,48},{80,96},{96,80},{112,128},... | collective-permute-start | bytes 122888 | tf_op jit(solution)/shard_map/ppermute | solution.py:333
  54.6 6.2 %collective-permute-start.11 = (f32[80,128]{1,0:T(8,128)S(1)}, f32[80,128]{1,0:T(8,128)S(1)}, u32[]{:S(2)}, u32[]{:S(2)}) collective-permute-start(f32[80,128]{1,0:T(8,128)S(1)} %get-tuple-element.65), channel_id=1, source_target_pairs={{0,16},{16,0},{32,48},{48,32},{64,80},{80,64},{96,112},{112,96},{1... | collective-permute-start | bytes 122888 | tf_op jit(solution)/shard_map/ppermute | solution.py:333
  56.7 4.7 %collective-permute-start.12 = (f32[80,128]{1,0:T(8,128)S(1)}, f32[80,128]{1,0:T(8,128)S(1)}, u32[]{:S(2)}, u32[]{:S(2)}) collective-permute-start(f32[80,128]{1,0:T(8,128)S(1)} %get-tuple-element.66), channel_id=1, source_target_pairs={{0,1},{1,2},{2,3},{3,4},{4,5},{5,6},{6,7},{7,8},{8,9},{9,10},{10,1... | collective-permute-start | bytes 122888 | tf_op jit(solution)/shard_map/ppermute | solution.py:323
  56.7 4.9 %collective-permute-start.13 = (f32[80,128]{1,0:T(8,128)S(1)}, f32[80,128]{1,0:T(8,128)S(1)}, u32[]{:S(2)}, u32[]{:S(2)}) collective-permute-start(f32[80,128]{1,0:T(8,128)S(1)} %get-tuple-element.67), channel_id=1, source_target_pairs={{0,15},{1,0},{2,1},{3,2},{4,3},{5,4},{6,5},{7,6},{8,7},{9,8},{10,9... | collective-permute-start | bytes 122888 | tf_op jit(solution)/shard_map/ppermute | solution.py:323
  64.8 8.0 %collective-permute-start.14 = (f32[80,128]{1,0:T(8,128)S(1)}, f32[80,128]{1,0:T(8,128)S(1)}, u32[]{:S(2)}, u32[]{:S(2)}) collective-permute-start(f32[80,128]{1,0:T(8,128)S(1)} %get-tuple-element.72), channel_id=1, source_target_pairs={{0,496},{16,0},{32,16},{48,32},{64,48},{80,64},{96,80},{112,96},{1... | collective-permute-start | bytes 122888 | tf_op jit(solution)/shard_map/ppermute | solution.py:323
  68.8 4.9 %collective-permute-start.15 = (f32[80,128]{1,0:T(8,128)S(1)}, f32[80,128]{1,0:T(8,128)S(1)}, u32[]{:S(2)}, u32[]{:S(2)}) collective-permute-start(f32[80,128]{1,0:T(8,128)S(1)} %get-tuple-element.73), channel_id=1, source_target_pairs={{0,15},{1,0},{2,1},{3,2},{4,3},{5,4},{6,5},{7,6},{8,7},{9,8},{10,9... | collective-permute-start | bytes 122888 | tf_op jit(solution)/shard_map/ppermute | solution.py:323

commit v3 on v2

--- a/solution.py
+++ b/solution.py
@@ -72,9 +72,21 @@
     return dot_last(first[0], second[0]) + (dot_last(first[0], second[1]) + dot_last(first[1], second[0]))
 
 
+def by_face(value, rows_ref, slot):
+    rows, columns = value.shape
+    parts = []
+    for start in range(0, columns, 128):
+        width = min(128, columns - start)
+        rows_ref[slot, :, :width] = value[:, start : start + width]
+        part = jnp.concatenate([rows_ref[slot, pl.ds(k, rows // 4, stride=4), :] for k in range(4)], axis=0)
+        parts.append(part[:, :width])
+        slot += 1
+    return jnp.concatenate(parts, axis=1)
+
+
 def prepare_kernel(
     table_hbm, inverse_hbm, lifting_hbm, block_hbm, select_ref, weight_ref, scale_ref,
-    table_ref, inverse_ref, lifting_ref, block_ref, semaphores,
+    table_ref, inverse_ref, lifting_ref, block_ref, rows_ref, semaphores,
 ):
     have_table, have_inverse, have_lifting, have_block = fetched(
         (table_hbm, inverse_hbm, lifting_hbm, block_hbm),
@@ -83,14 +95,7 @@
     )
     faces = select_ref.shape[0]
     elements = table_ref.shape[1]
-    trace = block_ref.shape[1]
     shapes = block_ref.shape[0]
-    dofs = trace // 4
-    place = lax.broadcasted_iota(jnp.int32, (trace, trace), 0)
-    k = sum(jnp.where(place >= m * dofs, 1, 0) for m in range(1, 4))
-    order = jnp.where(
-        lax.broadcasted_iota(jnp.int32, (trace, trace), 1) == (place - k * dofs) * 4 + k, 1.0, 0.0
-    ).astype(BF16)
     have_table()
     group = elements // shapes
     ids = lax.broadcasted_iota(jnp.int32, (faces, group), 0)
@@ -106,17 +111,12 @@
     have_lifting()
     have_block()
     for t in range(shapes):
-        lifted = [dot_last(order, part).astype(BF16) for part in halves(lifting_ref[t])]
-        half = three_pass(lifted, halves(inverse_ref[t]))
-        inner = three_pass(halves(half), lifted)
-        turned = [dot_last(order, part).astype(BF16) for part in halves(block_ref[t])]
-        block = [dot_last(part, order) for part in turned]
-        square = block[0] + block[1]
-        block_bound = jnp.maximum(block_bound, jnp.sum(square * square, keepdims=True))
+        lifted = halves(by_face(lifting_ref[t].T, rows_ref, 8 * t))
+        inner = three_pass(halves(three_pass(lifted, halves(inverse_ref[t]))), lifted)
+        block = by_face(by_face(block_ref[t], rows_ref, 8 * t + 2).T, rows_ref, 8 * t + 5)
+        block_bound = jnp.maximum(block_bound, jnp.sum(block * block, keepdims=True))
         inner_bound = jnp.maximum(inner_bound, jnp.sum(inner * inner, keepdims=True))
-        inner_high, inner_low = halves(inner)
-        high = jnp.concatenate([block[0].astype(BF16), inner_high], axis=0)
-        low = jnp.concatenate([block[1].astype(BF16), inner_low], axis=0)
+        high, low = halves(jnp.concatenate([block, inner], axis=0))
         weight_ref[t] = jnp.concatenate([high, high, low], axis=1)
     bound = 4.0 * (6.0 + jnp.sqrt(block_bound) + 2.0 * jnp.sqrt(inner_bound)) + SHIFT
     scale_ref[...] = jnp.broadcast_to(
@@ -155,7 +155,7 @@
     if not final:
         message = [refs.pop(0) for _ in range(4)]
     (wide_ref,) = refs
-    odd = odd_ref[...] != 0
+    odd = odd_ref[:1, :] != 0
 
     dofs, owned = own_ref.shape
     shared = pick_ref.shape[1] // 2
@@ -390,7 +390,7 @@
     select, weights, scale = call(
         prepare_kernel,
         (
-            shape(faces, 4 * elements, dtype=BF16),
+            pltpu.VMEM((faces, 4 * elements), BF16),
             shape(shapes, 2 * trace, 3 * trace, dtype=BF16),
             shape(1, 128),
         ),
@@ -403,13 +403,16 @@
             pltpu.VMEM(inverse.shape, F32),
             pltpu.VMEM(turned.shape, F32),
             pltpu.VMEM(trace_block.shape, F32),
+            pltpu.VMEM((8 * shapes, trace, 128), F32),
             pltpu.SemaphoreType.DMA((4,)),
         ],
         flops=2 * 10**9,
         name="prepare",
         space=pltpu.HBM,
     )
-    odd = jnp.full((1, 128), lax.axis_index("gx") % 2, jnp.int32)
+    odd = jnp.broadcast_to(
+        jnp.stack([lax.axis_index("gx"), lax.axis_index("yz")])[:, None] % 2, (2, 128)
+    ).astype(jnp.int32)
     vectors = [source]
     grams = []
     own, exchanged = source, ghosts

time: 108 us -> 103 us (0.954)
  local copies, waits for them, and re-layouts: 4.12 us -> 0.08 us
  starting transfers between devices: 47 us -> 48.8 us
  Pallas kernels: 20.5 us -> 18.8 us
    unnamed x10 -> x6, local copies, waits for them, and re-layouts: 4.12 us -> 0.01 us
    pallas_call x9, Pallas kernels: 20.5 us -> 18.8 us  [call(): pl.pallas_call(kernel, out_shape=out_shape, in_specs=[pl.BlockSpec(memory...]
    ppermute x10, starting transfers between devices: 26.1 us -> 27.6 us  [passed_along(): return lax.ppermute(value, axis, pairs)]
  transfers between devices with their start and end apart: 16 -> 16, of which waited for: 7 -> 7; matrix products, arithmetic and copies ran while one was open for 0% -> 0% of each run, Pallas kernels for 5% -> 3%
where the time goes in v3:
time: 103 us
  starting transfers between devices  48.8 us (47%)
  blocking collectives  31.5 us (31%)
  Pallas kernels  18.8 us (18%)
  waiting for transfers between devices  3.48 us (3%)
    all_to_all x2, blocking collectives, every(): lax.all_to_all(row.reshape(count, 1, 128), axis, 0, 0).reshape(count, 128)  31.5 us
    ppermute x10, starting transfers between devices, passed_along(): return lax.ppermute(value, axis, pairs)  27.6 us
    ppermute x6, starting transfers between devices, exchange(): return lax.ppermute(value, axis, pairs)  21.2 us
    pallas_call x9, Pallas kernels, call(): pl.pallas_call(kernel, out_shape=out_shape, in_specs=[pl.BlockSpec(memory...  18.8 us
    ppermute x10, waiting for transfers between devices, passed_along(): return lax.ppermute(value, axis, pairs)  3.47 us
  transfers between devices with their start and end apart: 16, of which 7 were waited for; matrix products, arithmetic and copies ran while one was open for 0% of the time, Pallas kernels for 3%

profile of v3, /device:TPU:1, one launch (start us, length us, event | category | flops | bytes accessed | tf_op | source)
XLA Modules:
  0.0 102.9 jit_solution(7527307819029161027)
XLA Ops:
  0.0 0.0 copy-start
  0.0 0.0 copy-start.2
  0.0 0.0 copy-start.1
  0.0 1.3 %first.1 = (bf16[768,256]{1,0:T(8,128)(2,1)S(1)}, f32[80,128]{1,0:T(8,128)S(1)}, f32[80,128]{1,0:T(8,128)S(1)}) custom-call(f32[80,768]{1,0:T(8,128)} %bitcast.17, s32[2,128]{1,0:T(2,128)} %bitcast.36), custom_call_target="tpu_custom_call" | custom-call | bytes 4194304 | tf_op jit(solution)/shard_map/first/pallas_call | solution.py:348
  1.3 3.9 %collective-permute-start = (f32[80,128]{1,0:T(8,128)S(1)}, f32[80,128]{1,0:T(8,128)S(1)}, u32[]{:S(2)}, u32[]{:S(2)}) collective-permute-start(f32[80,128]{1,0:T(8,128)S(1)} %get-tuple-element.42), channel_id=1, source_target_pairs={{0,16},{16,32},{32,48},{48,64},{64,80},{80,96},{96,112},{112,128},... | collective-permute-start | bytes 122888 | tf_op jit(solution)/shard_map/ppermute | solution.py:323
  5.2 2.9 %collective-permute-start.1 = (f32[80,128]{1,0:T(8,128)S(1)}, f32[80,128]{1,0:T(8,128)S(1)}, u32[]{:S(2)}, u32[]{:S(2)}) collective-permute-start(f32[80,128]{1,0:T(8,128)S(1)} %get-tuple-element.43), channel_id=1, source_target_pairs={{0,1},{1,2},{2,3},{3,4},{4,5},{5,6},{6,7},{7,8},{8,9},{9,10},{10,1... | collective-permute-start | bytes 122888 | tf_op jit(solution)/shard_map/ppermute | solution.py:323
  8.2 3.2 %prepare.1 = (bf16[1024,2048]{1,0:T(8,128)(2,1)S(1)}, bf16[2,640,960]{2,1,0:T(8,128)(2,1)S(1)}, f32[1,128]{1,0:T(1,128)S(1)}) custom-call(s32[4,512]{1,0:T(4,128)} %bitcast.38, f32[2,192,192]{2,1,0:T(8,128)} %inverse_hbm.1, f32[2,192,320]{2,1,0:T(8,128)} %bitcast.37, f32[2,320,320]{2,1,0:T(8,128)} %block_hbm.1), custom_call_target="tpu_custom_call" | custom-call | flops 2000000000 | bytes 4194304 | tf_op jit(solution)/shard_map/prepare/pallas_call | solution.py:348
  11.4 0.1 and_select_fusion
  11.5 0.0 collective-permute-done.refs_1_
  11.5 0.0 collective-permute-done.1.refs_2_
  11.5 0.1 broadcast_in_dim.4.refs_9_.refs_14_.refs_15_.refs_16_
  11.6 0.0 copy-done
  11.6 0.0 copy-done.2
  11.6 0.0 copy-done.1
  11.6 2.9 %apply0.1 = (f32[8,128]{1,0:T(8,128)S(1)}, f32[80,768]{1,0:T(8,128)S(1)}, f32[80,128]{1,0:T(8,128)S(1)}, f32[80,128]{1,0:T(8,128)S(1)}, f32[80,128]{1,0:T(8,128)...) custom-call(f32[80,768]{1,0:T(8,128)S(1)} %bitcast.18, ...), custom_call_target="tpu_custom_call" | custom-call | flops 2000000000 | bytes 4194304 | tf_op jit(solution)/shard_map/apply0/pallas_call | solution.py:348
  14.5 6.3 %collective-permute-start.2 = (f32[80,128]{1,0:T(8,128)S(1)}, f32[80,128]{1,0:T(8,128)S(1)}, u32[]{:S(2)}, u32[]{:S(2)}) collective-permute-start(f32[80,128]{1,0:T(8,128)S(1)} %get-tuple-element.49), channel_id=1, source_target_pairs={{0,496},{16,32},{32,16},{48,64},{64,48},{80,96},{96,80},{112,128},... | collective-permute-start | bytes 122888 | tf_op jit(solution)/shard_map/ppermute | solution.py:333
  20.8 1.9 %collective-permute-start.3 = (f32[80,128]{1,0:T(8,128)S(1)}, f32[80,128]{1,0:T(8,128)S(1)}, u32[]{:S(2)}, u32[]{:S(2)}) collective-permute-start(f32[80,128]{1,0:T(8,128)S(1)} %get-tuple-element.50), channel_id=1, source_target_pairs={{0,16},{16,0},{32,48},{48,32},{64,80},{80,64},{96,112},{112,96},{1... | collective-permute-start | bytes 122888 | tf_op jit(solution)/shard_map/ppermute | solution.py:333
  22.7 0.5 collective-permute-start.4
  23.2 4.3 %collective-permute-start.5 = (f32[80,128]{1,0:T(8,128)S(1)}, f32[80,128]{1,0:T(8,128)S(1)}, u32[]{:S(2)}, u32[]{:S(2)}) collective-permute-start(f32[80,128]{1,0:T(8,128)S(1)} %get-tuple-element.52), channel_id=1, source_target_pairs={{0,15},{1,0},{2,1},{3,2},{4,3},{5,4},{6,5},{7,6},{8,7},{9,8},{10,9... | collective-permute-start | bytes 122888 | tf_op jit(solution)/shard_map/ppermute | solution.py:323
  27.4 0.0 collective-permute-done.2.refs_1_
  27.4 0.0 collective-permute-done.3.refs_2_
  27.5 0.7 collective-permute-done.4.refs_3_
  28.1 0.2 collective-permute-done.5.refs_4_
  28.3 3.3 %apply1.1 = (f32[80,768]{1,0:T(8,128)S(1)}, f32[8,128]{1,0:T(8,128)S(1)}, f32[80,768]{1,0:T(8,128)S(1)}, f32[80,128]{1,0:T(8,128)S(1)}, f32[80,128]{1,0:T(8,128)...) custom-call(f32[80,768]{1,0:T(8,128)S(1)} %get-tuple-element.48.refs_0_, ...), custom_call_target="tpu_custom_call" | custom-call | flops 2000000000 | bytes 4194304 | tf_op jit(solution)/shard_map/apply1/pallas_call | solution.py:348
  31.6 4.2 %collective-permute-start.6 = (f32[80,128]{1,0:T(8,128)S(1)}, f32[80,128]{1,0:T(8,128)S(1)}, u32[]{:S(2)}, u32[]{:S(2)}) collective-permute-start(f32[80,128]{1,0:T(8,128)S(1)} %get-tuple-element.56), channel_id=1, source_target_pairs={{0,496},{16,32},{32,16},{48,64},{64,48},{80,96},{96,80},{112,128},... | collective-permute-start | bytes 122888 | tf_op jit(solution)/shard_map/ppermute | solution.py:333
  35.8 1.9 %collective-permute-start.7 = (f32[80,128]{1,0:T(8,128)S(1)}, f32[80,128]{1,0:T(8,128)S(1)}, u32[]{:S(2)}, u32[]{:S(2)}) collective-permute-start(f32[80,128]{1,0:T(8,128)S(1)} %get-tuple-element.57), channel_id=1, source_target_pairs={{0,16},{16,0},{32,48},{48,32},{64,80},{80,64},{96,112},{112,96},{1... | collective-permute-start | bytes 122888 | tf_op jit(solution)/shard_map/ppermute | solution.py:333
  37.7 0.0 collective-permute-start.8
  37.7 4.0 %collective-permute-start.9 = (f32[80,128]{1,0:T(8,128)S(1)}, f32[80,128]{1,0:T(8,128)S(1)}, u32[]{:S(2)}, u32[]{:S(2)}) collective-permute-start(f32[80,128]{1,0:T(8,128)S(1)} %get-tuple-element.59), channel_id=1, source_target_pairs={{0,15},{1,0},{2,1},{3,2},{4,3},{5,4},{6,5},{7,6},{8,7},{9,8},{10,9... | collective-permute-start | bytes 122888 | tf_op jit(solution)/shard_map/ppermute | solution.py:323
  41.8 0.0 collective-permute-done.6.refs_1_
  41.8 0.0 collective-permute-done.7.refs_2_
  41.8 0.7 collective-permute-done.8.refs_3_
  42.5 0.2 collective-permute-done.9.refs_4_
  42.6 3.3 %apply2.1 = (f32[80,768]{1,0:T(8,128)S(1)}, f32[8,128]{1,0:T(8,128)S(1)}, f32[80,768]{1,0:T(8,128)S(1)}, f32[80,128]{1,0:T(8,128)S(1)}, f32[80,128]{1,0:T(8,128)...) custom-call(f32[80,768]{1,0:T(8,128)S(1)} %get-tuple-element.55.refs_0_, ...), custom_call_target="tpu_custom_call" | custom-call | flops 2000000000 | bytes 4194304 | tf_op jit(solution)/shard_map/apply2/pallas_call | solution.py:348
  45.9 4.8 %collective-permute-start.10 = (f32[80,128]{1,0:T(8,128)S(1)}, f32[80,128]{1,0:T(8,128)S(1)}, u32[]{:S(2)}, u32[]{:S(2)}) collective-permute-start(f32[80,128]{1,0:T(8,128)S(1)} %get-tuple-element.64), channel_id=1, source_target_pairs={{0,496},{16,32},{32,16},{48,64},{64,48},{80,96},{96,80},{112,128},... | collective-permute-start | bytes 122888 | tf_op jit(solution)/shard_map/ppermute | solution.py:333
  50.7 2.1 %collective-permute-start.11 = (f32[80,128]{1,0:T(8,128)S(1)}, f32[80,128]{1,0:T(8,128)S(1)}, u32[]{:S(2)}, u32[]{:S(2)}) collective-permute-start(f32[80,128]{1,0:T(8,128)S(1)} %get-tuple-element.65), channel_id=1, source_target_pairs={{0,16},{16,0},{32,48},{48,32},{64,80},{80,64},{96,112},{112,96},{1... | collective-permute-start | bytes 122888 | tf_op jit(solution)/shard_map/ppermute | solution.py:333
  52.9 0.0 collective-permute-start.12
  52.9 4.0 %collective-permute-start.13 = (f32[80,128]{1,0:T(8,128)S(1)}, f32[80,128]{1,0:T(8,128)S(1)}, u32[]{:S(2)}, u32[]{:S(2)}) collective-permute-start(f32[80,128]{1,0:T(8,128)S(1)} %get-tuple-element.67), channel_id=1, source_target_pairs={{0,15},{1,0},{2,1},{3,2},{4,3},{5,4},{6,5},{7,6},{8,7},{9,8},{10,9... | collective-permute-start | bytes 122888 | tf_op jit(solution)/shard_map/ppermute | solution.py:323
  56.9 0.0 collective-permute-done.10.refs_1_
  56.9 0.0 collective-permute-done.11.refs_2_
  56.9 0.7 collective-permute-done.12.refs_3_
  57.6 0.2 collective-permute-done.13.refs_4_
  57.8 3.3 %apply3.1 = (f32[80,768]{1,0:T(8,128)S(1)}, f32[8,128]{1,0:T(8,128)S(1)}, f32[80,768]{1,0:T(8,128)S(1)}, f32[80,128]{1,0:T(8,128)S(1)}, f32[80,128]{1,0:T(8,128)S(1)}) custom-call(f32[80,768]{1,0:T(8,128)S(1)} %get-tuple-element.63.refs_0_, f32[80,128]{1,0:T(8,128)S(1)} %collective-permute-done.10.refs_1_, f32[80,128]{1,0:T(8,128)S(1)} %collective-permute-done.11.refs_2_, ...), custom_call_target="tpu_custom_call" | custom-call | flops 2000000000 | bytes 4194304 | tf_op jit(solution)/shard_map/apply3/pallas_call | solution.py:348
  61.0 3.9 %collective-permute-start.14 = (f32[80,128]{1,0:T(8,128)S(1)}, f32[80,128]{1,0:T(8,128)S(1)}, u32[]{:S(2)}, u32[]{:S(2)}) collective-permute-start(f32[80,128]{1,0:T(8,128)S(1)} %get-tuple-element.72), channel_id=1, source_target_pairs={{0,496},{16,0},{32,16},{48,32},{64,48},{80,64},{96,80},{112,96},{1... | collective-permute-start | bytes 122888 | tf_op jit(solution)/shard_map/ppermute | solution.py:323
  64.9 4.0 %collective-permute-start.15 = (f32[80,128]{1,0:T(8,128)S(1)}, f32[80,128]{1,0:T(8,128)S(1)}, u32[]{:S(2)}, u32[]{:S(2)}) collective-permute-start(f32[80,128]{1,0:T(8,128)S(1)} %get-tuple-element.73), channel_id=1, source_target_pairs={{0,15},{1,0},{2,1},{3,2},{4,3},{5,4},{6,5},{7,6},{8,7},{9,8},{10,9... | collective-permute-start | bytes 122888 | tf_op jit(solution)/shard_map/ppermute | solution.py:323
  68.9 0.0 collective-permute-done.14.refs_1_
  69.0 0.9 collective-permute-done.15.refs_2_
  69.8 0.4 last.1
  70.2 15.6 %all_to_all.10 = f32[16,1,128]{2,1,0:T(1,128)S(1)} all-to-all(f32[16,1,128]{2,1,0:T(1,128)S(1)} %bitcast.26), channel_id=1, replica_groups=mesh['gx'=32,'yz'=16] {'yz'}, dimensions={0} | all-to-all | bytes 16384 | tf_op jit(solution)/shard_map/all_to_all | solution.py:338
  85.9 15.9 %all_to_all.11 = f32[32,1,128]{2,1,0:T(1,128)S(1)} all-to-all(f32[32,1,128]{2,1,0:T(1,128)S(1)} %bitcast.25), channel_id=1, replica_groups=mesh['gx'=32,'yz'=16] {'gx'}, dimensions={0} | all-to-all | bytes 32768 | tf_op jit(solution)/shard_map/all_to_all | solution.py:338
  101.7 1.2 %solve.1 = f32[80,768]{1,0:T(8,128)} custom-call(f32[32,128]{1,0:T(8,128)S(1)} %bitcast.24, f32[1,128]{1,0:T(1,128)S(1)} %get-tuple-element.47.refs_8_.refs_13_.refs_14_.refs_15_.scale_ref, f32[80,768]{1,0:T(8,128)S(1)} %bitcast.23, f32[80,768]{1,0:T(8,128)S(1)} %get-tuple-element.62.refs_8_.refs_4_.refs_1_, ...), custom_call_target="tpu_custom_call" | custom-call | bytes 4194304 | tf_op jit(solution)/shard_map/solve/pallas_call | solution.py:348
  (1 shorter events, 0.0 us)
Async XLA Ops:
  0.0 11.6 %copy-start = (f32[1,1,80,768]{3,2,1,0:T(8,128)S(1)}, f32[1,1,80,768]{3,2,1,0:T(8,128)}, u32[]{:S(2)}) copy-start(f32[1,1,80,768]{3,2,1,0:T(8,128)} %param.8) | copy-start | bytes 737284
  0.0 11.6 %copy-start.2 = (f32[1,1,512]{2,1,0:T(1,128)S(1)}, f32[1,1,512]{2,1,0:T(1,128)}, u32[]{:S(2)}) copy-start(f32[1,1,512]{2,1,0:T(1,128)} %param.12) | copy-start | bytes 6148
  0.0 11.6 %copy-start.1 = (f32[1,1,512]{2,1,0:T(1,128)S(1)}, f32[1,1,512]{2,1,0:T(1,128)}, u32[]{:S(2)}) copy-start(f32[1,1,512]{2,1,0:T(1,128)} %param.11) | copy-start | bytes 6148
  1.3 10.2 %collective-permute-start = (f32[80,128]{1,0:T(8,128)S(1)}, f32[80,128]{1,0:T(8,128)S(1)}, u32[]{:S(2)}, u32[]{:S(2)}) collective-permute-start(f32[80,128]{1,0:T(8,128)S(1)} %get-tuple-element.42), channel_id=1, source_target_pairs={{0,16},{16,32},{32,48},{48,64},{64,80},{80,96},{96,112},{112,128},... | collective-permute-start | bytes 122888 | tf_op jit(solution)/shard_map/ppermute | solution.py:323
  5.2 6.3 %collective-permute-start.1 = (f32[80,128]{1,0:T(8,128)S(1)}, f32[80,128]{1,0:T(8,128)S(1)}, u32[]{:S(2)}, u32[]{:S(2)}) collective-permute-start(f32[80,128]{1,0:T(8,128)S(1)} %get-tuple-element.43), channel_id=1, source_target_pairs={{0,1},{1,2},{2,3},{3,4},{4,5},{5,6},{6,7},{7,8},{8,9},{9,10},{10,1... | collective-permute-start | bytes 122888 | tf_op jit(solution)/shard_map/ppermute | solution.py:323
  14.5 12.9 %collective-permute-start.2 = (f32[80,128]{1,0:T(8,128)S(1)}, f32[80,128]{1,0:T(8,128)S(1)}, u32[]{:S(2)}, u32[]{:S(2)}) collective-permute-start(f32[80,128]{1,0:T(8,128)S(1)} %get-tuple-element.49), channel_id=1, source_target_pairs={{0,496},{16,32},{32,16},{48,64},{64,48},{80,96},{96,80},{112,128},... | collective-permute-start | bytes 122888 | tf_op jit(solution)/shard_map/ppermute | solution.py:333
  20.8 6.7 %collective-permute-start.3 = (f32[80,128]{1,0:T(8,128)S(1)}, f32[80,128]{1,0:T(8,128)S(1)}, u32[]{:S(2)}, u32[]{:S(2)}) collective-permute-start(f32[80,128]{1,0:T(8,128)S(1)} %get-tuple-element.50), channel_id=1, source_target_pairs={{0,16},{16,0},{32,48},{48,32},{64,80},{80,64},{96,112},{112,96},{1... | collective-permute-start | bytes 122888 | tf_op jit(solution)/shard_map/ppermute | solution.py:333
  22.7 5.4 %collective-permute-start.4 = (f32[80,128]{1,0:T(8,128)S(1)}, f32[80,128]{1,0:T(8,128)S(1)}, u32[]{:S(2)}, u32[]{:S(2)}) collective-permute-start(f32[80,128]{1,0:T(8,128)S(1)} %get-tuple-element.51), channel_id=1, source_target_pairs={{0,1},{1,2},{2,3},{3,4},{4,5},{5,6},{6,7},{7,8},{8,9},{9,10},{10,1... | collective-permute-start | bytes 122888 | tf_op jit(solution)/shard_map/ppermute | solution.py:323
  23.2 5.2 %collective-permute-start.5 = (f32[80,128]{1,0:T(8,128)S(1)}, f32[80,128]{1,0:T(8,128)S(1)}, u32[]{:S(2)}, u32[]{:S(2)}) collective-permute-start(f32[80,128]{1,0:T(8,128)S(1)} %get-tuple-element.52), channel_id=1, source_target_pairs={{0,15},{1,0},{2,1},{3,2},{4,3},{5,4},{6,5},{7,6},{8,7},{9,8},{10,9... | collective-permute-start | bytes 122888 | tf_op jit(solution)/shard_map/ppermute | solution.py:323
  31.6 10.2 %collective-permute-start.6 = (f32[80,128]{1,0:T(8,128)S(1)}, f32[80,128]{1,0:T(8,128)S(1)}, u32[]{:S(2)}, u32[]{:S(2)}) collective-permute-start(f32[80,128]{1,0:T(8,128)S(1)} %get-tuple-element.56), channel_id=1, source_target_pairs={{0,496},{16,32},{32,16},{48,64},{64,48},{80,96},{96,80},{112,128},... | collective-permute-start | bytes 122888 | tf_op jit(solution)/shard_map/ppermute | solution.py:333
  35.8 6.0 %collective-permute-start.7 = (f32[80,128]{1,0:T(8,128)S(1)}, f32[80,128]{1,0:T(8,128)S(1)}, u32[]{:S(2)}, u32[]{:S(2)}) collective-permute-start(f32[80,128]{1,0:T(8,128)S(1)} %get-tuple-element.57), channel_id=1, source_target_pairs={{0,16},{16,0},{32,48},{48,32},{64,80},{80,64},{96,112},{112,96},{1... | collective-permute-start | bytes 122888 | tf_op jit(solution)/shard_map/ppermute | solution.py:333
  37.7 4.7 %collective-permute-start.8 = (f32[80,128]{1,0:T(8,128)S(1)}, f32[80,128]{1,0:T(8,128)S(1)}, u32[]{:S(2)}, u32[]{:S(2)}) collective-permute-start(f32[80,128]{1,0:T(8,128)S(1)} %get-tuple-element.58), channel_id=1, source_target_pairs={{0,1},{1,2},{2,3},{3,4},{4,5},{5,6},{6,7},{7,8},{8,9},{9,10},{10,1... | collective-permute-start | bytes 122888 | tf_op jit(solution)/shard_map/ppermute | solution.py:323
  37.7 4.9 %collective-permute-start.9 = (f32[80,128]{1,0:T(8,128)S(1)}, f32[80,128]{1,0:T(8,128)S(1)}, u32[]{:S(2)}, u32[]{:S(2)}) collective-permute-start(f32[80,128]{1,0:T(8,128)S(1)} %get-tuple-element.59), channel_id=1, source_target_pairs={{0,15},{1,0},{2,1},{3,2},{4,3},{5,4},{6,5},{7,6},{8,7},{9,8},{10,9... | collective-permute-start | bytes 122888 | tf_op jit(solution)/shard_map/ppermute | solution.py:323
  45.9 11.0 %collective-permute-start.10 = (f32[80,128]{1,0:T(8,128)S(1)}, f32[80,128]{1,0:T(8,128)S(1)}, u32[]{:S(2)}, u32[]{:S(2)}) collective-permute-start(f32[80,128]{1,0:T(8,128)S(1)} %get-tuple-element.64), channel_id=1, source_target_pairs={{0,496},{16,32},{32,16},{48,64},{64,48},{80,96},{96,80},{112,128},... | collective-permute-start | bytes 122888 | tf_op jit(solution)/shard_map/ppermute | solution.py:333
  50.7 6.2 %collective-permute-start.11 = (f32[80,128]{1,0:T(8,128)S(1)}, f32[80,128]{1,0:T(8,128)S(1)}, u32[]{:S(2)}, u32[]{:S(2)}) collective-permute-start(f32[80,128]{1,0:T(8,128)S(1)} %get-tuple-element.65), channel_id=1, source_target_pairs={{0,16},{16,0},{32,48},{48,32},{64,80},{80,64},{96,112},{112,96},{1... | collective-permute-start | bytes 122888 | tf_op jit(solution)/shard_map/ppermute | solution.py:333
  52.9 4.7 %collective-permute-start.12 = (f32[80,128]{1,0:T(8,128)S(1)}, f32[80,128]{1,0:T(8,128)S(1)}, u32[]{:S(2)}, u32[]{:S(2)}) collective-permute-start(f32[80,128]{1,0:T(8,128)S(1)} %get-tuple-element.66), channel_id=1, source_target_pairs={{0,1},{1,2},{2,3},{3,4},{4,5},{5,6},{6,7},{7,8},{8,9},{9,10},{10,1... | collective-permute-start | bytes 122888 | tf_op jit(solution)/shard_map/ppermute | solution.py:323
  52.9 4.9 %collective-permute-start.13 = (f32[80,128]{1,0:T(8,128)S(1)}, f32[80,128]{1,0:T(8,128)S(1)}, u32[]{:S(2)}, u32[]{:S(2)}) collective-permute-start(f32[80,128]{1,0:T(8,128)S(1)} %get-tuple-element.67), channel_id=1, source_target_pairs={{0,15},{1,0},{2,1},{3,2},{4,3},{5,4},{6,5},{7,6},{8,7},{9,8},{10,9... | collective-permute-start | bytes 122888 | tf_op jit(solution)/shard_map/ppermute | solution.py:323
  61.0 7.9 %collective-permute-start.14 = (f32[80,128]{1,0:T(8,128)S(1)}, f32[80,128]{1,0:T(8,128)S(1)}, u32[]{:S(2)}, u32[]{:S(2)}) collective-permute-start(f32[80,128]{1,0:T(8,128)S(1)} %get-tuple-element.72), channel_id=1, source_target_pairs={{0,496},{16,0},{32,16},{48,32},{64,48},{80,64},{96,80},{112,96},{1... | collective-permute-start | bytes 122888 | tf_op jit(solution)/shard_map/ppermute | solution.py:323
  64.9 4.9 %collective-permute-start.15 = (f32[80,128]{1,0:T(8,128)S(1)}, f32[80,128]{1,0:T(8,128)S(1)}, u32[]{:S(2)}, u32[]{:S(2)}) collective-permute-start(f32[80,128]{1,0:T(8,128)S(1)} %get-tuple-element.73), channel_id=1, source_target_pairs={{0,15},{1,0},{2,1},{3,2},{4,3},{5,4},{6,5},{7,6},{8,7},{9,8},{10,9... | collective-permute-start | bytes 122888 | tf_op jit(solution)/shard_map/ppermute | solution.py:323

commit v4 on v3

--- a/solution.py
+++ b/solution.py
@@ -84,13 +84,24 @@
     return jnp.concatenate(parts, axis=1)
 
 
+def columns(table_ref):
+    table = table_ref[...].astype(F32)
+    return jnp.concatenate([table, jnp.zeros((8 - table.shape[0], table.shape[1]), F32)], axis=0).T
+
+
+def split_index(index):
+    block = index // 128
+    return block.astype(F32).astype(BF16), (index - block * 128).astype(F32).astype(BF16)
+
+
 def prepare_kernel(
-    table_hbm, inverse_hbm, lifting_hbm, block_hbm, select_ref, weight_ref, scale_ref,
-    table_ref, inverse_ref, lifting_ref, block_ref, rows_ref, semaphores,
+    table_hbm, send_hbm, inverse_hbm, lifting_hbm, block_hbm,
+    select_ref, spread_ref, place_ref, weight_ref, scale_ref,
+    table_ref, send_ref, inverse_ref, lifting_ref, block_ref, rows_ref, semaphores,
 ):
-    have_table, have_inverse, have_lifting, have_block = fetched(
-        (table_hbm, inverse_hbm, lifting_hbm, block_hbm),
-        (table_ref, inverse_ref, lifting_ref, block_ref),
+    have_table, have_send, have_inverse, have_lifting, have_block = fetched(
+        (table_hbm, send_hbm, inverse_hbm, lifting_hbm, block_hbm),
+        (table_ref, send_ref, inverse_ref, lifting_ref, block_ref),
         semaphores,
     )
     faces = select_ref.shape[0]
@@ -98,13 +109,28 @@
     shapes = block_ref.shape[0]
     have_table()
     group = elements // shapes
-    ids = lax.broadcasted_iota(jnp.int32, (faces, group), 0)
+    block, place_in = split_index(table_ref[...])
+    down = lax.broadcasted_iota(jnp.int32, (128, group), 0).astype(F32).astype(BF16)
+    one, zero = jnp.ones((), BF16), jnp.zeros((), BF16)
     for t in range(shapes):
+        part = slice(t * group, (t + 1) * group)
         for k in range(4):
             start = (t * 4 + k) * group
-            select_ref[:, start : start + group] = jnp.where(
-                ids == table_ref[k : k + 1, t * group : (t + 1) * group], 1.0, 0.0
-            ).astype(BF16)
+            in_block = jnp.broadcast_to(block[k : k + 1, part], (128, group))
+            hit = jnp.where(jnp.broadcast_to(place_in[k : k + 1, part], (128, group)) == down, one, zero)
+            for b in range(faces // 128):
+                select_ref[b * 128 : (b + 1) * 128, start : start + group] = jnp.where(
+                    in_block == jnp.full((), b, BF16), hit, zero
+                )
+            spread_ref[start : start + group, :] = select_ref[:, start : start + group].T
+    have_send()
+    turned = columns(send_ref)
+    shared, owned = turned.shape[0], place_ref.shape[1]
+    lanes = lax.broadcasted_iota(jnp.int32, (shared, owned), 1).astype(F32)
+    for row in range(2):
+        place_ref[row * shared : (row + 1) * shared, :] = jnp.where(
+            turned[:, row : row + 1] == lanes, 1.0, 0.0
+        ).astype(BF16)
     block_bound = jnp.zeros((1, 1), F32)
     inner_bound = jnp.zeros((1, 1), F32)
     have_inverse()
@@ -145,8 +171,9 @@
         got = [refs.pop(0) for _ in range(4)]
         down = [refs.pop(0) for _ in range(2)]
     vectors = [refs.pop(0) for _ in range(earlier)]
-    select_ref, weight_ref, pick_ref, stabilize_ref, coupling_ref, scale_ref, odd_ref = refs[:7]
-    refs = refs[7:]
+    select_ref, spread_ref, weight_ref, pick_ref, place_ref = refs[:5]
+    stabilize_ref, coupling_ref, scale_ref, odd_ref = refs[5:9]
+    refs = refs[9:]
     if not first:
         vector_ref = refs.pop(0)
     gram_ref = refs.pop(0)
@@ -166,13 +193,13 @@
 
     if first:
         vector = own_ref[...]
-        ghost = jnp.concatenate([ref[...] for ref in ghosts], axis=1)
+        ghost = jnp.concatenate([ref[...] for ref in reversed(ghosts)], axis=1)
     else:
         parts = dict(zip(STARTS, [ref[...] for ref in got]))
         back = [jnp.where(odd, parts["gx later"], parts["gx first"]), parts["yz down"]]
         up = [jnp.where(odd, parts["gx first"], parts["gx later"]), parts["yz up"]]
         received = jnp.concatenate(back, axis=1)
-        vector = own_ref[...] + folded(dot_last(stacked(received), pick_ref[...]))
+        vector = own_ref[...] + folded(dot(stacked(received), place_ref[...]))
         vector_ref[...] = vector
         ghost = jnp.concatenate([a + b[...] for a, b in zip(up, down)], axis=1)
     extended = jnp.concatenate([vector, ghost], axis=1)
@@ -196,7 +223,7 @@
     inner_products([ref[...] for ref in vectors] + [vector], vector, gram_ref, 0)
     gram_ref[earlier + 1 :, :] = jnp.zeros((8 - earlier - 1, 128), F32)
     shrink = 1.0 / scale_ref[:, :1]
-    summed = folded(dot_last(jnp.concatenate(results, axis=1), select_ref[...])) * shrink
+    summed = folded(dot(jnp.concatenate(results, axis=1), spread_ref[...])) * shrink
     part = summed[:, :owned] - (SHIFT * shrink) * vector
     part_ref[...] = part
     for i in range(2):
@@ -219,9 +246,9 @@
     own_ref, slab_ref, section_ref = refs[:3]
     vectors = refs[3 : 3 + ITERS]
     grams = refs[3 + ITERS : 3 + 2 * ITERS]
-    pick_ref, row_ref, sums_ref = refs[3 + 2 * ITERS :]
+    place_ref, row_ref, sums_ref = refs[3 + 2 * ITERS :]
     received = jnp.concatenate([slab_ref[...], section_ref[...]], axis=1)
-    vector = own_ref[...] + folded(dot_last(stacked(received), pick_ref[...]))
+    vector = own_ref[...] + folded(dot(stacked(received), place_ref[...]))
     sums_ref[...] = jnp.zeros(sums_ref.shape, F32)
     for j in range(ITERS):
         start = j * (j + 1) // 2
@@ -385,26 +412,30 @@
         name="first",
         space=pltpu.HBM,
     )
-    ghosts = [passed_along(slab, "gx", 1), passed_along(section, "yz", 1)]
+    ghosts = [passed_along(section, "yz", 1), passed_along(slab, "gx", 1)]
     turned = jnp.swapaxes(lifting, 1, 2)
-    select, weights, scale = call(
+    select, spread, place, weights, scale = call(
         prepare_kernel,
         (
             pltpu.VMEM((faces, 4 * elements), BF16),
+            pltpu.VMEM((4 * elements, faces), BF16),
+            shape(2 * shared, owned, dtype=BF16),
             shape(shapes, 2 * trace, 3 * trace, dtype=BF16),
             shape(1, 128),
         ),
         table,
+        send_lists,
         inverse,
         turned,
         trace_block,
         scratch=[
             pltpu.VMEM(table.shape, jnp.int32),
+            pltpu.VMEM(send_lists.shape, jnp.int32),
             pltpu.VMEM(inverse.shape, F32),
             pltpu.VMEM(turned.shape, F32),
             pltpu.VMEM(trace_block.shape, F32),
             pltpu.VMEM((8 * shapes, trace, 128), F32),
-            pltpu.SemaphoreType.DMA((4,)),
+            pltpu.SemaphoreType.DMA((5,)),
         ],
         flops=2 * 10**9,
         name="prepare",
@@ -431,8 +462,10 @@
             *exchanged,
             *earlier,
             select,
+            spread,
             weights,
             pick,
+            place,
             penalty,
             scaling,
             scale,
@@ -459,7 +492,7 @@
         *exchanged,
         *vectors,
         *grams,
-        pick,
+        place,
         scratch=[pltpu.VMEM((16, 128), F32)],
         name="last",
     )

time: 103 us -> 100 us (0.971)
  starting transfers between devices: 48.8 us -> 46.2 us
  Pallas kernels: 18.8 us -> 16.8 us
  waiting for transfers between devices: 3.48 us -> 4.96 us
    pallas_call x9, Pallas kernels: 18.8 us -> 16.8 us  [call(): pl.pallas_call(kernel, out_shape=out_shape, in_specs=[pl.BlockSpec(memory...]
    ppermute x6, starting transfers between devices: 21.2 us -> 19.5 us  [exchange(): return lax.ppermute(value, axis, pairs)]
    ppermute x10, waiting for transfers between devices: 3.47 us -> 4.94 us  [passed_along(): return lax.ppermute(value, axis, pairs)]
  transfers between devices with their start and end apart: 16 -> 16, of which waited for: 7 -> 8; matrix products, arithmetic and copies ran while one was open for 0% -> 0% of each run, Pallas kernels for 3% -> 4%
where the time goes in v4:
time: 100 us; the launch traced here: 99.7 us
  starting transfers between devices  46.2 us (46%)
  blocking collectives  31.4 us (31%)
  Pallas kernels  16.8 us (17%)
  waiting for transfers between devices  4.96 us (5%)
    all_to_all x2, blocking collectives, every(): lax.all_to_all(row.reshape(count, 1, 128), axis, 0, 0).reshape(count, 128)  31.4 us
    ppermute x10, starting transfers between devices, passed_along(): return lax.ppermute(value, axis, pairs)  26.7 us
    ppermute x6, starting transfers between devices, exchange(): return lax.ppermute(value, axis, pairs)  19.5 us
    pallas_call x9, Pallas kernels, call(): pl.pallas_call(kernel, out_shape=out_shape, in_specs=[pl.BlockSpec(memory...  16.8 us
    ppermute x10, waiting for transfers between devices, passed_along(): return lax.ppermute(value, axis, pairs)  4.94 us
  transfers between devices with their start and end apart: 16, of which 8 were waited for; matrix products, arithmetic and copies ran while one was open for 0% of the time, Pallas kernels for 4%

profile of v4, /device:TPU:1, one launch (start us, length us, event | category | flops | bytes accessed | tf_op | source)
XLA Modules:
  0.0 99.7 jit_solution(12180776381482748314)
XLA Ops:
  0.0 0.0 copy-start
  0.0 0.0 copy-start.2
  0.0 0.0 copy-start.1
  0.0 1.3 %first.1 = (bf16[768,256]{1,0:T(8,128)(2,1)S(1)}, f32[80,128]{1,0:T(8,128)S(1)}, f32[80,128]{1,0:T(8,128)S(1)}) custom-call(f32[80,768]{1,0:T(8,128)} %bitcast.17, s32[2,128]{1,0:T(2,128)} %bitcast.36), custom_call_target="tpu_custom_call" | custom-call | bytes 4194304 | tf_op jit(solution)/shard_map/first/pallas_call | solution.py:375
  1.3 3.5 %collective-permute-start = (f32[80,128]{1,0:T(8,128)S(1)}, f32[80,128]{1,0:T(8,128)S(1)}, u32[]{:S(2)}, u32[]{:S(2)}) collective-permute-start(f32[80,128]{1,0:T(8,128)S(1)} %get-tuple-element.44), channel_id=1, source_target_pairs={{0,1},{1,2},{2,3},{3,4},{4,5},{5,6},{6,7},{7,8},{8,9},{9,10},{10,1... | collective-permute-start | bytes 122888 | tf_op jit(solution)/shard_map/ppermute | solution.py:350
  4.8 3.1 %collective-permute-start.1 = (f32[80,128]{1,0:T(8,128)S(1)}, f32[80,128]{1,0:T(8,128)S(1)}, u32[]{:S(2)}, u32[]{:S(2)}) collective-permute-start(f32[80,128]{1,0:T(8,128)S(1)} %get-tuple-element.45), channel_id=1, source_target_pairs={{0,16},{16,32},{32,48},{48,64},{64,80},{80,96},{96,112},{112,128},... | collective-permute-start | bytes 122888 | tf_op jit(solution)/shard_map/ppermute | solution.py:350
  7.9 4.0 %prepare.1 = (bf16[1024,2048]{1,0:T(8,128)(2,1)S(1)}, bf16[2048,1024]{1,0:T(8,128)(2,1)S(1)}, bf16[256,768]{1,0:T(8,128)(2,1)S(1)}, bf16[2,640,960]{2,1,0:T(8,128)(2,1)S(1)}, f32[1,128]{1,0:T(1,128)S(1)}) custom-call(s32[4,512]{1,0:T(4,128)} %bitcast.39, s32[2,128]{1,0:T(2,128)} %bitcast.37, f32[2,192,192]{2,1,0:T(8,128)} %inverse_hbm.1, ...), custom_call_target="tpu_custom_call" | custom-call | flops 2000000000 | bytes 4194304 | tf_op jit(solution)/shard_map/prepare/pallas_call | solution.py:375
  11.9 0.1 and_select_fusion
  12.0 0.0 collective-permute-done.refs_1_
  12.0 1.5 %collective-permute-done.1.refs_2_ = f32[80,128]{1,0:T(8,128)S(1)} collective-permute-done((f32[80,128]{1,0:T(8,128)S(1)}, f32[80,128]{1,0:T(8,128)S(1)}, u32[]{:S(2)}, u32[]{:S(2)}) %collective-permute-start.1) | collective-permute-done | bytes 40992 | tf_op jit(solution)/shard_map/ppermute | solution.py:350
  13.4 0.1 broadcast_in_dim.4.refs_11_.refs_16_.refs_17_.refs_18_
  13.5 0.0 copy-done
  13.5 0.0 copy-done.2
  13.5 0.0 copy-done.1
  13.5 2.4 %apply0.1 = (f32[8,128]{1,0:T(8,128)S(1)}, f32[80,768]{1,0:T(8,128)S(1)}, f32[80,128]{1,0:T(8,128)S(1)}, f32[80,128]{1,0:T(8,128)S(1)}, f32[80,128]{1,0:T(8,128)...) custom-call(f32[80,768]{1,0:T(8,128)S(1)} %bitcast.18, ...), custom_call_target="tpu_custom_call" | custom-call | flops 2000000000 | bytes 4194304 | tf_op jit(solution)/shard_map/apply0/pallas_call | solution.py:375
  15.9 4.6 %collective-permute-start.2 = (f32[80,128]{1,0:T(8,128)S(1)}, f32[80,128]{1,0:T(8,128)S(1)}, u32[]{:S(2)}, u32[]{:S(2)}) collective-permute-start(f32[80,128]{1,0:T(8,128)S(1)} %get-tuple-element.53), channel_id=1, source_target_pairs={{0,496},{16,32},{32,16},{48,64},{64,48},{80,96},{96,80},{112,128},... | collective-permute-start | bytes 122888 | tf_op jit(solution)/shard_map/ppermute | solution.py:360
  20.5 1.9 %collective-permute-start.3 = (f32[80,128]{1,0:T(8,128)S(1)}, f32[80,128]{1,0:T(8,128)S(1)}, u32[]{:S(2)}, u32[]{:S(2)}) collective-permute-start(f32[80,128]{1,0:T(8,128)S(1)} %get-tuple-element.54), channel_id=1, source_target_pairs={{0,16},{16,0},{32,48},{48,32},{64,80},{80,64},{96,112},{112,96},{1... | collective-permute-start | bytes 122888 | tf_op jit(solution)/shard_map/ppermute | solution.py:360
  22.4 0.3 collective-permute-start.4
  22.8 3.1 %collective-permute-start.5 = (f32[80,128]{1,0:T(8,128)S(1)}, f32[80,128]{1,0:T(8,128)S(1)}, u32[]{:S(2)}, u32[]{:S(2)}) collective-permute-start(f32[80,128]{1,0:T(8,128)S(1)} %get-tuple-element.56), channel_id=1, source_target_pairs={{0,15},{1,0},{2,1},{3,2},{4,3},{5,4},{6,5},{7,6},{8,7},{9,8},{10,9... | collective-permute-start | bytes 122888 | tf_op jit(solution)/shard_map/ppermute | solution.py:350
  25.8 0.0 collective-permute-done.2.refs_1_
  25.9 0.0 collective-permute-done.3.refs_2_
  25.9 0.7 collective-permute-done.4.refs_3_
  26.5 0.2 collective-permute-done.5.refs_4_
  26.7 2.6 %apply1.1 = (f32[80,768]{1,0:T(8,128)S(1)}, f32[8,128]{1,0:T(8,128)S(1)}, f32[80,768]{1,0:T(8,128)S(1)}, f32[80,128]{1,0:T(8,128)S(1)}, f32[80,128]{1,0:T(8,128)...) custom-call(f32[80,768]{1,0:T(8,128)S(1)} %get-tuple-element.52.refs_0_, ...), custom_call_target="tpu_custom_call" | custom-call | flops 2000000000 | bytes 4194304 | tf_op jit(solution)/shard_map/apply1/pallas_call | solution.py:375
  29.3 4.9 %collective-permute-start.6 = (f32[80,128]{1,0:T(8,128)S(1)}, f32[80,128]{1,0:T(8,128)S(1)}, u32[]{:S(2)}, u32[]{:S(2)}) collective-permute-start(f32[80,128]{1,0:T(8,128)S(1)} %get-tuple-element.60), channel_id=1, source_target_pairs={{0,496},{16,32},{32,16},{48,64},{64,48},{80,96},{96,80},{112,128},... | collective-permute-start | bytes 122888 | tf_op jit(solution)/shard_map/ppermute | solution.py:360
  34.2 1.9 %collective-permute-start.7 = (f32[80,128]{1,0:T(8,128)S(1)}, f32[80,128]{1,0:T(8,128)S(1)}, u32[]{:S(2)}, u32[]{:S(2)}) collective-permute-start(f32[80,128]{1,0:T(8,128)S(1)} %get-tuple-element.61), channel_id=1, source_target_pairs={{0,16},{16,0},{32,48},{48,32},{64,80},{80,64},{96,112},{112,96},{1... | collective-permute-start | bytes 122888 | tf_op jit(solution)/shard_map/ppermute | solution.py:360
  36.1 0.4 collective-permute-start.8
  36.5 3.7 %collective-permute-start.9 = (f32[80,128]{1,0:T(8,128)S(1)}, f32[80,128]{1,0:T(8,128)S(1)}, u32[]{:S(2)}, u32[]{:S(2)}) collective-permute-start(f32[80,128]{1,0:T(8,128)S(1)} %get-tuple-element.63), channel_id=1, source_target_pairs={{0,15},{1,0},{2,1},{3,2},{4,3},{5,4},{6,5},{7,6},{8,7},{9,8},{10,9... | collective-permute-start | bytes 122888 | tf_op jit(solution)/shard_map/ppermute | solution.py:350
  40.2 0.0 collective-permute-done.6.refs_1_
  40.2 0.0 collective-permute-done.7.refs_2_
  40.2 0.7 collective-permute-done.8.refs_3_
  40.8 0.2 collective-permute-done.9.refs_4_
  41.0 2.6 %apply2.1 = (f32[80,768]{1,0:T(8,128)S(1)}, f32[8,128]{1,0:T(8,128)S(1)}, f32[80,768]{1,0:T(8,128)S(1)}, f32[80,128]{1,0:T(8,128)S(1)}, f32[80,128]{1,0:T(8,128)...) custom-call(f32[80,768]{1,0:T(8,128)S(1)} %get-tuple-element.59.refs_0_, ...), custom_call_target="tpu_custom_call" | custom-call | flops 2000000000 | bytes 4194304 | tf_op jit(solution)/shard_map/apply2/pallas_call | solution.py:375
  43.6 4.1 %collective-permute-start.10 = (f32[80,128]{1,0:T(8,128)S(1)}, f32[80,128]{1,0:T(8,128)S(1)}, u32[]{:S(2)}, u32[]{:S(2)}) collective-permute-start(f32[80,128]{1,0:T(8,128)S(1)} %get-tuple-element.68), channel_id=1, source_target_pairs={{0,496},{16,32},{32,16},{48,64},{64,48},{80,96},{96,80},{112,128},... | collective-permute-start | bytes 122888 | tf_op jit(solution)/shard_map/ppermute | solution.py:360
  47.7 2.1 %collective-permute-start.11 = (f32[80,128]{1,0:T(8,128)S(1)}, f32[80,128]{1,0:T(8,128)S(1)}, u32[]{:S(2)}, u32[]{:S(2)}) collective-permute-start(f32[80,128]{1,0:T(8,128)S(1)} %get-tuple-element.69), channel_id=1, source_target_pairs={{0,16},{16,0},{32,48},{48,32},{64,80},{80,64},{96,112},{112,96},{1... | collective-permute-start | bytes 122888 | tf_op jit(solution)/shard_map/ppermute | solution.py:360
  49.8 0.0 collective-permute-start.12
  49.8 4.0 %collective-permute-start.13 = (f32[80,128]{1,0:T(8,128)S(1)}, f32[80,128]{1,0:T(8,128)S(1)}, u32[]{:S(2)}, u32[]{:S(2)}) collective-permute-start(f32[80,128]{1,0:T(8,128)S(1)} %get-tuple-element.71), channel_id=1, source_target_pairs={{0,15},{1,0},{2,1},{3,2},{4,3},{5,4},{6,5},{7,6},{8,7},{9,8},{10,9... | collective-permute-start | bytes 122888 | tf_op jit(solution)/shard_map/ppermute | solution.py:350
  53.9 0.0 collective-permute-done.10.refs_1_
  53.9 0.0 collective-permute-done.11.refs_2_
  53.9 0.7 collective-permute-done.12.refs_3_
  54.5 0.2 collective-permute-done.13.refs_4_
  54.7 2.5 %apply3.1 = (f32[80,768]{1,0:T(8,128)S(1)}, f32[8,128]{1,0:T(8,128)S(1)}, f32[80,768]{1,0:T(8,128)S(1)}, f32[80,128]{1,0:T(8,128)S(1)}, f32[80,128]{1,0:T(8,128)S(1)}) custom-call(f32[80,768]{1,0:T(8,128)S(1)} %get-tuple-element.67.refs_0_, f32[80,128]{1,0:T(8,128)S(1)} %collective-permute-done.10.refs_1_, f32[80,128]{1,0:T(8,128)S(1)} %collective-permute-done.11.refs_2_, ...), custom_call_target="tpu_custom_call" | custom-call | flops 2000000000 | bytes 4194304 | tf_op jit(solution)/shard_map/apply3/pallas_call | solution.py:375
  57.3 4.6 %collective-permute-start.14 = (f32[80,128]{1,0:T(8,128)S(1)}, f32[80,128]{1,0:T(8,128)S(1)}, u32[]{:S(2)}, u32[]{:S(2)}) collective-permute-start(f32[80,128]{1,0:T(8,128)S(1)} %get-tuple-element.76), channel_id=1, source_target_pairs={{0,496},{16,0},{32,16},{48,32},{64,48},{80,64},{96,80},{112,96},{1... | collective-permute-start | bytes 122888 | tf_op jit(solution)/shard_map/ppermute | solution.py:350
  61.8 4.0 %collective-permute-start.15 = (f32[80,128]{1,0:T(8,128)S(1)}, f32[80,128]{1,0:T(8,128)S(1)}, u32[]{:S(2)}, u32[]{:S(2)}) collective-permute-start(f32[80,128]{1,0:T(8,128)S(1)} %get-tuple-element.77), channel_id=1, source_target_pairs={{0,15},{1,0},{2,1},{3,2},{4,3},{5,4},{6,5},{7,6},{8,7},{9,8},{10,9... | collective-permute-start | bytes 122888 | tf_op jit(solution)/shard_map/ppermute | solution.py:350
  65.8 0.0 collective-permute-done.14.refs_1_
  65.8 0.9 collective-permute-done.15.refs_2_
  66.7 0.4 last.1
  67.1 15.8 %all_to_all.10 = f32[16,1,128]{2,1,0:T(1,128)S(1)} all-to-all(f32[16,1,128]{2,1,0:T(1,128)S(1)} %bitcast.34), channel_id=1, replica_groups=mesh['gx'=32,'yz'=16] {'yz'}, dimensions={0} | all-to-all | bytes 16384 | tf_op jit(solution)/shard_map/all_to_all | solution.py:365
  83.0 15.6 %all_to_all.11 = f32[32,1,128]{2,1,0:T(1,128)S(1)} all-to-all(f32[32,1,128]{2,1,0:T(1,128)S(1)} %bitcast.25), channel_id=1, replica_groups=mesh['gx'=32,'yz'=16] {'gx'}, dimensions={0} | all-to-all | bytes 32768 | tf_op jit(solution)/shard_map/all_to_all | solution.py:365
  98.5 1.2 %solve.1 = f32[80,768]{1,0:T(8,128)} custom-call(f32[32,128]{1,0:T(8,128)S(1)} %bitcast.24, f32[1,128]{1,0:T(1,128)S(1)} %get-tuple-element.51.refs_10_.refs_15_.refs_16_.refs_17_.scale_ref, f32[80,768]{1,0:T(8,128)S(1)} %bitcast.23, f32[80,768]{1,0:T(8,128)S(1)} %get-tuple-element.66.refs_8_.refs_4_.refs_1_, ...), custom_call_target="tpu_custom_call" | custom-call | bytes 4194304 | tf_op jit(solution)/shard_map/solve/pallas_call | solution.py:375
  (1 shorter events, 0.0 us)
Async XLA Ops:
  0.0 13.5 %copy-start = (f32[1,1,80,768]{3,2,1,0:T(8,128)S(1)}, f32[1,1,80,768]{3,2,1,0:T(8,128)}, u32[]{:S(2)}) copy-start(f32[1,1,80,768]{3,2,1,0:T(8,128)} %param.8) | copy-start | bytes 737284
  0.0 13.5 %copy-start.2 = (f32[1,1,512]{2,1,0:T(1,128)S(1)}, f32[1,1,512]{2,1,0:T(1,128)}, u32[]{:S(2)}) copy-start(f32[1,1,512]{2,1,0:T(1,128)} %param.12) | copy-start | bytes 6148
  0.0 13.5 %copy-start.1 = (f32[1,1,512]{2,1,0:T(1,128)S(1)}, f32[1,1,512]{2,1,0:T(1,128)}, u32[]{:S(2)}) copy-start(f32[1,1,512]{2,1,0:T(1,128)} %param.11) | copy-start | bytes 6148
  1.3 10.7 %collective-permute-start = (f32[80,128]{1,0:T(8,128)S(1)}, f32[80,128]{1,0:T(8,128)S(1)}, u32[]{:S(2)}, u32[]{:S(2)}) collective-permute-start(f32[80,128]{1,0:T(8,128)S(1)} %get-tuple-element.44), channel_id=1, source_target_pairs={{0,1},{1,2},{2,3},{3,4},{4,5},{5,6},{6,7},{7,8},{8,9},{9,10},{10,1... | collective-permute-start | bytes 122888 | tf_op jit(solution)/shard_map/ppermute | solution.py:350
  4.8 8.7 %collective-permute-start.1 = (f32[80,128]{1,0:T(8,128)S(1)}, f32[80,128]{1,0:T(8,128)S(1)}, u32[]{:S(2)}, u32[]{:S(2)}) collective-permute-start(f32[80,128]{1,0:T(8,128)S(1)} %get-tuple-element.45), channel_id=1, source_target_pairs={{0,16},{16,32},{32,48},{48,64},{64,80},{80,96},{96,112},{112,128},... | collective-permute-start | bytes 122888 | tf_op jit(solution)/shard_map/ppermute | solution.py:350
  15.9 10.0 %collective-permute-start.2 = (f32[80,128]{1,0:T(8,128)S(1)}, f32[80,128]{1,0:T(8,128)S(1)}, u32[]{:S(2)}, u32[]{:S(2)}) collective-permute-start(f32[80,128]{1,0:T(8,128)S(1)} %get-tuple-element.53), channel_id=1, source_target_pairs={{0,496},{16,32},{32,16},{48,64},{64,48},{80,96},{96,80},{112,128},... | collective-permute-start | bytes 122888 | tf_op jit(solution)/shard_map/ppermute | solution.py:360
  20.5 5.3 %collective-permute-start.3 = (f32[80,128]{1,0:T(8,128)S(1)}, f32[80,128]{1,0:T(8,128)S(1)}, u32[]{:S(2)}, u32[]{:S(2)}) collective-permute-start(f32[80,128]{1,0:T(8,128)S(1)} %get-tuple-element.54), channel_id=1, source_target_pairs={{0,16},{16,0},{32,48},{48,32},{64,80},{80,64},{96,112},{112,96},{1... | collective-permute-start | bytes 122888 | tf_op jit(solution)/shard_map/ppermute | solution.py:360
  22.4 4.1 %collective-permute-start.4 = (f32[80,128]{1,0:T(8,128)S(1)}, f32[80,128]{1,0:T(8,128)S(1)}, u32[]{:S(2)}, u32[]{:S(2)}) collective-permute-start(f32[80,128]{1,0:T(8,128)S(1)} %get-tuple-element.55), channel_id=1, source_target_pairs={{0,1},{1,2},{2,3},{3,4},{4,5},{5,6},{6,7},{7,8},{8,9},{9,10},{10,1... | collective-permute-start | bytes 122888 | tf_op jit(solution)/shard_map/ppermute | solution.py:350
  22.8 4.0 %collective-permute-start.5 = (f32[80,128]{1,0:T(8,128)S(1)}, f32[80,128]{1,0:T(8,128)S(1)}, u32[]{:S(2)}, u32[]{:S(2)}) collective-permute-start(f32[80,128]{1,0:T(8,128)S(1)} %get-tuple-element.56), channel_id=1, source_target_pairs={{0,15},{1,0},{2,1},{3,2},{4,3},{5,4},{6,5},{7,6},{8,7},{9,8},{10,9... | collective-permute-start | bytes 122888 | tf_op jit(solution)/shard_map/ppermute | solution.py:350
  29.3 10.9 %collective-permute-start.6 = (f32[80,128]{1,0:T(8,128)S(1)}, f32[80,128]{1,0:T(8,128)S(1)}, u32[]{:S(2)}, u32[]{:S(2)}) collective-permute-start(f32[80,128]{1,0:T(8,128)S(1)} %get-tuple-element.60), channel_id=1, source_target_pairs={{0,496},{16,32},{32,16},{48,64},{64,48},{80,96},{96,80},{112,128},... | collective-permute-start | bytes 122888 | tf_op jit(solution)/shard_map/ppermute | solution.py:360
  34.2 6.0 %collective-permute-start.7 = (f32[80,128]{1,0:T(8,128)S(1)}, f32[80,128]{1,0:T(8,128)S(1)}, u32[]{:S(2)}, u32[]{:S(2)}) collective-permute-start(f32[80,128]{1,0:T(8,128)S(1)} %get-tuple-element.61), channel_id=1, source_target_pairs={{0,16},{16,0},{32,48},{48,32},{64,80},{80,64},{96,112},{112,96},{1... | collective-permute-start | bytes 122888 | tf_op jit(solution)/shard_map/ppermute | solution.py:360
  36.1 4.8 %collective-permute-start.8 = (f32[80,128]{1,0:T(8,128)S(1)}, f32[80,128]{1,0:T(8,128)S(1)}, u32[]{:S(2)}, u32[]{:S(2)}) collective-permute-start(f32[80,128]{1,0:T(8,128)S(1)} %get-tuple-element.62), channel_id=1, source_target_pairs={{0,1},{1,2},{2,3},{3,4},{4,5},{5,6},{6,7},{7,8},{8,9},{9,10},{10,1... | collective-permute-start | bytes 122888 | tf_op jit(solution)/shard_map/ppermute | solution.py:350
  36.5 4.5 %collective-permute-start.9 = (f32[80,128]{1,0:T(8,128)S(1)}, f32[80,128]{1,0:T(8,128)S(1)}, u32[]{:S(2)}, u32[]{:S(2)}) collective-permute-start(f32[80,128]{1,0:T(8,128)S(1)} %get-tuple-element.63), channel_id=1, source_target_pairs={{0,15},{1,0},{2,1},{3,2},{4,3},{5,4},{6,5},{7,6},{8,7},{9,8},{10,9... | collective-permute-start | bytes 122888 | tf_op jit(solution)/shard_map/ppermute | solution.py:350
  43.6 10.2 %collective-permute-start.10 = (f32[80,128]{1,0:T(8,128)S(1)}, f32[80,128]{1,0:T(8,128)S(1)}, u32[]{:S(2)}, u32[]{:S(2)}) collective-permute-start(f32[80,128]{1,0:T(8,128)S(1)} %get-tuple-element.68), channel_id=1, source_target_pairs={{0,496},{16,32},{32,16},{48,64},{64,48},{80,96},{96,80},{112,128},... | collective-permute-start | bytes 122888 | tf_op jit(solution)/shard_map/ppermute | solution.py:360
  47.7 6.2 %collective-permute-start.11 = (f32[80,128]{1,0:T(8,128)S(1)}, f32[80,128]{1,0:T(8,128)S(1)}, u32[]{:S(2)}, u32[]{:S(2)}) collective-permute-start(f32[80,128]{1,0:T(8,128)S(1)} %get-tuple-element.69), channel_id=1, source_target_pairs={{0,16},{16,0},{32,48},{48,32},{64,80},{80,64},{96,112},{112,96},{1... | collective-permute-start | bytes 122888 | tf_op jit(solution)/shard_map/ppermute | solution.py:360
  49.8 4.8 %collective-permute-start.12 = (f32[80,128]{1,0:T(8,128)S(1)}, f32[80,128]{1,0:T(8,128)S(1)}, u32[]{:S(2)}, u32[]{:S(2)}) collective-permute-start(f32[80,128]{1,0:T(8,128)S(1)} %get-tuple-element.70), channel_id=1, source_target_pairs={{0,1},{1,2},{2,3},{3,4},{4,5},{5,6},{6,7},{7,8},{8,9},{9,10},{10,1... | collective-permute-start | bytes 122888 | tf_op jit(solution)/shard_map/ppermute | solution.py:350
  49.8 4.9 %collective-permute-start.13 = (f32[80,128]{1,0:T(8,128)S(1)}, f32[80,128]{1,0:T(8,128)S(1)}, u32[]{:S(2)}, u32[]{:S(2)}) collective-permute-start(f32[80,128]{1,0:T(8,128)S(1)} %get-tuple-element.71), channel_id=1, source_target_pairs={{0,15},{1,0},{2,1},{3,2},{4,3},{5,4},{6,5},{7,6},{8,7},{9,8},{10,9... | collective-permute-start | bytes 122888 | tf_op jit(solution)/shard_map/ppermute | solution.py:350
  57.3 8.6 %collective-permute-start.14 = (f32[80,128]{1,0:T(8,128)S(1)}, f32[80,128]{1,0:T(8,128)S(1)}, u32[]{:S(2)}, u32[]{:S(2)}) collective-permute-start(f32[80,128]{1,0:T(8,128)S(1)} %get-tuple-element.76), channel_id=1, source_target_pairs={{0,496},{16,0},{32,16},{48,32},{64,48},{80,64},{96,80},{112,96},{1... | collective-permute-start | bytes 122888 | tf_op jit(solution)/shard_map/ppermute | solution.py:350
  61.8 4.9 %collective-permute-start.15 = (f32[80,128]{1,0:T(8,128)S(1)}, f32[80,128]{1,0:T(8,128)S(1)}, u32[]{:S(2)}, u32[]{:S(2)}) collective-permute-start(f32[80,128]{1,0:T(8,128)S(1)} %get-tuple-element.77), channel_id=1, source_target_pairs={{0,15},{1,0},{2,1},{3,2},{4,3},{5,4},{6,5},{7,6},{8,7},{9,8},{10,9... | collective-permute-start | bytes 122888 | tf_op jit(solution)/shard_map/ppermute | solution.py:350

commit v5 on v4

v5 whole, which is shorter than its diff:
```python
import functools

import jax
import jax.numpy as jnp
from jax import lax
from jax.experimental import pallas as pl
from jax.experimental.pallas import tpu as pltpu
from jax.sharding import PartitionSpec as P

ITERS = 4
EPSILON = 1e-06
SHIFT = 12.0
NORM_ROOM = 1024.0
F32 = jnp.float32
BF16 = jnp.bfloat16
STARTS = ("gx later", "gx first", "yz up", "yz down")
PAIRS = [(i, j) for j in range(ITERS + 1) for i in range(j + 1)]
VMEM_BYTES = 20 * 1024 * 1024


def halves(value):
    high = value.astype(BF16)
    return high, (value - high.astype(F32)).astype(BF16)


def stacked(value):
    return jnp.concatenate(halves(value), axis=0)


def folded(value):
    half = value.shape[0] // 2
    return value[:half] + value[half:]


def dot(first, second):
    return jnp.dot(first, second, preferred_element_type=F32)


def dot_last(first, second, precision=None):
    return lax.dot_general(
        first, second, (((1,), (1,)), ((), ())), preferred_element_type=F32, precision=precision
    )


def fetched(sources, targets, semaphores):
    copies = [
        pltpu.make_async_copy(source, target, semaphores.at[k])
        for k, (source, target) in enumerate(zip(sources, targets))
    ]
    for copy in copies:
        copy.start()
    return [copy.wait for copy in copies]


def first_kernel(source_hbm, send_hbm, slab_ref, section_ref, send_ref, source_ref, semaphores):
    have_send, have_source = fetched((send_hbm, source_hbm), (send_ref, source_ref), semaphores)
    owned = source_ref.shape[1]
    shared = send_ref.shape[1]
    faces = lax.broadcasted_iota(jnp.int32, (owned, shared), 0)
    have_send()
    pick = jnp.concatenate(
        [jnp.where(faces == send_ref[row : row + 1, :], 1.0, 0.0).astype(BF16) for row in range(2)], axis=1
    )
    have_source()
    sent = folded(dot(stacked(source_ref[...]), pick))
    slab_ref[...] = sent[:, :shared]
    section_ref[...] = sent[:, shared:]


def three_pass(first, second):
    return dot_last(first[0], second[0]) + (dot_last(first[0], second[1]) + dot_last(first[1], second[0]))


def by_face(value, rows_ref, slot):
    rows, columns = value.shape
    parts = []
    for start in range(0, columns, 128):
        width = min(128, columns - start)
        rows_ref[slot, :, :width] = value[:, start : start + width]
        part = jnp.concatenate([rows_ref[slot, pl.ds(k, rows // 4, stride=4), :] for k in range(4)], axis=0)
        parts.append(part[:, :width])
        slot += 1
    return jnp.concatenate(parts, axis=1)


def columns(table_ref):
    table = table_ref[...].astype(F32)
    return jnp.concatenate([table, jnp.zeros((8 - table.shape[0], table.shape[1]), F32)], axis=0).T


def split_index(index):
    block = index // 128
    return block.astype(F32).astype(BF16), (index - block * 128).astype(F32).astype(BF16)


def tables_kernel(
    shapes, table_hbm, send_ref, select_ref, spread_ref, meet_ref, leave_ref, place_ref, table_ref, semaphores
):
    (have_table,) = fetched((table_hbm,), (table_ref,), semaphores)
    faces = select_ref.shape[0]
    elements = table_ref.shape[1]
    sends = columns(send_ref)
    shared, owned = sends.shape[0], place_ref.shape[1]
    lanes = lax.broadcasted_iota(jnp.int32, (shared, owned), 1).astype(F32)
    for row in range(2):
        place_ref[row * shared : (row + 1) * shared, :] = jnp.where(
            sends[:, row : row + 1] == lanes, 1.0, 0.0
        ).astype(BF16)
    group = elements // shapes
    have_table()
    block, place_in = split_index(table_ref[...])
    table = table_ref[...].astype(F32)
    down = lax.broadcasted_iota(jnp.int32, (128, group), 0).astype(F32).astype(BF16)
    one, zero = jnp.ones((), BF16), jnp.zeros((), BF16)
    for t in range(shapes):
        part = slice(t * group, (t + 1) * group)
        for k in range(4):
            start = (t * 4 + k) * group
            in_block = jnp.broadcast_to(block[k : k + 1, part], (128, group))
            hit = jnp.where(jnp.broadcast_to(place_in[k : k + 1, part], (128, group)) == down, one, zero)
            for b in range(faces // 128):
                select_ref[b * 128 : (b + 1) * 128, start : start + group] = jnp.where(
                    in_block == jnp.full((), b, BF16), hit, zero
                )
            spread_ref[start : start + group, :] = select_ref[:owned, start : start + group].T
            row = table[k : k + 1, part]
            for i in range(2):
                meet_ref[i * shared : (i + 1) * shared, start : start + group] = jnp.where(
                    sends[:, i : i + 1] == row, 1.0, 0.0
                ).astype(BF16)
            meet_ref[2 * shared :, start : start + group] = select_ref[owned:, start : start + group]
            leave_ref[start : start + group, :] = meet_ref[:, start : start + group].T


def weights_kernel(inverse_ref, lifting_ref, block_ref, weight_ref, scale_ref, rows_ref):
    shapes = block_ref.shape[0]
    block_bound = jnp.zeros((1, 1), F32)
    inner_bound = jnp.zeros((1, 1), F32)
    for t in range(shapes):
        lifted = halves(by_face(lifting_ref[t].T, rows_ref, 8 * t))
        inner = three_pass(halves(three_pass(lifted, halves(inverse_ref[t]))), lifted)
        block = by_face(by_face(block_ref[t], rows_ref, 8 * t + 2).T, rows_ref, 8 * t + 5)
        block_bound = jnp.maximum(block_bound, jnp.sum(block * block, keepdims=True))
        inner_bound = jnp.maximum(inner_bound, jnp.sum(inner * inner, keepdims=True))
        high, low = halves(jnp.concatenate([block, inner], axis=0))
        weight_ref[t] = jnp.concatenate([high, high, low], axis=1)
    bound = 4.0 * (6.0 + jnp.sqrt(block_bound) + 2.0 * jnp.sqrt(inner_bound)) + SHIFT
    scale_ref[...] = jnp.broadcast_to(
        jnp.maximum(1.0, bound * (1.0 / NORM_ROOM)), scale_ref.shape
    )


def inner_products(vectors, last, gram_ref, first_row):
    for i, vector in enumerate(vectors):
        gram_ref[first_row + i : first_row + i + 1, :] = lane_sums(vector * last)


def lane_sums(product):
    total = product[:, :128]
    for start in range(128, product.shape[1], 128):
        total = total + product[:, start : start + 128]
    return jnp.sum(total, axis=0, keepdims=True)


def arrived(got, odd):
    parts = dict(zip(STARTS, [ref[...] for ref in got]))
    back = [jnp.where(odd, parts["gx later"], parts["gx first"]), parts["yz down"]]
    up = [jnp.where(odd, parts["gx first"], parts["gx later"]), parts["yz up"]]
    return back, up


def gather_kernel(source_ref, select_ref, known_ref):
    known_ref[...] = folded(dot(stacked(source_ref[...]), select_ref[: source_ref.shape[1], :]))


def step_kernel(first, final, *refs):
    refs = list(refs)
    known_ref = refs.pop(0)
    got = [refs.pop(0) for _ in range(2 if first else 4)]
    sent_before = [refs.pop(0) for _ in range(2 if first else 1)]
    meet_ref, leave_ref, weight_ref, stabilize_ref, coupling_ref, scale_ref, odd_ref = refs[:7]
    result_ref, down_ref = refs[7:9]
    odd = odd_ref[:1, :] != 0
    dofs = known_ref.shape[0]
    shared = down_ref.shape[1] // 2
    shapes = weight_ref.shape[0]
    group = stabilize_ref.shape[1] // shapes
    trace = 4 * dofs

    own = jnp.concatenate([ref[...] for ref in sent_before], axis=1)
    if first:
        section, slab = [ref[...] for ref in got]
        arrivals = jnp.concatenate([slab, section], axis=1)
        read = folded(dot(stacked(arrivals), meet_ref[2 * shared :, :]))
    else:
        back, up = arrived(got, odd)
        own = own + jnp.concatenate(back, axis=1)
        read = folded(dot(stacked(jnp.concatenate(back + up, axis=1)), meet_ref[...]))
    read = known_ref[...] + read
    for t in range(shapes):
        columns = slice(t * group, (t + 1) * group)
        values = jnp.concatenate(
            [read[:, (t * 4 + k) * group : (t * 4 + k + 1) * group] for k in range(4)], axis=0
        )
        high, low = halves(values)
        product = dot(weight_ref[t], jnp.concatenate([high, low, high], axis=0))
        result = (
            stabilize_ref[:, columns] * values + product[:trace] - product[trace:] / coupling_ref[:, columns]
        )
        for k in range(4):
            start = (t * 4 + k) * group
            result_ref[:, start : start + group] = stacked(result[k * dofs : (k + 1) * dofs])
    shrink = 1.0 / scale_ref[:, :1]
    leaving = folded(dot(result_ref[...], leave_ref[...])) * shrink
    down = [leaving[:, (2 + i) * shared : (3 + i) * shared] for i in range(2)]
    down_ref[...] = leaving[:, 2 * shared :]
    if final:
        message = dict(zip(("slab", "section"), refs[9:11]))
        message["slab"][...] = down[0]
        message["section"][...] = down[1]
        return
    sent_ref = refs[9]
    sent = leaving[:, : 2 * shared] - (SHIFT * shrink) * own
    sent_ref[...] = sent
    up = [sent[:, i * shared : (i + 1) * shared] for i in range(2)]
    parts = {
        "gx later": jnp.where(odd, up[0], down[0]),
        "gx first": jnp.where(odd, down[0], up[0]),
        "yz up": up[1],
        "yz down": down[1],
    }
    for name, ref in zip(STARTS, refs[10:]):
        ref[...] = parts[name]


def between_kernel(first, final, earlier, *refs):
    refs = list(refs)
    result_ref, own_ref = refs[:2]
    refs = refs[2:]
    if not first:
        got, refs = refs[:4], refs[4:]
    if not final:
        down_ref = refs.pop(0)
    vectors, refs = refs[:earlier], refs[earlier:]
    select_ref, spread_ref, place_ref, scale_ref, odd_ref = refs[:5]
    refs = refs[5:]
    if first:
        vector = own_ref[...]
    else:
        back, _ = arrived(got, odd_ref[:1, :] != 0)
        vector = own_ref[...] + folded(dot(stacked(jnp.concatenate(back, axis=1)), place_ref[...]))
        refs.pop(0)[...] = vector
    gram_ref, part_ref = refs[:2]
    shrink = 1.0 / scale_ref[:, :1]
    part = folded(dot(result_ref[...], spread_ref[...])) * shrink - (SHIFT * shrink) * vector
    part_ref[...] = part
    if not final:
        refs[2][...] = folded(dot(stacked(jnp.concatenate([part, down_ref[...]], axis=1)), select_ref[...]))
    inner_products([ref[...] for ref in vectors] + [vector], vector, gram_ref, 0)
    gram_ref[earlier + 1 :, :] = jnp.zeros((8 - earlier - 1, 128), F32)


def last_kernel(*refs):
    own_ref, slab_ref, section_ref = refs[:3]
    vectors = refs[3 : 3 + ITERS]
    grams = refs[3 + ITERS : 3 + 2 * ITERS]
    place_ref, row_ref, sums_ref = refs[3 + 2 * ITERS :]
    received = jnp.concatenate([slab_ref[...], section_ref[...]], axis=1)
    vector = own_ref[...] + folded(dot(stacked(received), place_ref[...]))
    sums_ref[...] = jnp.zeros(sums_ref.shape, F32)
    for j in range(ITERS):
        start = j * (j + 1) // 2
        sums_ref[start : start + j + 1, :] = grams[j][: j + 1, :]
    inner_products([ref[...] for ref in vectors] + [vector], vector, sums_ref, ITERS * (ITERS + 1) // 2)
    totals = jnp.sum(sums_ref[...], axis=1, keepdims=True)
    count = sums_ref.shape[0]
    diagonal = lax.broadcasted_iota(jnp.int32, (count, 128), 0) == lax.broadcasted_iota(
        jnp.int32, (count, 128), 1
    )
    row = jnp.sum(jnp.where(diagonal, totals, 0.0), axis=0, keepdims=True)
    row_ref[...] = jnp.broadcast_to(row, row_ref.shape)


def least_squares(hessenberg, target):
    breadth = len(hessenberg)
    height = len(target)
    unit_columns = []
    triangle = {}
    shrink = {}
    for k in range(breadth):
        column = list(hessenberg[k])
        for i in range(k):
            triangle[i, k] = sum(unit_columns[i][r] * column[r] for r in range(height))
            column = [column[r] - triangle[i, k] * unit_columns[i][r] for r in range(height)]
        square = sum(c * c for c in column)
        shrink[k] = lax.rsqrt(square)
        unit_columns.append([c * shrink[k] for c in column])
    projected = [sum(v[r] * target[r] for r in range(height)) for v in unit_columns]
    outcome = [None] * breadth
    for k in reversed(range(breadth)):
        running = projected[k]
        for i in range(k + 1, breadth):
            running = running - triangle[k, i] * outcome[i]
        outcome[k] = running * shrink[k]
    return outcome


def coefficients(gram, scale):
    size = ITERS + 1
    zero = jnp.zeros_like(scale)

    def inner(a, b):
        total = zero
        for i in range(size):
            for j in range(size):
                if a[i] is not None and b[j] is not None:
                    total = total + a[i] * b[j] * gram[i][j]
        return total

    def plus(a, factor, b):
        out = []
        for x, y in zip(a, b):
            if y is None:
                out.append(x)
            else:
                out.append(factor * y if x is None else x + factor * y)
        return out

    square = gram[0][0] + EPSILON
    initial_norm = jnp.sqrt(square)
    krylov = [[lax.rsqrt(square)] + [None] * ITERS]
    columns = []
    for j in range(ITERS):
        shifted = [None] + [scale * c if c is not None else None for c in krylov[j][:-1]]
        fresh = plus(shifted, SHIFT, krylov[j])
        products = [inner(vector, fresh) for vector in krylov]
        for value, vector in zip(products, krylov):
            fresh = plus(fresh, -value, vector)
        square = jnp.maximum(inner(fresh, fresh), 0.0) + EPSILON
        columns.append(products + [jnp.sqrt(square)] + [zero] * (ITERS - 1 - j))
        shrink = lax.rsqrt(square)
        krylov.append([c * shrink if c is not None else None for c in fresh])
    combine = least_squares(columns, [initial_norm] + [zero] * ITERS)
    total = [None] * size
    for y, vector in zip(combine, krylov):
        total = plus(total, y, vector)
    return total[:ITERS]


def add_kernel(rows_ref, out_ref):
    total = jnp.sum(rows_ref[...], axis=0, keepdims=True)
    out_ref[...] = jnp.broadcast_to(total, out_ref.shape)


def solve_kernel(rows_ref, scale_ref, *refs):
    vectors = refs[:ITERS]
    out_ref = refs[ITERS]
    sums = jnp.sum(rows_ref[...], axis=0, keepdims=True)
    gram = [[None] * (ITERS + 1) for _ in range(ITERS + 1)]
    for p, (i, j) in enumerate(PAIRS):
        gram[i][j] = gram[j][i] = sums[:, p : p + 1]
    weights = coefficients(gram, scale_ref[:, :1])
    total = weights[0] * vectors[0][...]
    for weight, ref in zip(weights[1:], vectors[1:]):
        total = total + weight * ref[...]
    out_ref[...] = total


def passed_along(value, axis, steps):
    count = lax.axis_size(axis)
    pairs = [(source, (source + steps) % count) for source in range(count)]
    return lax.ppermute(value, axis, pairs)


def exchange(value, name):
    axis, kind = name.split()
    if kind in ("up", "down"):
        return passed_along(value, axis, 1 if kind == "up" else -1)
    count = lax.axis_size(axis)
    ahead = 1 if kind == "later" else 0
    pairs = [(i, (i + (1 if i % 2 == ahead else -1)) % count) for i in range(count)]
    return lax.ppermute(value, axis, pairs)


def every(row, axis):
    count = row.shape[0]
    return lax.all_to_all(row.reshape(count, 1, 128), axis, 0, 0).reshape(count, 128)


def shape(*dims, dtype=F32):
    return jax.ShapeDtypeStruct(dims, dtype)


def call(kernel, out_shape, *args, scratch=(), flops=0, name=None, in_hbm=()):
    spaces = [pltpu.HBM if i in in_hbm else pltpu.VMEM for i in range(len(args))]
    args = [
        pltpu.with_memory_space_constraint(arg, space) if space == pltpu.HBM else arg
        for arg, space in zip(args, spaces)
    ]
    return pl.pallas_call(
        kernel,
        out_shape=out_shape,
        in_specs=[pl.BlockSpec(memory_space=space) for space in spaces],
        out_specs=jax.tree.map(lambda _: pl.BlockSpec(memory_space=pltpu.VMEM), out_shape),
        scratch_shapes=list(scratch),
        cost_estimate=pl.CostEstimate(flops=flops, bytes_accessed=4 * 1024 * 1024, transcendentals=0),
        compiler_params=pltpu.CompilerParams(vmem_limit_bytes=VMEM_BYTES),
        name=name,
    )(*args)


def per_device(
    right_side, face_table, send_faces, stabilize, coupling, inverse, lifting, trace_block
):
    source = right_side[0, 0]
    table = face_table[0, 0]
    send_lists = send_faces[0, 0]
    penalty = stabilize[0]
    scaling = coupling[0]
    dofs, owned = source.shape
    elements = table.shape[1]
    shared = send_lists.shape[1]
    faces = owned + 2 * shared
    shapes, trace, _ = lifting.shape
    part = shape(dofs, shared)

    slab, section, send_lists = call(
        first_kernel,
        (part, part, shape(*send_lists.shape, dtype=jnp.int32)),
        source,
        send_lists,
        scratch=[pltpu.VMEM(source.shape, F32), pltpu.SemaphoreType.DMA((2,))],
        name="first",
        in_hbm=(0, 1),
    )
    ghosts = [passed_along(section, "yz", 1), passed_along(slab, "gx", 1)]
    select, spread, meet, leave, place = call(
        functools.partial(tables_kernel, shapes),
        (
            pltpu.VMEM((faces, 4 * elements), BF16),
            pltpu.VMEM((4 * elements, owned), BF16),
            pltpu.VMEM((4 * shared, 4 * elements), BF16),
            pltpu.VMEM((4 * elements, 4 * shared), BF16),
            shape(2 * shared, owned, dtype=BF16),
        ),
        table,
        send_lists,
        scratch=[pltpu.VMEM(table.shape, jnp.int32), pltpu.SemaphoreType.DMA((1,))],
        flops=10**9,
        name="tables",
        in_hbm=(0,),
    )
    weights, scale = call(
        weights_kernel,
        (shape(shapes, 2 * trace, 3 * trace, dtype=BF16), shape(1, 128)),
        inverse,
        jnp.swapaxes(lifting, 1, 2),
        trace_block,
        scratch=[pltpu.VMEM((8 * shapes, trace, 128), F32)],
        flops=10**9,
        name="weights",
    )
    odd = jnp.broadcast_to(
        jnp.stack([lax.axis_index("gx"), lax.axis_index("yz")])[:, None] % 2, (2, 128)
    ).astype(jnp.int32)
    known = call(gather_kernel, shape(dofs, 4 * elements), source, select, flops=10**9, name="gather")
    vectors = [source]
    grams = []
    own, got, sent = source, ghosts, [slab, section]
    both = shape(dofs, 2 * shared)
    for j in range(ITERS):
        first, final = j == 0, j == ITERS - 1
        outs = [shape(2 * dofs, 4 * elements, dtype=BF16), both]
        results = call(
            functools.partial(step_kernel, first, final),
            tuple(outs + ([part] * 2 if final else [both] + [part] * 4)),
            known,
            *got,
            *sent,
            meet,
            leave,
            weights,
            penalty,
            scaling,
            scale,
            odd,
            flops=10**9,
            name=f"step{j}",
        )
        result, down = results[:2]
        if final:
            after = [passed_along(results[2], "gx", -1), passed_along(results[3], "yz", -1)]
        else:
            sent = [results[2]]
            after = [exchange(value, name) for value, name in zip(results[3:], STARTS)]
        earlier = vectors[:j] if j else []
        outs = [shape(8, 128), shape(dofs, owned)]
        if not first:
            outs = [shape(dofs, owned)] + outs
        if not final:
            outs = outs + [shape(dofs, 4 * elements)]
        results = list(
            call(
                functools.partial(between_kernel, first, final, len(earlier)),
                tuple(outs),
                result,
                own,
                *([] if first else got),
                *([] if final else [down]),
                *earlier,
                select,
                spread,
                place,
                scale,
                odd,
                flops=10**9,
                name=f"between{j}",
            )
        )
        if not first:
            vectors.append(results.pop(0))
        grams.append(results.pop(0))
        own = results.pop(0)
        if not final:
            known = results.pop(0)
        got = after
    gx, yz = lax.axis_size("gx"), lax.axis_size("yz")
    rows = call(
        last_kernel,
        shape(yz, 128),
        own,
        *got,
        *vectors,
        *grams,
        place,
        scratch=[pltpu.VMEM((16, 128), F32)],
        name="last",
    )
    rows = call(add_kernel, shape(gx, 128), every(rows, "yz"), name="add")
    solution = call(solve_kernel, shape(dofs, owned), every(rows, "gx"), scale, *vectors, name="solve")
    return solution[None, None]


def solution(mesh):
    return jax.shard_map(
        per_device,
        mesh=mesh,
        in_specs=(
            P("gx", "yz", None, None),
            P("gx", "yz", None, None),
            P("gx", "yz", None, None),
            P("gx", "yz", None),
            P("gx", "yz", None),
            P(),
            P(),
            P(),
        ),
        out_specs=P("gx", "yz", None, None),
        check_vma=False,
    )
```

time: 100 us -> 99 us (0.990)
  waiting for transfers between devices: 4.96 us -> 0.08 us
  Pallas kernels: 16.8 us -> 21 us
  starting transfers between devices: 46.2 us -> 44.5 us
    ppermute x10, waiting for transfers between devices: 4.94 us -> 0.06 us  [passed_along(): return lax.ppermute(value, axis, pairs)]
    pallas_call x9 -> x15, Pallas kernels: 16.8 us -> 21 us  [call(): pl.pallas_call(kernel, out_shape=out_shape, in_specs=[pl.BlockSpec(memory...]
    ppermute x10, starting transfers between devices: 26.7 us -> 24.1 us  [passed_along(): return lax.ppermute(value, axis, pairs)]
  transfers between devices with their start and end apart: 16 -> 16, of which waited for: 8 -> 0; matrix products, arithmetic and copies ran while one was open for 0% -> 0% of each run, Pallas kernels for 4% -> 11%
where the time goes in v5:
time: 99 us; the launch traced here: 98.6 us
  starting transfers between devices  44.5 us (45%)
  blocking collectives  31.8 us (32%)
  Pallas kernels  21 us (21%)
    all_to_all x2, blocking collectives, every(): lax.all_to_all(row.reshape(count, 1, 128), axis, 0, 0).reshape(count, 128)  31.8 us
    ppermute x10, starting transfers between devices, passed_along(): return lax.ppermute(value, axis, pairs)  24.1 us
    pallas_call x15, Pallas kernels, call(): pl.pallas_call(kernel, out_shape=out_shape, in_specs=[pl.BlockSpec(memory...  21 us
    ppermute x6, starting transfers between devices, exchange(): return lax.ppermute(value, axis, pairs)  20.5 us
  transfers between devices with their start and end apart: 16, of which 0 were waited for; matrix products, arithmetic and copies ran while one was open for 0% of the time, Pallas kernels for 11%

profile of v5, /device:TPU:1, one launch (start us, length us, event | category | flops | bytes accessed | tf_op | source)
XLA Modules:
  0.0 98.6 jit_solution(2567300691163277762)
XLA Ops:
  0.0 0.0 copy-start
  0.0 1.2 %first.1 = (f32[80,128]{1,0:T(8,128)S(1)}, f32[80,128]{1,0:T(8,128)S(1)}, s32[2,128]{1,0:T(2,128)S(1)}) custom-call(f32[80,768]{1,0:T(8,128)} %bitcast.17, s32[2,128]{1,0:T(2,128)} %bitcast.38), custom_call_target="tpu_custom_call" | custom-call | bytes 4194304 | tf_op jit(solution)/shard_map/first/pallas_call | solution.py:400
  1.3 3.5 %collective-permute-start = (f32[80,128]{1,0:T(8,128)S(1)}, f32[80,128]{1,0:T(8,128)S(1)}, u32[]{:S(2)}, u32[]{:S(2)}) collective-permute-start(f32[80,128]{1,0:T(8,128)S(1)} %get-tuple-element.55.refs_4_), channel_id=1, source_target_pairs={{0,1},{1,2},{2,3},{3,4},{4,5},{5,6},{6,7},{7,8},{8,9},{9,10},{10,1... | collective-permute-start | bytes 122888 | tf_op jit(solution)/shard_map/ppermute | solution.py:372
  4.7 3.1 %collective-permute-start.1 = (f32[80,128]{1,0:T(8,128)S(1)}, f32[80,128]{1,0:T(8,128)S(1)}, u32[]{:S(2)}, u32[]{:S(2)}) collective-permute-start(f32[80,128]{1,0:T(8,128)S(1)} %get-tuple-element.56.refs_3_), channel_id=1, source_target_pairs={{0,16},{16,32},{32,48},{48,64},{64,80},{80,96},{96,112},{112,128},... | collective-permute-start | bytes 122888 | tf_op jit(solution)/shard_map/ppermute | solution.py:372
  7.9 2.4 %tables.1 = (bf16[1024,2048]{1,0:T(8,128)(2,1)S(1)}, bf16[2048,768]{1,0:T(8,128)(2,1)S(1)}, bf16[512,2048]{1,0:T(8,128)(2,1)S(1)}, bf16[2048,512]{1,0:T(8,128)(2,1)S(1)}, bf16[256,768]{1,0:T(8,128)(2,1)S(1)}) custom-call(s32[4,512]{1,0:T(4,128)} %bitcast.39, s32[2,128]{1,0:T(2,128)S(1)} %get-tuple-element.53.send_ref), custom_call_target="tpu_custom_call" | custom-call | flops 1000000000 | bytes 4194304 | tf_op jit(solution)/shard_map/tables/pallas_call | solution.py:400
  10.2 0.0 copy-start.3
  10.3 0.0 copy-start.4
  10.3 0.0 copy-start.5
  10.3 0.0 copy-done
  10.3 0.7 gather.1.refs_0_
  11.0 0.0 copy-start.1
  11.0 0.0 copy-start.2
  11.0 0.1 and_select_fusion
  11.1 0.4 copy-done.3
  11.4 0.2 copy-done.4
  11.6 0.1 copy-done.5
  11.7 1.6 %weights.1 = (bf16[2,640,960]{2,1,0:T(8,128)(2,1)S(1)}, f32[1,128]{1,0:T(1,128)S(1)}) custom-call(f32[2,192,192]{2,1,0:T(8,128)S(1)} %copy-done.5, f32[2,192,320]{2,1,0:T(8,128)S(1)} %bitcast.37, f32[2,320,320]{2,1,0:T(8,128)S(1)} %copy-done.3), custom_call_target="tpu_custom_call" | custom-call | flops 1000000000 | bytes 4194304 | tf_op jit(solution)/shard_map/weights/pallas_call | solution.py:400
  13.4 0.0 collective-permute-done.refs_1_
  13.4 0.0 collective-permute-done.1.refs_2_
  13.4 0.1 broadcast_in_dim.4.refs_11_.refs_7_.refs_12_.refs_13_
  13.5 0.0 copy-done.1
  13.5 0.0 copy-done.2
  13.5 1.5 %step0.1 = (bf16[160,2048]{1,0:T(8,128)(2,1)S(1)}, f32[80,256]{1,0:T(8,128)S(1)}, f32[80,256]{1,0:T(8,128)S(1)}, f32[80,128]{1,0:T(8,128)S(1)}, f32[80,128]{1,0:...) custom-call(f32[80,2048]{1,0:T(8,128)S(1)} %gather.1.refs_0_, f32[80,128]{1,0:T(8,128)S(1)} %collective-permute-done.refs_1_, ...), custom_call_target="tpu_custom_call" | custom-call | flops 1000000000 | bytes 4194304 | tf_op jit(solution)/shard_map/step0/pallas_call | solution.py:400
  15.0 6.1 %collective-permute-start.2 = (f32[80,128]{1,0:T(8,128)S(1)}, f32[80,128]{1,0:T(8,128)S(1)}, u32[]{:S(2)}, u32[]{:S(2)}) collective-permute-start(f32[80,128]{1,0:T(8,128)S(1)} %get-tuple-element.66), channel_id=1, source_target_pairs={{0,496},{16,32},{32,16},{48,64},{64,48},{80,96},{96,80},{112,128},... | collective-permute-start | bytes 122888 | tf_op jit(solution)/shard_map/ppermute | solution.py:382
  21.1 1.9 %collective-permute-start.3 = (f32[80,128]{1,0:T(8,128)S(1)}, f32[80,128]{1,0:T(8,128)S(1)}, u32[]{:S(2)}, u32[]{:S(2)}) collective-permute-start(f32[80,128]{1,0:T(8,128)S(1)} %get-tuple-element.67), channel_id=1, source_target_pairs={{0,16},{16,0},{32,48},{48,32},{64,80},{80,64},{96,112},{112,96},{1... | collective-permute-start | bytes 122888 | tf_op jit(solution)/shard_map/ppermute | solution.py:382
  23.0 0.3 collective-permute-start.4
  23.4 3.1 %collective-permute-start.5 = (f32[80,128]{1,0:T(8,128)S(1)}, f32[80,128]{1,0:T(8,128)S(1)}, u32[]{:S(2)}, u32[]{:S(2)}) collective-permute-start(f32[80,128]{1,0:T(8,128)S(1)} %get-tuple-element.69), channel_id=1, source_target_pairs={{0,15},{1,0},{2,1},{3,2},{4,3},{5,4},{6,5},{7,6},{8,7},{9,8},{10,9... | collective-permute-start | bytes 122888 | tf_op jit(solution)/shard_map/ppermute | solution.py:372
  26.5 1.7 %between0.1 = (f32[8,128]{1,0:T(8,128)S(1)}, f32[80,768]{1,0:T(8,128)S(1)}, f32[80,2048]{1,0:T(8,128)S(1)}) custom-call(bf16[160,2048]{1,0:T(8,128)(2,1)S(1)} %get-tuple-element.61.refs_0_, f32[80,768]{1,0:T(8,128)S(1)} %bitcast.19, f32[80,256]{1,0:T(8,128)S(1)} %get-tuple-element.62.refs_2_, ...), custom_call_target="tpu_custom_call" | custom-call | flops 1000000000 | bytes 4194304 | tf_op jit(solution)/shard_map/between0/pallas_call | solution.py:400
  28.2 0.0 collective-permute-done.2.refs_1_.refs_2_
  28.2 0.0 collective-permute-done.3.refs_2_.refs_3_
  28.2 0.0 collective-permute-done.4.refs_3_.refs_4_
  28.2 0.0 collective-permute-done.5.refs_4_.refs_5_
  28.3 1.7 %step1.1 = (bf16[160,2048]{1,0:T(8,128)(2,1)S(1)}, f32[80,256]{1,0:T(8,128)S(1)}, f32[80,256]{1,0:T(8,128)S(1)}, f32[80,128]{1,0:T(8,128)S(1)}, f32[80,128]{1,0:...) custom-call(f32[80,2048]{1,0:T(8,128)S(1)} %get-tuple-element.65.refs_0_, ...), custom_call_target="tpu_custom_call" | custom-call | flops 1000000000 | bytes 4194304 | tf_op jit(solution)/shard_map/step1/pallas_call | solution.py:400
  30.0 3.4 %collective-permute-start.6 = (f32[80,128]{1,0:T(8,128)S(1)}, f32[80,128]{1,0:T(8,128)S(1)}, u32[]{:S(2)}, u32[]{:S(2)}) collective-permute-start(f32[80,128]{1,0:T(8,128)S(1)} %get-tuple-element.75), channel_id=1, source_target_pairs={{0,496},{16,32},{32,16},{48,64},{64,48},{80,96},{96,80},{112,128},... | collective-permute-start | bytes 122888 | tf_op jit(solution)/shard_map/ppermute | solution.py:382
  33.4 2.2 %collective-permute-start.7 = (f32[80,128]{1,0:T(8,128)S(1)}, f32[80,128]{1,0:T(8,128)S(1)}, u32[]{:S(2)}, u32[]{:S(2)}) collective-permute-start(f32[80,128]{1,0:T(8,128)S(1)} %get-tuple-element.76), channel_id=1, source_target_pairs={{0,16},{16,0},{32,48},{48,32},{64,80},{80,64},{96,112},{112,96},{1... | collective-permute-start | bytes 122888 | tf_op jit(solution)/shard_map/ppermute | solution.py:382
  35.6 0.0 collective-permute-start.8
  35.6 3.7 %collective-permute-start.9 = (f32[80,128]{1,0:T(8,128)S(1)}, f32[80,128]{1,0:T(8,128)S(1)}, u32[]{:S(2)}, u32[]{:S(2)}) collective-permute-start(f32[80,128]{1,0:T(8,128)S(1)} %get-tuple-element.78), channel_id=1, source_target_pairs={{0,15},{1,0},{2,1},{3,2},{4,3},{5,4},{6,5},{7,6},{8,7},{9,8},{10,9... | collective-permute-start | bytes 122888 | tf_op jit(solution)/shard_map/ppermute | solution.py:372
  39.3 1.8 %between1.1 = (f32[80,768]{1,0:T(8,128)S(1)}, f32[8,128]{1,0:T(8,128)S(1)}, f32[80,768]{1,0:T(8,128)S(1)}, f32[80,2048]{1,0:T(8,128)S(1)}) custom-call(bf16[160,2048]{1,0:T(8,128)(2,1)S(1)} %get-tuple-element.71.refs_0_, f32[80,768]{1,0:T(8,128)S(1)} %get-tuple-element.72.refs_1_, f32[80,128]{1,0:T(8,128)S(1)} %collective-permute-done.2.refs_1_.refs_2_, ...), custom_call_target="tpu_custom_call" | custom-call | flops 1000000000 | bytes 4194304 | tf_op jit(solution)/shard_map/between1/pallas_call | solution.py:400
  41.1 0.0 collective-permute-done.6.refs_1_.refs_2_
  41.1 0.0 collective-permute-done.7.refs_2_.refs_3_
  41.1 0.0 collective-permute-done.8.refs_3_.refs_4_
  41.2 0.0 collective-permute-done.9.refs_4_.refs_5_
  41.2 1.7 %step2.1 = (bf16[160,2048]{1,0:T(8,128)(2,1)S(1)}, f32[80,256]{1,0:T(8,128)S(1)}, f32[80,256]{1,0:T(8,128)S(1)}, f32[80,128]{1,0:T(8,128)S(1)}, f32[80,128]{1,0:...) custom-call(f32[80,2048]{1,0:T(8,128)S(1)} %get-tuple-element.74.refs_0_, ...), custom_call_target="tpu_custom_call" | custom-call | flops 1000000000 | bytes 4194304 | tf_op jit(solution)/shard_map/step2/pallas_call | solution.py:400
  42.9 4.8 %collective-permute-start.10 = (f32[80,128]{1,0:T(8,128)S(1)}, f32[80,128]{1,0:T(8,128)S(1)}, u32[]{:S(2)}, u32[]{:S(2)}) collective-permute-start(f32[80,128]{1,0:T(8,128)S(1)} %get-tuple-element.85), channel_id=1, source_target_pairs={{0,496},{16,32},{32,16},{48,64},{64,48},{80,96},{96,80},{112,128},... | collective-permute-start | bytes 122888 | tf_op jit(solution)/shard_map/ppermute | solution.py:382
  47.7 2.1 %collective-permute-start.11 = (f32[80,128]{1,0:T(8,128)S(1)}, f32[80,128]{1,0:T(8,128)S(1)}, u32[]{:S(2)}, u32[]{:S(2)}) collective-permute-start(f32[80,128]{1,0:T(8,128)S(1)} %get-tuple-element.86), channel_id=1, source_target_pairs={{0,16},{16,0},{32,48},{48,32},{64,80},{80,64},{96,112},{112,96},{1... | collective-permute-start | bytes 122888 | tf_op jit(solution)/shard_map/ppermute | solution.py:382
  49.8 0.0 collective-permute-start.12
  49.9 3.2 %collective-permute-start.13 = (f32[80,128]{1,0:T(8,128)S(1)}, f32[80,128]{1,0:T(8,128)S(1)}, u32[]{:S(2)}, u32[]{:S(2)}) collective-permute-start(f32[80,128]{1,0:T(8,128)S(1)} %get-tuple-element.88), channel_id=1, source_target_pairs={{0,15},{1,0},{2,1},{3,2},{4,3},{5,4},{6,5},{7,6},{8,7},{9,8},{10,9... | collective-permute-start | bytes 122888 | tf_op jit(solution)/shard_map/ppermute | solution.py:372
  53.1 1.8 %between2.1 = (f32[80,768]{1,0:T(8,128)S(1)}, f32[8,128]{1,0:T(8,128)S(1)}, f32[80,768]{1,0:T(8,128)S(1)}, f32[80,2048]{1,0:T(8,128)S(1)}) custom-call(bf16[160,2048]{1,0:T(8,128)(2,1)S(1)} %get-tuple-element.80.refs_0_, f32[80,768]{1,0:T(8,128)S(1)} %get-tuple-element.81.refs_1_, f32[80,128]{1,0:T(8,128)S(1)} %collective-permute-done.6.refs_1_.refs_2_, ...), custom_call_target="tpu_custom_call" | custom-call | flops 1000000000 | bytes 4194304 | tf_op jit(solution)/shard_map/between2/pallas_call | solution.py:400
  54.9 0.0 collective-permute-done.10.refs_1_.refs_2_
  54.9 0.0 collective-permute-done.11.refs_2_.refs_3_
  54.9 0.0 collective-permute-done.12.refs_3_.refs_4_
  54.9 0.0 collective-permute-done.13.refs_4_.refs_5_
  55.0 2.3 %step3.1 = (bf16[160,2048]{1,0:T(8,128)(2,1)S(1)}, f32[80,256]{1,0:T(8,128)}, f32[80,128]{1,0:T(8,128)S(1)}, f32[80,128]{1,0:T(8,128)S(1)}) custom-call(f32[80,2048]{1,0:T(8,128)S(1)} %get-tuple-element.84.refs_0_, f32[80,128]{1,0:T(8,128)S(1)} %collective-permute-done.10.refs_1_.refs_2_, f32[80,128]{1,0:T(8,128)S(1)} %collective-permute-done.11.refs_2_.refs_3_, ...), custom_call_target="tpu_custom_call" | custom-call | flops 1000000000 | bytes 4194304 | tf_op jit(solution)/shard_map/step3/pallas_call | solution.py:400
  57.2 3.9 %collective-permute-start.14 = (f32[80,128]{1,0:T(8,128)S(1)}, f32[80,128]{1,0:T(8,128)S(1)}, u32[]{:S(2)}, u32[]{:S(2)}) collective-permute-start(f32[80,128]{1,0:T(8,128)S(1)} %get-tuple-element.94), channel_id=1, source_target_pairs={{0,496},{16,0},{32,16},{48,32},{64,48},{80,64},{96,80},{112,96},{1... | collective-permute-start | bytes 122888 | tf_op jit(solution)/shard_map/ppermute | solution.py:372
  61.1 3.2 %collective-permute-start.15 = (f32[80,128]{1,0:T(8,128)S(1)}, f32[80,128]{1,0:T(8,128)S(1)}, u32[]{:S(2)}, u32[]{:S(2)}) collective-permute-start(f32[80,128]{1,0:T(8,128)S(1)} %get-tuple-element.95), channel_id=1, source_target_pairs={{0,15},{1,0},{2,1},{3,2},{4,3},{5,4},{6,5},{7,6},{8,7},{9,8},{10,9... | collective-permute-start | bytes 122888 | tf_op jit(solution)/shard_map/ppermute | solution.py:372
  64.3 0.9 between3.1
  65.2 0.0 collective-permute-done.14.refs_1_
  65.2 0.0 collective-permute-done.15.refs_2_
  65.2 0.4 last.1
  65.6 15.9 %all_to_all.10 = f32[16,1,128]{2,1,0:T(1,128)S(1)} all-to-all(f32[16,1,128]{2,1,0:T(1,128)S(1)} %bitcast.27), channel_id=1, replica_groups=mesh['gx'=32,'yz'=16] {'yz'}, dimensions={0} | all-to-all | bytes 16384 | tf_op jit(solution)/shard_map/all_to_all | solution.py:387
  81.6 15.9 %all_to_all.11 = f32[32,1,128]{2,1,0:T(1,128)S(1)} all-to-all(f32[32,1,128]{2,1,0:T(1,128)S(1)} %bitcast.26), channel_id=1, replica_groups=mesh['gx'=32,'yz'=16] {'gx'}, dimensions={0} | all-to-all | bytes 32768 | tf_op jit(solution)/shard_map/all_to_all | solution.py:387
  97.4 1.1 %solve.1 = f32[80,768]{1,0:T(8,128)} custom-call(f32[32,128]{1,0:T(8,128)S(1)} %bitcast.25, f32[1,128]{1,0:T(1,128)S(1)} %get-tuple-element.60.refs_10_.refs_6_.refs_11_.refs_12_.scale_ref, f32[80,768]{1,0:T(8,128)S(1)} %bitcast.24, f32[80,768]{1,0:T(8,128)S(1)} %get-tuple-element.83.refs_8_.refs_7_.refs_4_.refs_1_, ...), custom_call_target="tpu_custom_call" | custom-call | bytes 4194304 | tf_op jit(solution)/shard_map/solve/pallas_call | solution.py:400
  (1 shorter events, 0.0 us)
Async XLA Ops:
  0.0 10.3 %copy-start = (f32[1,1,80,768]{3,2,1,0:T(8,128)S(1)}, f32[1,1,80,768]{3,2,1,0:T(8,128)}, u32[]{:S(2)}) copy-start(f32[1,1,80,768]{3,2,1,0:T(8,128)} %param.8) | copy-start | bytes 737284
  1.3 12.1 %collective-permute-start = (f32[80,128]{1,0:T(8,128)S(1)}, f32[80,128]{1,0:T(8,128)S(1)}, u32[]{:S(2)}, u32[]{:S(2)}) collective-permute-start(f32[80,128]{1,0:T(8,128)S(1)} %get-tuple-element.55.refs_4_), channel_id=1, source_target_pairs={{0,1},{1,2},{2,3},{3,4},{4,5},{5,6},{6,7},{7,8},{8,9},{9,10},{10,1... | collective-permute-start | bytes 122888 | tf_op jit(solution)/shard_map/ppermute | solution.py:372
  4.7 8.7 %collective-permute-start.1 = (f32[80,128]{1,0:T(8,128)S(1)}, f32[80,128]{1,0:T(8,128)S(1)}, u32[]{:S(2)}, u32[]{:S(2)}) collective-permute-start(f32[80,128]{1,0:T(8,128)S(1)} %get-tuple-element.56.refs_3_), channel_id=1, source_target_pairs={{0,16},{16,32},{32,48},{48,64},{64,80},{80,96},{96,112},{112,128},... | collective-permute-start | bytes 122888 | tf_op jit(solution)/shard_map/ppermute | solution.py:372
  10.2 1.2 %copy-start.3 = (f32[2,320,320]{2,1,0:T(8,128)S(1)}, f32[2,320,320]{2,1,0:T(8,128)}, u32[]{:S(2)}) copy-start(f32[2,320,320]{2,1,0:T(8,128)} %block_ref.1) | copy-start | bytes 2457604
  10.3 1.4 %copy-start.4 = (f32[2,320,192]{1,2,0:T(8,128)S(1)}, f32[2,320,192]{1,2,0:T(8,128)}, u32[]{:S(2)}) copy-start(f32[2,320,192]{1,2,0:T(8,128)} %param.14) | copy-start | bytes 1474564
  10.3 1.4 %copy-start.5 = (f32[2,192,192]{2,1,0:T(8,128)S(1)}, f32[2,192,192]{2,1,0:T(8,128)}, u32[]{:S(2)}) copy-start(f32[2,192,192]{2,1,0:T(8,128)} %inverse_ref.1) | copy-start | bytes 884740
  11.0 2.5 %copy-start.1 = (f32[1,1,512]{2,1,0:T(1,128)S(1)}, f32[1,1,512]{2,1,0:T(1,128)}, u32[]{:S(2)}) copy-start(f32[1,1,512]{2,1,0:T(1,128)} %param.11) | copy-start | bytes 6148
  11.0 2.5 %copy-start.2 = (f32[1,1,512]{2,1,0:T(1,128)S(1)}, f32[1,1,512]{2,1,0:T(1,128)}, u32[]{:S(2)}) copy-start(f32[1,1,512]{2,1,0:T(1,128)} %param.12) | copy-start | bytes 6148
  15.0 13.2 %collective-permute-start.2 = (f32[80,128]{1,0:T(8,128)S(1)}, f32[80,128]{1,0:T(8,128)S(1)}, u32[]{:S(2)}, u32[]{:S(2)}) collective-permute-start(f32[80,128]{1,0:T(8,128)S(1)} %get-tuple-element.66), channel_id=1, source_target_pairs={{0,496},{16,32},{32,16},{48,64},{64,48},{80,96},{96,80},{112,128},... | collective-permute-start | bytes 122888 | tf_op jit(solution)/shard_map/ppermute | solution.py:382
  21.1 7.1 %collective-permute-start.3 = (f32[80,128]{1,0:T(8,128)S(1)}, f32[80,128]{1,0:T(8,128)S(1)}, u32[]{:S(2)}, u32[]{:S(2)}) collective-permute-start(f32[80,128]{1,0:T(8,128)S(1)} %get-tuple-element.67), channel_id=1, source_target_pairs={{0,16},{16,0},{32,48},{48,32},{64,80},{80,64},{96,112},{112,96},{1... | collective-permute-start | bytes 122888 | tf_op jit(solution)/shard_map/ppermute | solution.py:382
  23.0 5.2 %collective-permute-start.4 = (f32[80,128]{1,0:T(8,128)S(1)}, f32[80,128]{1,0:T(8,128)S(1)}, u32[]{:S(2)}, u32[]{:S(2)}) collective-permute-start(f32[80,128]{1,0:T(8,128)S(1)} %get-tuple-element.68), channel_id=1, source_target_pairs={{0,1},{1,2},{2,3},{3,4},{4,5},{5,6},{6,7},{7,8},{8,9},{9,10},{10,1... | collective-permute-start | bytes 122888 | tf_op jit(solution)/shard_map/ppermute | solution.py:372
  23.4 4.9 %collective-permute-start.5 = (f32[80,128]{1,0:T(8,128)S(1)}, f32[80,128]{1,0:T(8,128)S(1)}, u32[]{:S(2)}, u32[]{:S(2)}) collective-permute-start(f32[80,128]{1,0:T(8,128)S(1)} %get-tuple-element.69), channel_id=1, source_target_pairs={{0,15},{1,0},{2,1},{3,2},{4,3},{5,4},{6,5},{7,6},{8,7},{9,8},{10,9... | collective-permute-start | bytes 122888 | tf_op jit(solution)/shard_map/ppermute | solution.py:372
  30.0 11.1 %collective-permute-start.6 = (f32[80,128]{1,0:T(8,128)S(1)}, f32[80,128]{1,0:T(8,128)S(1)}, u32[]{:S(2)}, u32[]{:S(2)}) collective-permute-start(f32[80,128]{1,0:T(8,128)S(1)} %get-tuple-element.75), channel_id=1, source_target_pairs={{0,496},{16,32},{32,16},{48,64},{64,48},{80,96},{96,80},{112,128},... | collective-permute-start | bytes 122888 | tf_op jit(solution)/shard_map/ppermute | solution.py:382
  33.4 7.7 %collective-permute-start.7 = (f32[80,128]{1,0:T(8,128)S(1)}, f32[80,128]{1,0:T(8,128)S(1)}, u32[]{:S(2)}, u32[]{:S(2)}) collective-permute-start(f32[80,128]{1,0:T(8,128)S(1)} %get-tuple-element.76), channel_id=1, source_target_pairs={{0,16},{16,0},{32,48},{48,32},{64,80},{80,64},{96,112},{112,96},{1... | collective-permute-start | bytes 122888 | tf_op jit(solution)/shard_map/ppermute | solution.py:382
  35.6 5.6 %collective-permute-start.8 = (f32[80,128]{1,0:T(8,128)S(1)}, f32[80,128]{1,0:T(8,128)S(1)}, u32[]{:S(2)}, u32[]{:S(2)}) collective-permute-start(f32[80,128]{1,0:T(8,128)S(1)} %get-tuple-element.77), channel_id=1, source_target_pairs={{0,1},{1,2},{2,3},{3,4},{4,5},{5,6},{6,7},{7,8},{8,9},{9,10},{10,1... | collective-permute-start | bytes 122888 | tf_op jit(solution)/shard_map/ppermute | solution.py:372
  35.6 5.5 %collective-permute-start.9 = (f32[80,128]{1,0:T(8,128)S(1)}, f32[80,128]{1,0:T(8,128)S(1)}, u32[]{:S(2)}, u32[]{:S(2)}) collective-permute-start(f32[80,128]{1,0:T(8,128)S(1)} %get-tuple-element.78), channel_id=1, source_target_pairs={{0,15},{1,0},{2,1},{3,2},{4,3},{5,4},{6,5},{7,6},{8,7},{9,8},{10,9... | collective-permute-start | bytes 122888 | tf_op jit(solution)/shard_map/ppermute | solution.py:372
  42.9 12.0 %collective-permute-start.10 = (f32[80,128]{1,0:T(8,128)S(1)}, f32[80,128]{1,0:T(8,128)S(1)}, u32[]{:S(2)}, u32[]{:S(2)}) collective-permute-start(f32[80,128]{1,0:T(8,128)S(1)} %get-tuple-element.85), channel_id=1, source_target_pairs={{0,496},{16,32},{32,16},{48,64},{64,48},{80,96},{96,80},{112,128},... | collective-permute-start | bytes 122888 | tf_op jit(solution)/shard_map/ppermute | solution.py:382
  47.7 7.2 %collective-permute-start.11 = (f32[80,128]{1,0:T(8,128)S(1)}, f32[80,128]{1,0:T(8,128)S(1)}, u32[]{:S(2)}, u32[]{:S(2)}) collective-permute-start(f32[80,128]{1,0:T(8,128)S(1)} %get-tuple-element.86), channel_id=1, source_target_pairs={{0,16},{16,0},{32,48},{48,32},{64,80},{80,64},{96,112},{112,96},{1... | collective-permute-start | bytes 122888 | tf_op jit(solution)/shard_map/ppermute | solution.py:382
  49.8 5.1 %collective-permute-start.12 = (f32[80,128]{1,0:T(8,128)S(1)}, f32[80,128]{1,0:T(8,128)S(1)}, u32[]{:S(2)}, u32[]{:S(2)}) collective-permute-start(f32[80,128]{1,0:T(8,128)S(1)} %get-tuple-element.87), channel_id=1, source_target_pairs={{0,1},{1,2},{2,3},{3,4},{4,5},{5,6},{6,7},{7,8},{8,9},{9,10},{10,1... | collective-permute-start | bytes 122888 | tf_op jit(solution)/shard_map/ppermute | solution.py:372
  49.9 5.1 %collective-permute-start.13 = (f32[80,128]{1,0:T(8,128)S(1)}, f32[80,128]{1,0:T(8,128)S(1)}, u32[]{:S(2)}, u32[]{:S(2)}) collective-permute-start(f32[80,128]{1,0:T(8,128)S(1)} %get-tuple-element.88), channel_id=1, source_target_pairs={{0,15},{1,0},{2,1},{3,2},{4,3},{5,4},{6,5},{7,6},{8,7},{9,8},{10,9... | collective-permute-start | bytes 122888 | tf_op jit(solution)/shard_map/ppermute | solution.py:372
  57.2 8.0 %collective-permute-start.14 = (f32[80,128]{1,0:T(8,128)S(1)}, f32[80,128]{1,0:T(8,128)S(1)}, u32[]{:S(2)}, u32[]{:S(2)}) collective-permute-start(f32[80,128]{1,0:T(8,128)S(1)} %get-tuple-element.94), channel_id=1, source_target_pairs={{0,496},{16,0},{32,16},{48,32},{64,48},{80,64},{96,80},{112,96},{1... | collective-permute-start | bytes 122888 | tf_op jit(solution)/shard_map/ppermute | solution.py:372
  61.1 4.1 %collective-permute-start.15 = (f32[80,128]{1,0:T(8,128)S(1)}, f32[80,128]{1,0:T(8,128)S(1)}, u32[]{:S(2)}, u32[]{:S(2)}) collective-permute-start(f32[80,128]{1,0:T(8,128)S(1)} %get-tuple-element.95), channel_id=1, source_target_pairs={{0,15},{1,0},{2,1},{3,2},{4,3},{5,4},{6,5},{7,6},{8,7},{9,8},{10,9... | collective-permute-start | bytes 122888 | tf_op jit(solution)/shard_map/ppermute | solution.py:372

commit v6 on v5

--- a/solution.py
+++ b/solution.py
@@ -179,10 +179,10 @@
     got = [refs.pop(0) for _ in range(2 if first else 4)]
     sent_before = [refs.pop(0) for _ in range(2 if first else 1)]
     meet_ref, leave_ref, weight_ref, stabilize_ref, coupling_ref, scale_ref, odd_ref = refs[:7]
-    result_ref, down_ref = refs[7:9]
+    result_ref = refs[7]
     odd = odd_ref[:1, :] != 0
     dofs = known_ref.shape[0]
-    shared = down_ref.shape[1] // 2
+    shared = leave_ref.shape[1] // 4
     shapes = weight_ref.shape[0]
     group = stabilize_ref.shape[1] // shapes
     trace = 4 * dofs
@@ -211,15 +211,15 @@
             start = (t * 4 + k) * group
             result_ref[:, start : start + group] = stacked(result[k * dofs : (k + 1) * dofs])
     shrink = 1.0 / scale_ref[:, :1]
+    if final:
+        leaving = folded(dot(result_ref[...], leave_ref[:, 2 * shared :])) * shrink
+        for i in range(2):
+            refs[8 + i][...] = leaving[:, i * shared : (i + 1) * shared]
+        return
+    down_ref, sent_ref = refs[8:10]
     leaving = folded(dot(result_ref[...], leave_ref[...])) * shrink
     down = [leaving[:, (2 + i) * shared : (3 + i) * shared] for i in range(2)]
     down_ref[...] = leaving[:, 2 * shared :]
-    if final:
-        message = dict(zip(("slab", "section"), refs[9:11]))
-        message["slab"][...] = down[0]
-        message["section"][...] = down[1]
-        return
-    sent_ref = refs[9]
     sent = leaving[:, : 2 * shared] - (SHIFT * shrink) * own
     sent_ref[...] = sent
     up = [sent[:, i * shared : (i + 1) * shared] for i in range(2)]
@@ -281,6 +281,13 @@
     row_ref[...] = jnp.broadcast_to(row, row_ref.shape)
 
 
+def added(terms):
+    terms = list(terms)
+    while len(terms) > 1:
+        terms = [a + b for a, b in zip(terms[::2], terms[1::2])] + terms[len(terms) // 2 * 2 :]
+    return terms[0]
+
+
 def least_squares(hessenberg, target):
     breadth = len(hessenberg)
     height = len(target)
@@ -290,12 +297,12 @@
     for k in range(breadth):
         column = list(hessenberg[k])
         for i in range(k):
-            triangle[i, k] = sum(unit_columns[i][r] * column[r] for r in range(height))
+            triangle[i, k] = added(unit_columns[i][r] * column[r] for r in range(height))
             column = [column[r] - triangle[i, k] * unit_columns[i][r] for r in range(height)]
-        square = sum(c * c for c in column)
+        square = added(c * c for c in column)
         shrink[k] = lax.rsqrt(square)
         unit_columns.append([c * shrink[k] for c in column])
-    projected = [sum(v[r] * target[r] for r in range(height)) for v in unit_columns]
+    projected = [added(v[r] * target[r] for r in range(height)) for v in unit_columns]
     outcome = [None] * breadth
     for k in reversed(range(breadth)):
         running = projected[k]
@@ -310,12 +317,8 @@
     zero = jnp.zeros_like(scale)
 
     def inner(a, b):
-        total = zero
-        for i in range(size):
-            for j in range(size):
-                if a[i] is not None and b[j] is not None:
-                    total = total + a[i] * b[j] * gram[i][j]
-        return total
+        rows = [(x, row) for x, row in zip(a, gram) if x is not None]
+        return added(x * added(y * g for y, g in zip(b, row) if y is not None) for x, row in rows)
 
     def plus(a, factor, b):
         out = []
@@ -470,10 +473,10 @@
     both = shape(dofs, 2 * shared)
     for j in range(ITERS):
         first, final = j == 0, j == ITERS - 1
-        outs = [shape(2 * dofs, 4 * elements, dtype=BF16), both]
+        outs = [shape(2 * dofs, 4 * elements, dtype=BF16)]
         results = call(
             functools.partial(step_kernel, first, final),
-            tuple(outs + ([part] * 2 if final else [both] + [part] * 4)),
+            tuple(outs + ([part] * 2 if final else [both] * 2 + [part] * 4)),
             known,
             *got,
             *sent,
@@ -487,11 +490,11 @@
             flops=10**9,
             name=f"step{j}",
         )
-        result, down = results[:2]
+        result = results[0]
         if final:
-            after = [passed_along(results[2], "gx", -1), passed_along(results[3], "yz", -1)]
+            after = [passed_along(results[1], "gx", -1), passed_along(results[2], "yz", -1)]
         else:
-            sent = [results[2]]
+            down, sent = results[1], [results[2]]
             after = [exchange(value, name) for value, name in zip(results[3:], STARTS)]
         earlier = vectors[:j] if j else []
         outs = [shape(8, 128), shape(dofs, owned)]

time: 99 us -> 98.4 us (level)
  no operation moved by 1% of the time
where the time goes in v6:
time: 98.4 us; the launch traced here: 97.9 us
  starting transfers between devices  44.5 us (45%)
  blocking collectives  31.8 us (32%)
  Pallas kernels  20.3 us (21%)
    all_to_all x2, blocking collectives, every(): lax.all_to_all(row.reshape(count, 1, 128), axis, 0, 0).reshape(count, 128)  31.8 us
    ppermute x10, starting transfers between devices, passed_along(): return lax.ppermute(value, axis, pairs)  24.1 us
    ppermute x6, starting transfers between devices, exchange(): return lax.ppermute(value, axis, pairs)  20.5 us
    pallas_call x15, Pallas kernels, call(): pl.pallas_call(kernel, out_shape=out_shape, in_specs=[pl.BlockSpec(memory...  20.3 us
  transfers between devices with their start and end apart: 16, of which 0 were waited for; matrix products, arithmetic and copies ran while one was open for 0% of the time, Pallas kernels for 11%

profile of v6, /device:TPU:1, one launch (start us, length us, event | category | flops | bytes accessed | tf_op | source)
XLA Modules:
  0.0 97.9 jit_solution(18111502010995859196)
XLA Ops:
  0.0 0.0 copy-start
  0.0 1.2 %first.1 = (f32[80,128]{1,0:T(8,128)S(1)}, f32[80,128]{1,0:T(8,128)S(1)}, s32[2,128]{1,0:T(2,128)S(1)}) custom-call(f32[80,768]{1,0:T(8,128)} %bitcast.17, s32[2,128]{1,0:T(2,128)} %bitcast.38), custom_call_target="tpu_custom_call" | custom-call | bytes 4194304 | tf_op jit(solution)/shard_map/first/pallas_call | solution.py:403
  1.3 3.5 %collective-permute-start = (f32[80,128]{1,0:T(8,128)S(1)}, f32[80,128]{1,0:T(8,128)S(1)}, u32[]{:S(2)}, u32[]{:S(2)}) collective-permute-start(f32[80,128]{1,0:T(8,128)S(1)} %get-tuple-element.55.refs_4_), channel_id=1, source_target_pairs={{0,1},{1,2},{2,3},{3,4},{4,5},{5,6},{6,7},{7,8},{8,9},{9,10},{10,1... | collective-permute-start | bytes 122888 | tf_op jit(solution)/shard_map/ppermute | solution.py:375
  4.7 3.1 %collective-permute-start.1 = (f32[80,128]{1,0:T(8,128)S(1)}, f32[80,128]{1,0:T(8,128)S(1)}, u32[]{:S(2)}, u32[]{:S(2)}) collective-permute-start(f32[80,128]{1,0:T(8,128)S(1)} %get-tuple-element.56.refs_3_), channel_id=1, source_target_pairs={{0,16},{16,32},{32,48},{48,64},{64,80},{80,96},{96,112},{112,128},... | collective-permute-start | bytes 122888 | tf_op jit(solution)/shard_map/ppermute | solution.py:375
  7.9 2.4 %tables.1 = (bf16[1024,2048]{1,0:T(8,128)(2,1)S(1)}, bf16[2048,768]{1,0:T(8,128)(2,1)S(1)}, bf16[512,2048]{1,0:T(8,128)(2,1)S(1)}, bf16[2048,512]{1,0:T(8,128)(2,1)S(1)}, bf16[256,768]{1,0:T(8,128)(2,1)S(1)}) custom-call(s32[4,512]{1,0:T(4,128)} %bitcast.39, s32[2,128]{1,0:T(2,128)S(1)} %get-tuple-element.53.send_ref), custom_call_target="tpu_custom_call" | custom-call | flops 1000000000 | bytes 4194304 | tf_op jit(solution)/shard_map/tables/pallas_call | solution.py:403
  10.2 0.0 copy-start.3
  10.3 0.0 copy-start.4
  10.3 0.0 copy-start.5
  10.3 0.0 copy-done
  10.3 0.7 gather.1.refs_0_
  11.0 0.0 copy-start.1
  11.0 0.0 copy-start.2
  11.0 0.1 and_select_fusion
  11.1 0.4 copy-done.3
  11.4 0.2 copy-done.4
  11.6 0.1 copy-done.5
  11.7 1.6 %weights.1 = (bf16[2,640,960]{2,1,0:T(8,128)(2,1)S(1)}, f32[1,128]{1,0:T(1,128)S(1)}) custom-call(f32[2,192,192]{2,1,0:T(8,128)S(1)} %copy-done.5, f32[2,192,320]{2,1,0:T(8,128)S(1)} %bitcast.37, f32[2,320,320]{2,1,0:T(8,128)S(1)} %copy-done.3), custom_call_target="tpu_custom_call" | custom-call | flops 1000000000 | bytes 4194304 | tf_op jit(solution)/shard_map/weights/pallas_call | solution.py:403
  13.4 0.0 collective-permute-done.refs_1_
  13.4 0.0 collective-permute-done.1.refs_2_
  13.4 0.1 broadcast_in_dim.4.refs_11_.refs_7_.refs_12_.refs_13_
  13.5 0.0 copy-done.1
  13.5 0.0 copy-done.2
  13.5 1.5 %step0.1 = (bf16[160,2048]{1,0:T(8,128)(2,1)S(1)}, f32[80,256]{1,0:T(8,128)S(1)}, f32[80,256]{1,0:T(8,128)S(1)}, f32[80,128]{1,0:T(8,128)S(1)}, f32[80,128]{1,0:...) custom-call(f32[80,2048]{1,0:T(8,128)S(1)} %gather.1.refs_0_, f32[80,128]{1,0:T(8,128)S(1)} %collective-permute-done.refs_1_, ...), custom_call_target="tpu_custom_call" | custom-call | flops 1000000000 | bytes 4194304 | tf_op jit(solution)/shard_map/step0/pallas_call | solution.py:403
  15.0 6.1 %collective-permute-start.2 = (f32[80,128]{1,0:T(8,128)S(1)}, f32[80,128]{1,0:T(8,128)S(1)}, u32[]{:S(2)}, u32[]{:S(2)}) collective-permute-start(f32[80,128]{1,0:T(8,128)S(1)} %get-tuple-element.66), channel_id=1, source_target_pairs={{0,496},{16,32},{32,16},{48,64},{64,48},{80,96},{96,80},{112,128},... | collective-permute-start | bytes 122888 | tf_op jit(solution)/shard_map/ppermute | solution.py:385
  21.1 1.9 %collective-permute-start.3 = (f32[80,128]{1,0:T(8,128)S(1)}, f32[80,128]{1,0:T(8,128)S(1)}, u32[]{:S(2)}, u32[]{:S(2)}) collective-permute-start(f32[80,128]{1,0:T(8,128)S(1)} %get-tuple-element.67), channel_id=1, source_target_pairs={{0,16},{16,0},{32,48},{48,32},{64,80},{80,64},{96,112},{112,96},{1... | collective-permute-start | bytes 122888 | tf_op jit(solution)/shard_map/ppermute | solution.py:385
  23.0 0.3 collective-permute-start.4
  23.4 3.1 %collective-permute-start.5 = (f32[80,128]{1,0:T(8,128)S(1)}, f32[80,128]{1,0:T(8,128)S(1)}, u32[]{:S(2)}, u32[]{:S(2)}) collective-permute-start(f32[80,128]{1,0:T(8,128)S(1)} %get-tuple-element.69), channel_id=1, source_target_pairs={{0,15},{1,0},{2,1},{3,2},{4,3},{5,4},{6,5},{7,6},{8,7},{9,8},{10,9... | collective-permute-start | bytes 122888 | tf_op jit(solution)/shard_map/ppermute | solution.py:375
  26.5 1.7 %between0.1 = (f32[8,128]{1,0:T(8,128)S(1)}, f32[80,768]{1,0:T(8,128)S(1)}, f32[80,2048]{1,0:T(8,128)S(1)}) custom-call(bf16[160,2048]{1,0:T(8,128)(2,1)S(1)} %get-tuple-element.61.refs_0_, f32[80,768]{1,0:T(8,128)S(1)} %bitcast.19, f32[80,256]{1,0:T(8,128)S(1)} %get-tuple-element.62.refs_2_, ...), custom_call_target="tpu_custom_call" | custom-call | flops 1000000000 | bytes 4194304 | tf_op jit(solution)/shard_map/between0/pallas_call | solution.py:403
  28.2 0.0 collective-permute-done.2.refs_1_.refs_2_
  28.2 0.0 collective-permute-done.3.refs_2_.refs_3_
  28.2 0.0 collective-permute-done.4.refs_3_.refs_4_
  28.2 0.0 collective-permute-done.5.refs_4_.refs_5_
  28.3 1.7 %step1.1 = (bf16[160,2048]{1,0:T(8,128)(2,1)S(1)}, f32[80,256]{1,0:T(8,128)S(1)}, f32[80,256]{1,0:T(8,128)S(1)}, f32[80,128]{1,0:T(8,128)S(1)}, f32[80,128]{1,0:...) custom-call(f32[80,2048]{1,0:T(8,128)S(1)} %get-tuple-element.65.refs_0_, ...), custom_call_target="tpu_custom_call" | custom-call | flops 1000000000 | bytes 4194304 | tf_op jit(solution)/shard_map/step1/pallas_call | solution.py:403
  30.0 3.4 %collective-permute-start.6 = (f32[80,128]{1,0:T(8,128)S(1)}, f32[80,128]{1,0:T(8,128)S(1)}, u32[]{:S(2)}, u32[]{:S(2)}) collective-permute-start(f32[80,128]{1,0:T(8,128)S(1)} %get-tuple-element.75), channel_id=1, source_target_pairs={{0,496},{16,32},{32,16},{48,64},{64,48},{80,96},{96,80},{112,128},... | collective-permute-start | bytes 122888 | tf_op jit(solution)/shard_map/ppermute | solution.py:385
  33.4 2.2 %collective-permute-start.7 = (f32[80,128]{1,0:T(8,128)S(1)}, f32[80,128]{1,0:T(8,128)S(1)}, u32[]{:S(2)}, u32[]{:S(2)}) collective-permute-start(f32[80,128]{1,0:T(8,128)S(1)} %get-tuple-element.76), channel_id=1, source_target_pairs={{0,16},{16,0},{32,48},{48,32},{64,80},{80,64},{96,112},{112,96},{1... | collective-permute-start | bytes 122888 | tf_op jit(solution)/shard_map/ppermute | solution.py:385
  35.6 0.0 collective-permute-start.8
  35.6 3.7 %collective-permute-start.9 = (f32[80,128]{1,0:T(8,128)S(1)}, f32[80,128]{1,0:T(8,128)S(1)}, u32[]{:S(2)}, u32[]{:S(2)}) collective-permute-start(f32[80,128]{1,0:T(8,128)S(1)} %get-tuple-element.78), channel_id=1, source_target_pairs={{0,15},{1,0},{2,1},{3,2},{4,3},{5,4},{6,5},{7,6},{8,7},{9,8},{10,9... | collective-permute-start | bytes 122888 | tf_op jit(solution)/shard_map/ppermute | solution.py:375
  39.3 1.8 %between1.1 = (f32[80,768]{1,0:T(8,128)S(1)}, f32[8,128]{1,0:T(8,128)S(1)}, f32[80,768]{1,0:T(8,128)S(1)}, f32[80,2048]{1,0:T(8,128)S(1)}) custom-call(bf16[160,2048]{1,0:T(8,128)(2,1)S(1)} %get-tuple-element.71.refs_0_, f32[80,768]{1,0:T(8,128)S(1)} %get-tuple-element.72.refs_1_, f32[80,128]{1,0:T(8,128)S(1)} %collective-permute-done.2.refs_1_.refs_2_, ...), custom_call_target="tpu_custom_call" | custom-call | flops 1000000000 | bytes 4194304 | tf_op jit(solution)/shard_map/between1/pallas_call | solution.py:403
  41.1 0.0 collective-permute-done.6.refs_1_.refs_2_
  41.1 0.0 collective-permute-done.7.refs_2_.refs_3_
  41.1 0.0 collective-permute-done.8.refs_3_.refs_4_
  41.2 0.0 collective-permute-done.9.refs_4_.refs_5_
  41.2 1.7 %step2.1 = (bf16[160,2048]{1,0:T(8,128)(2,1)S(1)}, f32[80,256]{1,0:T(8,128)S(1)}, f32[80,256]{1,0:T(8,128)S(1)}, f32[80,128]{1,0:T(8,128)S(1)}, f32[80,128]{1,0:...) custom-call(f32[80,2048]{1,0:T(8,128)S(1)} %get-tuple-element.74.refs_0_, ...), custom_call_target="tpu_custom_call" | custom-call | flops 1000000000 | bytes 4194304 | tf_op jit(solution)/shard_map/step2/pallas_call | solution.py:403
  42.9 4.8 %collective-permute-start.10 = (f32[80,128]{1,0:T(8,128)S(1)}, f32[80,128]{1,0:T(8,128)S(1)}, u32[]{:S(2)}, u32[]{:S(2)}) collective-permute-start(f32[80,128]{1,0:T(8,128)S(1)} %get-tuple-element.85), channel_id=1, source_target_pairs={{0,496},{16,32},{32,16},{48,64},{64,48},{80,96},{96,80},{112,128},... | collective-permute-start | bytes 122888 | tf_op jit(solution)/shard_map/ppermute | solution.py:385
  47.7 2.1 %collective-permute-start.11 = (f32[80,128]{1,0:T(8,128)S(1)}, f32[80,128]{1,0:T(8,128)S(1)}, u32[]{:S(2)}, u32[]{:S(2)}) collective-permute-start(f32[80,128]{1,0:T(8,128)S(1)} %get-tuple-element.86), channel_id=1, source_target_pairs={{0,16},{16,0},{32,48},{48,32},{64,80},{80,64},{96,112},{112,96},{1... | collective-permute-start | bytes 122888 | tf_op jit(solution)/shard_map/ppermute | solution.py:385
  49.8 0.0 collective-permute-start.12
  49.9 3.2 %collective-permute-start.13 = (f32[80,128]{1,0:T(8,128)S(1)}, f32[80,128]{1,0:T(8,128)S(1)}, u32[]{:S(2)}, u32[]{:S(2)}) collective-permute-start(f32[80,128]{1,0:T(8,128)S(1)} %get-tuple-element.88), channel_id=1, source_target_pairs={{0,15},{1,0},{2,1},{3,2},{4,3},{5,4},{6,5},{7,6},{8,7},{9,8},{10,9... | collective-permute-start | bytes 122888 | tf_op jit(solution)/shard_map/ppermute | solution.py:375
  53.1 1.8 %between2.1 = (f32[80,768]{1,0:T(8,128)S(1)}, f32[8,128]{1,0:T(8,128)S(1)}, f32[80,768]{1,0:T(8,128)S(1)}, f32[80,2048]{1,0:T(8,128)S(1)}) custom-call(bf16[160,2048]{1,0:T(8,128)(2,1)S(1)} %get-tuple-element.80.refs_0_, f32[80,768]{1,0:T(8,128)S(1)} %get-tuple-element.81.refs_1_, f32[80,128]{1,0:T(8,128)S(1)} %collective-permute-done.6.refs_1_.refs_2_, ...), custom_call_target="tpu_custom_call" | custom-call | flops 1000000000 | bytes 4194304 | tf_op jit(solution)/shard_map/between2/pallas_call | solution.py:403
  54.9 0.0 collective-permute-done.10.refs_1_.refs_2_
  54.9 0.0 collective-permute-done.11.refs_2_.refs_3_
  54.9 0.0 collective-permute-done.12.refs_3_.refs_4_
  54.9 0.0 collective-permute-done.13.refs_4_.refs_5_
  55.0 1.6 %step3.1 = (bf16[160,2048]{1,0:T(8,128)(2,1)S(1)}, f32[80,128]{1,0:T(8,128)S(1)}, f32[80,128]{1,0:T(8,128)S(1)}) custom-call(f32[80,2048]{1,0:T(8,128)S(1)} %get-tuple-element.84.refs_0_, f32[80,128]{1,0:T(8,128)S(1)} %collective-permute-done.10.refs_1_.refs_2_, f32[80,128]{1,0:T(8,128)S(1)} %collective-permute-done.11.refs_2_.refs_3_, ...), custom_call_target="tpu_custom_call" | custom-call | flops 1000000000 | bytes 4194304 | tf_op jit(solution)/shard_map/step3/pallas_call | solution.py:403
  56.6 3.9 %collective-permute-start.14 = (f32[80,128]{1,0:T(8,128)S(1)}, f32[80,128]{1,0:T(8,128)S(1)}, u32[]{:S(2)}, u32[]{:S(2)}) collective-permute-start(f32[80,128]{1,0:T(8,128)S(1)} %get-tuple-element.94), channel_id=1, source_target_pairs={{0,496},{16,0},{32,16},{48,32},{64,48},{80,64},{96,80},{112,96},{1... | collective-permute-start | bytes 122888 | tf_op jit(solution)/shard_map/ppermute | solution.py:375
  60.5 3.2 %collective-permute-start.15 = (f32[80,128]{1,0:T(8,128)S(1)}, f32[80,128]{1,0:T(8,128)S(1)}, u32[]{:S(2)}, u32[]{:S(2)}) collective-permute-start(f32[80,128]{1,0:T(8,128)S(1)} %get-tuple-element.95), channel_id=1, source_target_pairs={{0,15},{1,0},{2,1},{3,2},{4,3},{5,4},{6,5},{7,6},{8,7},{9,8},{10,9... | collective-permute-start | bytes 122888 | tf_op jit(solution)/shard_map/ppermute | solution.py:375
  63.7 0.9 between3.1
  64.6 0.0 collective-permute-done.14.refs_1_
  64.6 0.0 collective-permute-done.15.refs_2_
  64.6 0.4 last.1
  65.0 15.9 %all_to_all.10 = f32[16,1,128]{2,1,0:T(1,128)S(1)} all-to-all(f32[16,1,128]{2,1,0:T(1,128)S(1)} %bitcast.27), channel_id=1, replica_groups=mesh['gx'=32,'yz'=16] {'yz'}, dimensions={0} | all-to-all | bytes 16384 | tf_op jit(solution)/shard_map/all_to_all | solution.py:390
  81.0 15.9 %all_to_all.11 = f32[32,1,128]{2,1,0:T(1,128)S(1)} all-to-all(f32[32,1,128]{2,1,0:T(1,128)S(1)} %bitcast.26), channel_id=1, replica_groups=mesh['gx'=32,'yz'=16] {'gx'}, dimensions={0} | all-to-all | bytes 32768 | tf_op jit(solution)/shard_map/all_to_all | solution.py:390
  96.8 1.1 %solve.1 = f32[80,768]{1,0:T(8,128)} custom-call(f32[32,128]{1,0:T(8,128)S(1)} %bitcast.25, f32[1,128]{1,0:T(1,128)S(1)} %get-tuple-element.60.refs_10_.refs_6_.refs_11_.refs_12_.scale_ref, f32[80,768]{1,0:T(8,128)S(1)} %bitcast.24, f32[80,768]{1,0:T(8,128)S(1)} %get-tuple-element.83.refs_8_.refs_7_.refs_4_.refs_1_, ...), custom_call_target="tpu_custom_call" | custom-call | bytes 4194304 | tf_op jit(solution)/shard_map/solve/pallas_call | solution.py:403
  (1 shorter events, 0.0 us)
Async XLA Ops:
  0.0 10.3 %copy-start = (f32[1,1,80,768]{3,2,1,0:T(8,128)S(1)}, f32[1,1,80,768]{3,2,1,0:T(8,128)}, u32[]{:S(2)}) copy-start(f32[1,1,80,768]{3,2,1,0:T(8,128)} %param.8) | copy-start | bytes 737284
  1.3 12.1 %collective-permute-start = (f32[80,128]{1,0:T(8,128)S(1)}, f32[80,128]{1,0:T(8,128)S(1)}, u32[]{:S(2)}, u32[]{:S(2)}) collective-permute-start(f32[80,128]{1,0:T(8,128)S(1)} %get-tuple-element.55.refs_4_), channel_id=1, source_target_pairs={{0,1},{1,2},{2,3},{3,4},{4,5},{5,6},{6,7},{7,8},{8,9},{9,10},{10,1... | collective-permute-start | bytes 122888 | tf_op jit(solution)/shard_map/ppermute | solution.py:375
  4.7 8.7 %collective-permute-start.1 = (f32[80,128]{1,0:T(8,128)S(1)}, f32[80,128]{1,0:T(8,128)S(1)}, u32[]{:S(2)}, u32[]{:S(2)}) collective-permute-start(f32[80,128]{1,0:T(8,128)S(1)} %get-tuple-element.56.refs_3_), channel_id=1, source_target_pairs={{0,16},{16,32},{32,48},{48,64},{64,80},{80,96},{96,112},{112,128},... | collective-permute-start | bytes 122888 | tf_op jit(solution)/shard_map/ppermute | solution.py:375
  10.2 1.2 %copy-start.3 = (f32[2,320,320]{2,1,0:T(8,128)S(1)}, f32[2,320,320]{2,1,0:T(8,128)}, u32[]{:S(2)}) copy-start(f32[2,320,320]{2,1,0:T(8,128)} %block_ref.1) | copy-start | bytes 2457604
  10.3 1.4 %copy-start.4 = (f32[2,320,192]{1,2,0:T(8,128)S(1)}, f32[2,320,192]{1,2,0:T(8,128)}, u32[]{:S(2)}) copy-start(f32[2,320,192]{1,2,0:T(8,128)} %param.14) | copy-start | bytes 1474564
  10.3 1.4 %copy-start.5 = (f32[2,192,192]{2,1,0:T(8,128)S(1)}, f32[2,192,192]{2,1,0:T(8,128)}, u32[]{:S(2)}) copy-start(f32[2,192,192]{2,1,0:T(8,128)} %inverse_ref.1) | copy-start | bytes 884740
  11.0 2.5 %copy-start.1 = (f32[1,1,512]{2,1,0:T(1,128)S(1)}, f32[1,1,512]{2,1,0:T(1,128)}, u32[]{:S(2)}) copy-start(f32[1,1,512]{2,1,0:T(1,128)} %param.11) | copy-start | bytes 6148
  11.0 2.5 %copy-start.2 = (f32[1,1,512]{2,1,0:T(1,128)S(1)}, f32[1,1,512]{2,1,0:T(1,128)}, u32[]{:S(2)}) copy-start(f32[1,1,512]{2,1,0:T(1,128)} %param.12) | copy-start | bytes 6148
  15.0 13.2 %collective-permute-start.2 = (f32[80,128]{1,0:T(8,128)S(1)}, f32[80,128]{1,0:T(8,128)S(1)}, u32[]{:S(2)}, u32[]{:S(2)}) collective-permute-start(f32[80,128]{1,0:T(8,128)S(1)} %get-tuple-element.66), channel_id=1, source_target_pairs={{0,496},{16,32},{32,16},{48,64},{64,48},{80,96},{96,80},{112,128},... | collective-permute-start | bytes 122888 | tf_op jit(solution)/shard_map/ppermute | solution.py:385
  21.1 7.1 %collective-permute-start.3 = (f32[80,128]{1,0:T(8,128)S(1)}, f32[80,128]{1,0:T(8,128)S(1)}, u32[]{:S(2)}, u32[]{:S(2)}) collective-permute-start(f32[80,128]{1,0:T(8,128)S(1)} %get-tuple-element.67), channel_id=1, source_target_pairs={{0,16},{16,0},{32,48},{48,32},{64,80},{80,64},{96,112},{112,96},{1... | collective-permute-start | bytes 122888 | tf_op jit(solution)/shard_map/ppermute | solution.py:385
  23.0 5.2 %collective-permute-start.4 = (f32[80,128]{1,0:T(8,128)S(1)}, f32[80,128]{1,0:T(8,128)S(1)}, u32[]{:S(2)}, u32[]{:S(2)}) collective-permute-start(f32[80,128]{1,0:T(8,128)S(1)} %get-tuple-element.68), channel_id=1, source_target_pairs={{0,1},{1,2},{2,3},{3,4},{4,5},{5,6},{6,7},{7,8},{8,9},{9,10},{10,1... | collective-permute-start | bytes 122888 | tf_op jit(solution)/shard_map/ppermute | solution.py:375
  23.4 4.9 %collective-permute-start.5 = (f32[80,128]{1,0:T(8,128)S(1)}, f32[80,128]{1,0:T(8,128)S(1)}, u32[]{:S(2)}, u32[]{:S(2)}) collective-permute-start(f32[80,128]{1,0:T(8,128)S(1)} %get-tuple-element.69), channel_id=1, source_target_pairs={{0,15},{1,0},{2,1},{3,2},{4,3},{5,4},{6,5},{7,6},{8,7},{9,8},{10,9... | collective-permute-start | bytes 122888 | tf_op jit(solution)/shard_map/ppermute | solution.py:375
  30.0 11.1 %collective-permute-start.6 = (f32[80,128]{1,0:T(8,128)S(1)}, f32[80,128]{1,0:T(8,128)S(1)}, u32[]{:S(2)}, u32[]{:S(2)}) collective-permute-start(f32[80,128]{1,0:T(8,128)S(1)} %get-tuple-element.75), channel_id=1, source_target_pairs={{0,496},{16,32},{32,16},{48,64},{64,48},{80,96},{96,80},{112,128},... | collective-permute-start | bytes 122888 | tf_op jit(solution)/shard_map/ppermute | solution.py:385
  33.4 7.7 %collective-permute-start.7 = (f32[80,128]{1,0:T(8,128)S(1)}, f32[80,128]{1,0:T(8,128)S(1)}, u32[]{:S(2)}, u32[]{:S(2)}) collective-permute-start(f32[80,128]{1,0:T(8,128)S(1)} %get-tuple-element.76), channel_id=1, source_target_pairs={{0,16},{16,0},{32,48},{48,32},{64,80},{80,64},{96,112},{112,96},{1... | collective-permute-start | bytes 122888 | tf_op jit(solution)/shard_map/ppermute | solution.py:385
  35.6 5.6 %collective-permute-start.8 = (f32[80,128]{1,0:T(8,128)S(1)}, f32[80,128]{1,0:T(8,128)S(1)}, u32[]{:S(2)}, u32[]{:S(2)}) collective-permute-start(f32[80,128]{1,0:T(8,128)S(1)} %get-tuple-element.77), channel_id=1, source_target_pairs={{0,1},{1,2},{2,3},{3,4},{4,5},{5,6},{6,7},{7,8},{8,9},{9,10},{10,1... | collective-permute-start | bytes 122888 | tf_op jit(solution)/shard_map/ppermute | solution.py:375
  35.6 5.5 %collective-permute-start.9 = (f32[80,128]{1,0:T(8,128)S(1)}, f32[80,128]{1,0:T(8,128)S(1)}, u32[]{:S(2)}, u32[]{:S(2)}) collective-permute-start(f32[80,128]{1,0:T(8,128)S(1)} %get-tuple-element.78), channel_id=1, source_target_pairs={{0,15},{1,0},{2,1},{3,2},{4,3},{5,4},{6,5},{7,6},{8,7},{9,8},{10,9... | collective-permute-start | bytes 122888 | tf_op jit(solution)/shard_map/ppermute | solution.py:375
  42.9 12.0 %collective-permute-start.10 = (f32[80,128]{1,0:T(8,128)S(1)}, f32[80,128]{1,0:T(8,128)S(1)}, u32[]{:S(2)}, u32[]{:S(2)}) collective-permute-start(f32[80,128]{1,0:T(8,128)S(1)} %get-tuple-element.85), channel_id=1, source_target_pairs={{0,496},{16,32},{32,16},{48,64},{64,48},{80,96},{96,80},{112,128},... | collective-permute-start | bytes 122888 | tf_op jit(solution)/shard_map/ppermute | solution.py:385
  47.7 7.2 %collective-permute-start.11 = (f32[80,128]{1,0:T(8,128)S(1)}, f32[80,128]{1,0:T(8,128)S(1)}, u32[]{:S(2)}, u32[]{:S(2)}) collective-permute-start(f32[80,128]{1,0:T(8,128)S(1)} %get-tuple-element.86), channel_id=1, source_target_pairs={{0,16},{16,0},{32,48},{48,32},{64,80},{80,64},{96,112},{112,96},{1... | collective-permute-start | bytes 122888 | tf_op jit(solution)/shard_map/ppermute | solution.py:385
  49.8 5.1 %collective-permute-start.12 = (f32[80,128]{1,0:T(8,128)S(1)}, f32[80,128]{1,0:T(8,128)S(1)}, u32[]{:S(2)}, u32[]{:S(2)}) collective-permute-start(f32[80,128]{1,0:T(8,128)S(1)} %get-tuple-element.87), channel_id=1, source_target_pairs={{0,1},{1,2},{2,3},{3,4},{4,5},{5,6},{6,7},{7,8},{8,9},{9,10},{10,1... | collective-permute-start | bytes 122888 | tf_op jit(solution)/shard_map/ppermute | solution.py:375
  49.9 5.1 %collective-permute-start.13 = (f32[80,128]{1,0:T(8,128)S(1)}, f32[80,128]{1,0:T(8,128)S(1)}, u32[]{:S(2)}, u32[]{:S(2)}) collective-permute-start(f32[80,128]{1,0:T(8,128)S(1)} %get-tuple-element.88), channel_id=1, source_target_pairs={{0,15},{1,0},{2,1},{3,2},{4,3},{5,4},{6,5},{7,6},{8,7},{9,8},{10,9... | collective-permute-start | bytes 122888 | tf_op jit(solution)/shard_map/ppermute | solution.py:375
  56.6 8.0 %collective-permute-start.14 = (f32[80,128]{1,0:T(8,128)S(1)}, f32[80,128]{1,0:T(8,128)S(1)}, u32[]{:S(2)}, u32[]{:S(2)}) collective-permute-start(f32[80,128]{1,0:T(8,128)S(1)} %get-tuple-element.94), channel_id=1, source_target_pairs={{0,496},{16,0},{32,16},{48,32},{64,48},{80,64},{96,80},{112,96},{1... | collective-permute-start | bytes 122888 | tf_op jit(solution)/shard_map/ppermute | solution.py:375
  60.5 4.1 %collective-permute-start.15 = (f32[80,128]{1,0:T(8,128)S(1)}, f32[80,128]{1,0:T(8,128)S(1)}, u32[]{:S(2)}, u32[]{:S(2)}) collective-permute-start(f32[80,128]{1,0:T(8,128)S(1)} %get-tuple-element.95), channel_id=1, source_target_pairs={{0,15},{1,0},{2,1},{3,2},{4,3},{5,4},{6,5},{7,6},{8,7},{9,8},{10,9... | collective-permute-start | bytes 122888 | tf_op jit(solution)/shard_map/ppermute | solution.py:375

commit v7 on v6

--- a/solution.py
+++ b/solution.py
@@ -94,9 +94,12 @@
 
 
 def tables_kernel(
-    shapes, table_hbm, send_ref, select_ref, spread_ref, meet_ref, leave_ref, place_ref, table_ref, semaphores
+    shapes, table_hbm, inverse_hbm, lifting_hbm, block_hbm, send_ref,
+    select_ref, spread_ref, meet_ref, leave_ref, place_ref, inverse_ref, lifting_ref, block_ref, table_ref, semaphores,
 ):
-    (have_table,) = fetched((table_hbm,), (table_ref,), semaphores)
+    have_table, *have_weights = fetched(
+        (table_hbm, block_hbm, lifting_hbm, inverse_hbm), (table_ref, block_ref, lifting_ref, inverse_ref), semaphores
+    )
     faces = select_ref.shape[0]
     elements = table_ref.shape[1]
     sends = columns(send_ref)
@@ -130,6 +133,8 @@
                 ).astype(BF16)
             meet_ref[2 * shared :, start : start + group] = select_ref[owned:, start : start + group]
             leave_ref[start : start + group, :] = meet_ref[:, start : start + group].T
+    for have in have_weights:
+        have()
 
 
 def weights_kernel(inverse_ref, lifting_ref, block_ref, weight_ref, scale_ref, rows_ref):
@@ -212,9 +217,9 @@
             result_ref[:, start : start + group] = stacked(result[k * dofs : (k + 1) * dofs])
     shrink = 1.0 / scale_ref[:, :1]
     if final:
-        leaving = folded(dot(result_ref[...], leave_ref[:, 2 * shared :])) * shrink
-        for i in range(2):
-            refs[8 + i][...] = leaving[:, i * shared : (i + 1) * shared]
+        leaving = folded(dot(result_ref[...], leave_ref[:, shared : 3 * shared])) * shrink
+        refs[8][...] = leaving[:, shared:]
+        refs[9][...] = leaving[:, :shared] - (SHIFT * shrink) * own[:, shared:]
         return
     down_ref, sent_ref = refs[8:10]
     leaving = folded(dot(result_ref[...], leave_ref[...])) * shrink
@@ -244,6 +249,8 @@
     vectors, refs = refs[:earlier], refs[earlier:]
     select_ref, spread_ref, place_ref, scale_ref, odd_ref = refs[:5]
     refs = refs[5:]
+    if final:
+        leave_ref = refs.pop(0)
     if first:
         vector = own_ref[...]
     else:
@@ -254,24 +261,37 @@
     shrink = 1.0 / scale_ref[:, :1]
     part = folded(dot(result_ref[...], spread_ref[...])) * shrink - (SHIFT * shrink) * vector
     part_ref[...] = part
-    if not final:
+    if final:
+        ghost = leave_ref[:, 3 * leave_ref.shape[1] // 4 :]
+        refs[2][...] = folded(dot(result_ref[...], ghost)) * shrink
+    else:
         refs[2][...] = folded(dot(stacked(jnp.concatenate([part, down_ref[...]], axis=1)), select_ref[...]))
     inner_products([ref[...] for ref in vectors] + [vector], vector, gram_ref, 0)
     gram_ref[earlier + 1 :, :] = jnp.zeros((8 - earlier - 1, 128), F32)
 
 
 def last_kernel(*refs):
-    own_ref, slab_ref, section_ref = refs[:3]
-    vectors = refs[3 : 3 + ITERS]
-    grams = refs[3 + ITERS : 3 + 2 * ITERS]
-    place_ref, row_ref, sums_ref = refs[3 + 2 * ITERS :]
-    received = jnp.concatenate([slab_ref[...], section_ref[...]], axis=1)
-    vector = own_ref[...] + folded(dot(stacked(received), place_ref[...]))
+    refs = list(refs)
+    own_ref, slab_ref, section_ref, ghost_ref = [refs.pop(0) for _ in range(4)]
+    vectors = [refs.pop(0) for _ in range(ITERS)]
+    grams = [refs.pop(0) for _ in range(ITERS)]
+    ghosts = [refs.pop(0)[...]]
+    for _ in range(1, ITERS):
+        arrived_ref, sums_ref = refs.pop(0), refs.pop(0)
+        shared = arrived_ref.shape[1]
+        ghosts.append(arrived_ref[...] + sums_ref[:, shared:])
+    place_ref, row_ref, sums_ref = refs
+    vector = own_ref[...] + folded(dot(stacked(slab_ref[...]), place_ref[:shared, :]))
+    sent_along_yz = jnp.sum(place_ref[shared:, :].astype(F32), axis=0, keepdims=True)
+    vector = jnp.where(sent_along_yz > 0.5, 0.0, vector)
+    ghost = ghost_ref[...] + section_ref[...]
     sums_ref[...] = jnp.zeros(sums_ref.shape, F32)
     for j in range(ITERS):
         start = j * (j + 1) // 2
         sums_ref[start : start + j + 1, :] = grams[j][: j + 1, :]
-    inner_products([ref[...] for ref in vectors] + [vector], vector, sums_ref, ITERS * (ITERS + 1) // 2)
+    start = ITERS * (ITERS + 1) // 2
+    for i, (whole, part) in enumerate(zip([ref[...] for ref in vectors] + [vector], ghosts + [ghost])):
+        sums_ref[start + i : start + i + 1, :] = lane_sums(whole * vector) + lane_sums(part * ghost)
     totals = jnp.sum(sums_ref[...], axis=1, keepdims=True)
     count = sums_ref.shape[0]
     diagonal = lax.broadcasted_iota(jnp.int32, (count, 128), 0) == lax.broadcasted_iota(
@@ -437,7 +457,8 @@
         in_hbm=(0, 1),
     )
     ghosts = [passed_along(section, "yz", 1), passed_along(slab, "gx", 1)]
-    select, spread, meet, leave, place = call(
+    turned = jnp.swapaxes(lifting, 1, 2)
+    select, spread, meet, leave, place, inverse, turned, trace_block = call(
         functools.partial(tables_kernel, shapes),
         (
             pltpu.VMEM((faces, 4 * elements), BF16),
@@ -445,19 +466,25 @@
             pltpu.VMEM((4 * shared, 4 * elements), BF16),
             pltpu.VMEM((4 * elements, 4 * shared), BF16),
             shape(2 * shared, owned, dtype=BF16),
+            shape(*inverse.shape),
+            shape(*turned.shape),
+            shape(*trace_block.shape),
         ),
         table,
+        inverse,
+        turned,
+        trace_block,
         send_lists,
-        scratch=[pltpu.VMEM(table.shape, jnp.int32), pltpu.SemaphoreType.DMA((1,))],
+        scratch=[pltpu.VMEM(table.shape, jnp.int32), pltpu.SemaphoreType.DMA((4,))],
         flops=10**9,
         name="tables",
-        in_hbm=(0,),
+        in_hbm=(0, 1, 2, 3),
     )
     weights, scale = call(
         weights_kernel,
         (shape(shapes, 2 * trace, 3 * trace, dtype=BF16), shape(1, 128)),
         inverse,
-        jnp.swapaxes(lifting, 1, 2),
+        turned,
         trace_block,
         scratch=[pltpu.VMEM((8 * shapes, trace, 128), F32)],
         flops=10**9,
@@ -470,6 +497,8 @@
     vectors = [source]
     grams = []
     own, got, sent = source, ghosts, [slab, section]
+    along_yz = []
+    ghost_sums = None
     both = shape(dofs, 2 * shared)
     for j in range(ITERS):
         first, final = j == 0, j == ITERS - 1
@@ -492,7 +521,7 @@
         )
         result = results[0]
         if final:
-            after = [passed_along(results[1], "gx", -1), passed_along(results[2], "yz", -1)]
+            after = [passed_along(results[1], "gx", -1), passed_along(results[2], "yz", 1)]
         else:
             down, sent = results[1], [results[2]]
             after = [exchange(value, name) for value, name in zip(results[3:], STARTS)]
@@ -500,8 +529,7 @@
         outs = [shape(8, 128), shape(dofs, owned)]
         if not first:
             outs = [shape(dofs, owned)] + outs
-        if not final:
-            outs = outs + [shape(dofs, 4 * elements)]
+        outs = outs + [part if final else shape(dofs, 4 * elements)]
         results = list(
             call(
                 functools.partial(between_kernel, first, final, len(earlier)),
@@ -516,6 +544,7 @@
                 place,
                 scale,
                 odd,
+                *([leave] if final else []),
                 flops=10**9,
                 name=f"between{j}",
             )
@@ -524,8 +553,9 @@
             vectors.append(results.pop(0))
         grams.append(results.pop(0))
         own = results.pop(0)
-        if not final:
-            known = results.pop(0)
+        known = results.pop(0)
+        along_yz += [got[0]] if first else [got[STARTS.index("yz up")], ghost_sums]
+        ghost_sums = down
         got = after
     gx, yz = lax.axis_size("gx"), lax.axis_size("yz")
     rows = call(
@@ -533,8 +563,10 @@
         shape(yz, 128),
         own,
         *got,
+        known,
         *vectors,
         *grams,
+        *along_yz,
         place,
         scratch=[pltpu.VMEM((16, 128), F32)],
         name="last",

time: 98.4 us -> 97.8 us (level)
  starting transfers between devices: 44.5 us -> 40.6 us
  waiting for transfers between devices: 0.08 us -> 3.68 us
    ppermute x10, starting transfers between devices: 24.1 us -> 20.4 us  [passed_along(): return lax.ppermute(value, axis, pairs)]
    ppermute x10, waiting for transfers between devices: 0.06 us -> 3.66 us  [passed_along(): return lax.ppermute(value, axis, pairs)]
  transfers between devices with their start and end apart: 16 -> 16, of which waited for: 0 -> 3; matrix products, arithmetic and copies ran while one was open for 0% -> 0% of each run, Pallas kernels for 11% -> 11%
where the time goes in v7:
time: 97.8 us; the launch traced here: 97.4 us
  starting transfers between devices  40.6 us (42%)
  blocking collectives  32.2 us (33%)
  Pallas kernels  20.4 us (21%)
  waiting for transfers between devices  3.68 us (4%)
    all_to_all x2, blocking collectives, every(): lax.all_to_all(row.reshape(count, 1, 128), axis, 0, 0).reshape(count, 128)  32.2 us
    pallas_call x15, Pallas kernels, call(): pl.pallas_call(kernel, out_shape=out_shape, in_specs=[pl.BlockSpec(memory...  20.4 us
    ppermute x10, starting transfers between devices, passed_along(): return lax.ppermute(value, axis, pairs)  20.4 us
    ppermute x6, starting transfers between devices, exchange(): return lax.ppermute(value, axis, pairs)  20.2 us
    ppermute x10, waiting for transfers between devices, passed_along(): return lax.ppermute(value, axis, pairs)  3.66 us
  transfers between devices with their start and end apart: 16, of which 3 were waited for; matrix products, arithmetic and copies ran while one was open for 0% of the time, Pallas kernels for 11%

profile of v7, /device:TPU:1, one launch (start us, length us, event | category | flops | bytes accessed | tf_op | source)
XLA Modules:
  0.0 97.4 jit_solution(3698152631169877812)
XLA Ops:
  0.0 0.0 copy-start
  0.0 1.2 %first.1 = (f32[80,128]{1,0:T(8,128)S(1)}, f32[80,128]{1,0:T(8,128)S(1)}, s32[2,128]{1,0:T(2,128)S(1)}) custom-call(f32[80,768]{1,0:T(8,128)} %bitcast.17, s32[2,128]{1,0:T(2,128)} %bitcast.37), custom_call_target="tpu_custom_call" | custom-call | bytes 4194304 | tf_op jit(solution)/shard_map/first/pallas_call | solution.py:423
  1.3 3.5 %collective-permute-start = (f32[80,128]{1,0:T(8,128)S(1)}, f32[80,128]{1,0:T(8,128)S(1)}, u32[]{:S(2)}, u32[]{:S(2)}) collective-permute-start(f32[80,128]{1,0:T(8,128)S(1)} %get-tuple-element.59.refs_4_), channel_id=1, source_target_pairs={{0,1},{1,2},{2,3},{3,4},{4,5},{5,6},{6,7},{7,8},{8,9},{9,10},{10,1... | collective-permute-start | bytes 122888 | tf_op jit(solution)/shard_map/ppermute | solution.py:395
  4.7 3.1 %collective-permute-start.1 = (f32[80,128]{1,0:T(8,128)S(1)}, f32[80,128]{1,0:T(8,128)S(1)}, u32[]{:S(2)}, u32[]{:S(2)}) collective-permute-start(f32[80,128]{1,0:T(8,128)S(1)} %get-tuple-element.60.refs_3_), channel_id=1, source_target_pairs={{0,16},{16,32},{32,48},{48,64},{64,80},{80,96},{96,112},{112,128},... | collective-permute-start | bytes 122888 | tf_op jit(solution)/shard_map/ppermute | solution.py:395
  7.9 2.3 %tables.1 = (bf16[1024,2048]{1,0:T(8,128)(2,1)S(1)}, bf16[2048,768]{1,0:T(8,128)(2,1)S(1)}, bf16[512,2048]{1,0:T(8,128)(2,1)S(1)}, bf16[2048,512]{1,0:T(8,128)(2...) custom-call(s32[4,512]{1,0:T(4,128)} %bitcast.39, ...), custom_call_target="tpu_custom_call" | custom-call | flops 1000000000 | bytes 4194304 | tf_op jit(solution)/shard_map/tables/pallas_call | solution.py:423
  10.2 0.0 copy-done
  10.2 0.7 gather.1.refs_0_
  10.9 0.0 copy-start.1
  10.9 0.0 copy-start.2
  10.9 0.1 and_select_fusion
  11.0 1.6 %weights.1 = (bf16[2,640,960]{2,1,0:T(8,128)(2,1)S(1)}, f32[1,128]{1,0:T(1,128)S(1)}) custom-call(f32[2,192,192]{2,1,0:T(8,128)S(1)} %get-tuple-element.63.inverse_ref, f32[2,192,320]{2,1,0:T(8,128)S(1)} %get-tuple-element.64.lifting_ref, f32[2,320,320]{2,1,0:T(8,128)S(1)} %get-tuple-element.65.block_ref), custom_call_target="tpu_custom_call" | custom-call | flops 1000000000 | bytes 4194304 | tf_op jit(solution)/shard_map/weights/pallas_call | solution.py:423
  12.6 0.0 collective-permute-done.refs_1_.refs_12_
  12.6 0.8 collective-permute-done.1.refs_2_
  13.4 0.1 broadcast_in_dim.4.refs_11_.refs_7_.refs_12_.refs_13_
  13.5 0.0 copy-done.1
  13.5 0.0 copy-done.2
  13.5 1.6 %step0.1 = (bf16[160,2048]{1,0:T(8,128)(2,1)S(1)}, f32[80,256]{1,0:T(8,128)S(1)}, f32[80,256]{1,0:T(8,128)S(1)}, f32[80,128]{1,0:T(8,128)S(1)}, f32[80,128]{1,0:...) custom-call(f32[80,2048]{1,0:T(8,128)S(1)} %gather.1.refs_0_, ...), custom_call_target="tpu_custom_call" | custom-call | flops 1000000000 | bytes 4194304 | tf_op jit(solution)/shard_map/step0/pallas_call | solution.py:423
  15.1 5.3 %collective-permute-start.2 = (f32[80,128]{1,0:T(8,128)S(1)}, f32[80,128]{1,0:T(8,128)S(1)}, u32[]{:S(2)}, u32[]{:S(2)}) collective-permute-start(f32[80,128]{1,0:T(8,128)S(1)} %get-tuple-element.73), channel_id=1, source_target_pairs={{0,496},{16,32},{32,16},{48,64},{64,48},{80,96},{96,80},{112,128},... | collective-permute-start | bytes 122888 | tf_op jit(solution)/shard_map/ppermute | solution.py:405
  20.4 1.9 %collective-permute-start.3 = (f32[80,128]{1,0:T(8,128)S(1)}, f32[80,128]{1,0:T(8,128)S(1)}, u32[]{:S(2)}, u32[]{:S(2)}) collective-permute-start(f32[80,128]{1,0:T(8,128)S(1)} %get-tuple-element.74), channel_id=1, source_target_pairs={{0,16},{16,0},{32,48},{48,32},{64,80},{80,64},{96,112},{112,96},{1... | collective-permute-start | bytes 122888 | tf_op jit(solution)/shard_map/ppermute | solution.py:405
  22.3 0.3 collective-permute-start.4
  22.6 3.1 %collective-permute-start.5 = (f32[80,128]{1,0:T(8,128)S(1)}, f32[80,128]{1,0:T(8,128)S(1)}, u32[]{:S(2)}, u32[]{:S(2)}) collective-permute-start(f32[80,128]{1,0:T(8,128)S(1)} %get-tuple-element.76), channel_id=1, source_target_pairs={{0,15},{1,0},{2,1},{3,2},{4,3},{5,4},{6,5},{7,6},{8,7},{9,8},{10,9... | collective-permute-start | bytes 122888 | tf_op jit(solution)/shard_map/ppermute | solution.py:395
  25.7 1.7 %between0.1 = (f32[8,128]{1,0:T(8,128)S(1)}, f32[80,768]{1,0:T(8,128)S(1)}, f32[80,2048]{1,0:T(8,128)S(1)}) custom-call(bf16[160,2048]{1,0:T(8,128)(2,1)S(1)} %get-tuple-element.68.refs_0_, f32[80,768]{1,0:T(8,128)S(1)} %bitcast.19, f32[80,256]{1,0:T(8,128)S(1)} %get-tuple-element.69.refs_2_.refs_14_, ...), custom_call_target="tpu_custom_call" | custom-call | flops 1000000000 | bytes 4194304 | tf_op jit(solution)/shard_map/between0/pallas_call | solution.py:423
  27.5 0.0 collective-permute-done.2.refs_1_.refs_2_
  27.5 0.0 collective-permute-done.3.refs_2_.refs_3_
  27.5 0.0 collective-permute-done.4.refs_3_.refs_4_.refs_13_
  27.5 0.0 collective-permute-done.5.refs_4_.refs_5_
  27.5 1.7 %step1.1 = (bf16[160,2048]{1,0:T(8,128)(2,1)S(1)}, f32[80,256]{1,0:T(8,128)S(1)}, f32[80,256]{1,0:T(8,128)S(1)}, f32[80,128]{1,0:T(8,128)S(1)}, f32[80,128]{1,0:...) custom-call(f32[80,2048]{1,0:T(8,128)S(1)} %get-tuple-element.72.refs_0_, ...), custom_call_target="tpu_custom_call" | custom-call | flops 1000000000 | bytes 4194304 | tf_op jit(solution)/shard_map/step1/pallas_call | solution.py:423
  29.3 4.1 %collective-permute-start.6 = (f32[80,128]{1,0:T(8,128)S(1)}, f32[80,128]{1,0:T(8,128)S(1)}, u32[]{:S(2)}, u32[]{:S(2)}) collective-permute-start(f32[80,128]{1,0:T(8,128)S(1)} %get-tuple-element.82), channel_id=1, source_target_pairs={{0,496},{16,32},{32,16},{48,64},{64,48},{80,96},{96,80},{112,128},... | collective-permute-start | bytes 122888 | tf_op jit(solution)/shard_map/ppermute | solution.py:405
  33.4 1.9 %collective-permute-start.7 = (f32[80,128]{1,0:T(8,128)S(1)}, f32[80,128]{1,0:T(8,128)S(1)}, u32[]{:S(2)}, u32[]{:S(2)}) collective-permute-start(f32[80,128]{1,0:T(8,128)S(1)} %get-tuple-element.83), channel_id=1, source_target_pairs={{0,16},{16,0},{32,48},{48,32},{64,80},{80,64},{96,112},{112,96},{1... | collective-permute-start | bytes 122888 | tf_op jit(solution)/shard_map/ppermute | solution.py:405
  35.4 0.0 collective-permute-start.8
  35.4 3.2 %collective-permute-start.9 = (f32[80,128]{1,0:T(8,128)S(1)}, f32[80,128]{1,0:T(8,128)S(1)}, u32[]{:S(2)}, u32[]{:S(2)}) collective-permute-start(f32[80,128]{1,0:T(8,128)S(1)} %get-tuple-element.85), channel_id=1, source_target_pairs={{0,15},{1,0},{2,1},{3,2},{4,3},{5,4},{6,5},{7,6},{8,7},{9,8},{10,9... | collective-permute-start | bytes 122888 | tf_op jit(solution)/shard_map/ppermute | solution.py:395
  38.6 1.8 %between1.1 = (f32[80,768]{1,0:T(8,128)S(1)}, f32[8,128]{1,0:T(8,128)S(1)}, f32[80,768]{1,0:T(8,128)S(1)}, f32[80,2048]{1,0:T(8,128)S(1)}) custom-call(bf16[160,2048]{1,0:T(8,128)(2,1)S(1)} %get-tuple-element.78.refs_0_, f32[80,768]{1,0:T(8,128)S(1)} %get-tuple-element.79.refs_1_, f32[80,128]{1,0:T(8,128)S(1)} %collective-permute-done.2.refs_1_.refs_2_, ...), custom_call_target="tpu_custom_call" | custom-call | flops 1000000000 | bytes 4194304 | tf_op jit(solution)/shard_map/between1/pallas_call | solution.py:423
  40.4 0.0 collective-permute-done.6.refs_1_.refs_2_
  40.4 0.0 collective-permute-done.7.refs_2_.refs_3_
  40.4 0.0 collective-permute-done.8.refs_3_.refs_4_.refs_15_
  40.4 0.0 collective-permute-done.9.refs_4_.refs_5_
  40.5 1.7 %step2.1 = (bf16[160,2048]{1,0:T(8,128)(2,1)S(1)}, f32[80,256]{1,0:T(8,128)S(1)}, f32[80,256]{1,0:T(8,128)S(1)}, f32[80,128]{1,0:T(8,128)S(1)}, f32[80,128]{1,0:...) custom-call(f32[80,2048]{1,0:T(8,128)S(1)} %get-tuple-element.81.refs_0_, ...), custom_call_target="tpu_custom_call" | custom-call | flops 1000000000 | bytes 4194304 | tf_op jit(solution)/shard_map/step2/pallas_call | solution.py:423
  42.2 4.8 %collective-permute-start.10 = (f32[80,128]{1,0:T(8,128)S(1)}, f32[80,128]{1,0:T(8,128)S(1)}, u32[]{:S(2)}, u32[]{:S(2)}) collective-permute-start(f32[80,128]{1,0:T(8,128)S(1)} %get-tuple-element.92), channel_id=1, source_target_pairs={{0,496},{16,32},{32,16},{48,64},{64,48},{80,96},{96,80},{112,128},... | collective-permute-start | bytes 122888 | tf_op jit(solution)/shard_map/ppermute | solution.py:405
  47.0 2.1 %collective-permute-start.11 = (f32[80,128]{1,0:T(8,128)S(1)}, f32[80,128]{1,0:T(8,128)S(1)}, u32[]{:S(2)}, u32[]{:S(2)}) collective-permute-start(f32[80,128]{1,0:T(8,128)S(1)} %get-tuple-element.93), channel_id=1, source_target_pairs={{0,16},{16,0},{32,48},{48,32},{64,80},{80,64},{96,112},{112,96},{1... | collective-permute-start | bytes 122888 | tf_op jit(solution)/shard_map/ppermute | solution.py:405
  49.1 0.0 collective-permute-start.12
  49.1 3.2 %collective-permute-start.13 = (f32[80,128]{1,0:T(8,128)S(1)}, f32[80,128]{1,0:T(8,128)S(1)}, u32[]{:S(2)}, u32[]{:S(2)}) collective-permute-start(f32[80,128]{1,0:T(8,128)S(1)} %get-tuple-element.95), channel_id=1, source_target_pairs={{0,15},{1,0},{2,1},{3,2},{4,3},{5,4},{6,5},{7,6},{8,7},{9,8},{10,9... | collective-permute-start | bytes 122888 | tf_op jit(solution)/shard_map/ppermute | solution.py:395
  52.4 1.8 %between2.1 = (f32[80,768]{1,0:T(8,128)S(1)}, f32[8,128]{1,0:T(8,128)S(1)}, f32[80,768]{1,0:T(8,128)S(1)}, f32[80,2048]{1,0:T(8,128)S(1)}) custom-call(bf16[160,2048]{1,0:T(8,128)(2,1)S(1)} %get-tuple-element.87.refs_0_, f32[80,768]{1,0:T(8,128)S(1)} %get-tuple-element.88.refs_1_, f32[80,128]{1,0:T(8,128)S(1)} %collective-permute-done.6.refs_1_.refs_2_, ...), custom_call_target="tpu_custom_call" | custom-call | flops 1000000000 | bytes 4194304 | tf_op jit(solution)/shard_map/between2/pallas_call | solution.py:423
  54.2 0.0 collective-permute-done.10.refs_1_.refs_2_
  54.2 0.0 collective-permute-done.11.refs_2_.refs_3_
  54.2 0.0 collective-permute-done.12.refs_3_.refs_4_.refs_17_
  54.2 0.0 collective-permute-done.13.refs_4_.refs_5_
  54.2 1.6 %step3.1 = (bf16[160,2048]{1,0:T(8,128)(2,1)S(1)}, f32[80,128]{1,0:T(8,128)S(1)}, f32[80,128]{1,0:T(8,128)S(1)}) custom-call(f32[80,2048]{1,0:T(8,128)S(1)} %get-tuple-element.91.refs_0_, f32[80,128]{1,0:T(8,128)S(1)} %collective-permute-done.10.refs_1_.refs_2_, f32[80,128]{1,0:T(8,128)S(1)} %collective-permute-done.11.refs_2_.refs_3_, ...), custom_call_target="tpu_custom_call" | custom-call | flops 1000000000 | bytes 4194304 | tf_op jit(solution)/shard_map/step3/pallas_call | solution.py:423
  55.9 3.9 %collective-permute-start.14 = (f32[80,128]{1,0:T(8,128)S(1)}, f32[80,128]{1,0:T(8,128)S(1)}, u32[]{:S(2)}, u32[]{:S(2)}) collective-permute-start(f32[80,128]{1,0:T(8,128)S(1)} %get-tuple-element.101), channel_id=1, source_target_pairs={{0,496},{16,0},{32,16},{48,32},{64,48},{80,64},{96,80},{112,96},{1... | collective-permute-start | bytes 122888 | tf_op jit(solution)/shard_map/ppermute | solution.py:395
  59.7 0.0 collective-permute-start.15
  59.8 1.0 %between3.1 = (f32[80,768]{1,0:T(8,128)S(1)}, f32[8,128]{1,0:T(8,128)S(1)}, f32[80,768]{1,0:T(8,128)S(1)}, f32[80,128]{1,0:T(8,128)S(1)}) custom-call(bf16[160,2048]{1,0:T(8,128)(2,1)S(1)} %get-tuple-element.97.refs_0_, f32[80,768]{1,0:T(8,128)S(1)} %get-tuple-element.98.refs_1_, f32[80,128]{1,0:T(8,128)S(1)} %collective-permute-done.10.refs_1_.refs_2_, ...), custom_call_target="tpu_custom_call" | custom-call | flops 1000000000 | bytes 4194304 | tf_op jit(solution)/shard_map/between3/pallas_call | solution.py:423
  60.8 0.1 collective-permute-done.14.refs_1_
  60.9 2.8 %collective-permute-done.15.refs_2_ = f32[80,128]{1,0:T(8,128)S(1)} collective-permute-done((f32[80,128]{1,0:T(8,128)S(1)}, f32[80,128]{1,0:T(8,128)S(1)}, u32[]{:S(2)}, u32[]{:S(2)}) %collective-permute-start.15) | collective-permute-done | bytes 40992 | tf_op jit(solution)/shard_map/ppermute | solution.py:395
  63.7 0.4 last.1
  64.1 16.3 %all_to_all.10 = f32[16,1,128]{2,1,0:T(1,128)S(1)} all-to-all(f32[16,1,128]{2,1,0:T(1,128)S(1)} %bitcast.27), channel_id=1, replica_groups=mesh['gx'=32,'yz'=16] {'yz'}, dimensions={0} | all-to-all | bytes 16384 | tf_op jit(solution)/shard_map/all_to_all | solution.py:410
  80.4 15.9 %all_to_all.11 = f32[32,1,128]{2,1,0:T(1,128)S(1)} all-to-all(f32[32,1,128]{2,1,0:T(1,128)S(1)} %bitcast.26), channel_id=1, replica_groups=mesh['gx'=32,'yz'=16] {'gx'}, dimensions={0} | all-to-all | bytes 32768 | tf_op jit(solution)/shard_map/all_to_all | solution.py:410
  96.3 1.1 %solve.1 = f32[80,768]{1,0:T(8,128)} custom-call(f32[32,128]{1,0:T(8,128)S(1)} %bitcast.25, f32[1,128]{1,0:T(1,128)S(1)} %get-tuple-element.67.refs_10_.refs_6_.refs_11_.refs_12_.scale_ref, f32[80,768]{1,0:T(8,128)S(1)} %bitcast.24, f32[80,768]{1,0:T(8,128)S(1)} %get-tuple-element.90.refs_8_.refs_7_.refs_5_.refs_1_, ...), custom_call_target="tpu_custom_call" | custom-call | bytes 4194304 | tf_op jit(solution)/shard_map/solve/pallas_call | solution.py:423
  (1 shorter events, 0.0 us)
Async XLA Ops:
  0.0 10.2 %copy-start = (f32[1,1,80,768]{3,2,1,0:T(8,128)S(1)}, f32[1,1,80,768]{3,2,1,0:T(8,128)}, u32[]{:S(2)}) copy-start(f32[1,1,80,768]{3,2,1,0:T(8,128)} %param.8) | copy-start | bytes 737284
  1.3 11.4 %collective-permute-start = (f32[80,128]{1,0:T(8,128)S(1)}, f32[80,128]{1,0:T(8,128)S(1)}, u32[]{:S(2)}, u32[]{:S(2)}) collective-permute-start(f32[80,128]{1,0:T(8,128)S(1)} %get-tuple-element.59.refs_4_), channel_id=1, source_target_pairs={{0,1},{1,2},{2,3},{3,4},{4,5},{5,6},{6,7},{7,8},{8,9},{9,10},{10,1... | collective-permute-start | bytes 122888 | tf_op jit(solution)/shard_map/ppermute | solution.py:395
  4.7 8.7 %collective-permute-start.1 = (f32[80,128]{1,0:T(8,128)S(1)}, f32[80,128]{1,0:T(8,128)S(1)}, u32[]{:S(2)}, u32[]{:S(2)}) collective-permute-start(f32[80,128]{1,0:T(8,128)S(1)} %get-tuple-element.60.refs_3_), channel_id=1, source_target_pairs={{0,16},{16,32},{32,48},{48,64},{64,80},{80,96},{96,112},{112,128},... | collective-permute-start | bytes 122888 | tf_op jit(solution)/shard_map/ppermute | solution.py:395
  10.9 2.6 %copy-start.1 = (f32[1,1,512]{2,1,0:T(1,128)S(1)}, f32[1,1,512]{2,1,0:T(1,128)}, u32[]{:S(2)}) copy-start(f32[1,1,512]{2,1,0:T(1,128)} %param.11) | copy-start | bytes 6148
  10.9 2.6 %copy-start.2 = (f32[1,1,512]{2,1,0:T(1,128)S(1)}, f32[1,1,512]{2,1,0:T(1,128)}, u32[]{:S(2)}) copy-start(f32[1,1,512]{2,1,0:T(1,128)} %param.12) | copy-start | bytes 6148
  15.1 12.4 %collective-permute-start.2 = (f32[80,128]{1,0:T(8,128)S(1)}, f32[80,128]{1,0:T(8,128)S(1)}, u32[]{:S(2)}, u32[]{:S(2)}) collective-permute-start(f32[80,128]{1,0:T(8,128)S(1)} %get-tuple-element.73), channel_id=1, source_target_pairs={{0,496},{16,32},{32,16},{48,64},{64,48},{80,96},{96,80},{112,128},... | collective-permute-start | bytes 122888 | tf_op jit(solution)/shard_map/ppermute | solution.py:405
  20.4 7.1 %collective-permute-start.3 = (f32[80,128]{1,0:T(8,128)S(1)}, f32[80,128]{1,0:T(8,128)S(1)}, u32[]{:S(2)}, u32[]{:S(2)}) collective-permute-start(f32[80,128]{1,0:T(8,128)S(1)} %get-tuple-element.74), channel_id=1, source_target_pairs={{0,16},{16,0},{32,48},{48,32},{64,80},{80,64},{96,112},{112,96},{1... | collective-permute-start | bytes 122888 | tf_op jit(solution)/shard_map/ppermute | solution.py:405
  22.3 5.2 %collective-permute-start.4 = (f32[80,128]{1,0:T(8,128)S(1)}, f32[80,128]{1,0:T(8,128)S(1)}, u32[]{:S(2)}, u32[]{:S(2)}) collective-permute-start(f32[80,128]{1,0:T(8,128)S(1)} %get-tuple-element.75), channel_id=1, source_target_pairs={{0,1},{1,2},{2,3},{3,4},{4,5},{5,6},{6,7},{7,8},{8,9},{9,10},{10,1... | collective-permute-start | bytes 122888 | tf_op jit(solution)/shard_map/ppermute | solution.py:395
  22.6 4.9 %collective-permute-start.5 = (f32[80,128]{1,0:T(8,128)S(1)}, f32[80,128]{1,0:T(8,128)S(1)}, u32[]{:S(2)}, u32[]{:S(2)}) collective-permute-start(f32[80,128]{1,0:T(8,128)S(1)} %get-tuple-element.76), channel_id=1, source_target_pairs={{0,15},{1,0},{2,1},{3,2},{4,3},{5,4},{6,5},{7,6},{8,7},{9,8},{10,9... | collective-permute-start | bytes 122888 | tf_op jit(solution)/shard_map/ppermute | solution.py:395
  29.3 11.1 %collective-permute-start.6 = (f32[80,128]{1,0:T(8,128)S(1)}, f32[80,128]{1,0:T(8,128)S(1)}, u32[]{:S(2)}, u32[]{:S(2)}) collective-permute-start(f32[80,128]{1,0:T(8,128)S(1)} %get-tuple-element.82), channel_id=1, source_target_pairs={{0,496},{16,32},{32,16},{48,64},{64,48},{80,96},{96,80},{112,128},... | collective-permute-start | bytes 122888 | tf_op jit(solution)/shard_map/ppermute | solution.py:405
  33.4 7.0 %collective-permute-start.7 = (f32[80,128]{1,0:T(8,128)S(1)}, f32[80,128]{1,0:T(8,128)S(1)}, u32[]{:S(2)}, u32[]{:S(2)}) collective-permute-start(f32[80,128]{1,0:T(8,128)S(1)} %get-tuple-element.83), channel_id=1, source_target_pairs={{0,16},{16,0},{32,48},{48,32},{64,80},{80,64},{96,112},{112,96},{1... | collective-permute-start | bytes 122888 | tf_op jit(solution)/shard_map/ppermute | solution.py:405
  35.4 5.1 %collective-permute-start.8 = (f32[80,128]{1,0:T(8,128)S(1)}, f32[80,128]{1,0:T(8,128)S(1)}, u32[]{:S(2)}, u32[]{:S(2)}) collective-permute-start(f32[80,128]{1,0:T(8,128)S(1)} %get-tuple-element.84), channel_id=1, source_target_pairs={{0,1},{1,2},{2,3},{3,4},{4,5},{5,6},{6,7},{7,8},{8,9},{9,10},{10,1... | collective-permute-start | bytes 122888 | tf_op jit(solution)/shard_map/ppermute | solution.py:395
  35.4 5.1 %collective-permute-start.9 = (f32[80,128]{1,0:T(8,128)S(1)}, f32[80,128]{1,0:T(8,128)S(1)}, u32[]{:S(2)}, u32[]{:S(2)}) collective-permute-start(f32[80,128]{1,0:T(8,128)S(1)} %get-tuple-element.85), channel_id=1, source_target_pairs={{0,15},{1,0},{2,1},{3,2},{4,3},{5,4},{6,5},{7,6},{8,7},{9,8},{10,9... | collective-permute-start | bytes 122888 | tf_op jit(solution)/shard_map/ppermute | solution.py:395
  42.2 12.0 %collective-permute-start.10 = (f32[80,128]{1,0:T(8,128)S(1)}, f32[80,128]{1,0:T(8,128)S(1)}, u32[]{:S(2)}, u32[]{:S(2)}) collective-permute-start(f32[80,128]{1,0:T(8,128)S(1)} %get-tuple-element.92), channel_id=1, source_target_pairs={{0,496},{16,32},{32,16},{48,64},{64,48},{80,96},{96,80},{112,128},... | collective-permute-start | bytes 122888 | tf_op jit(solution)/shard_map/ppermute | solution.py:405
  47.0 7.2 %collective-permute-start.11 = (f32[80,128]{1,0:T(8,128)S(1)}, f32[80,128]{1,0:T(8,128)S(1)}, u32[]{:S(2)}, u32[]{:S(2)}) collective-permute-start(f32[80,128]{1,0:T(8,128)S(1)} %get-tuple-element.93), channel_id=1, source_target_pairs={{0,16},{16,0},{32,48},{48,32},{64,80},{80,64},{96,112},{112,96},{1... | collective-permute-start | bytes 122888 | tf_op jit(solution)/shard_map/ppermute | solution.py:405
  49.1 5.1 %collective-permute-start.12 = (f32[80,128]{1,0:T(8,128)S(1)}, f32[80,128]{1,0:T(8,128)S(1)}, u32[]{:S(2)}, u32[]{:S(2)}) collective-permute-start(f32[80,128]{1,0:T(8,128)S(1)} %get-tuple-element.94), channel_id=1, source_target_pairs={{0,1},{1,2},{2,3},{3,4},{4,5},{5,6},{6,7},{7,8},{8,9},{9,10},{10,1... | collective-permute-start | bytes 122888 | tf_op jit(solution)/shard_map/ppermute | solution.py:395
  49.1 5.1 %collective-permute-start.13 = (f32[80,128]{1,0:T(8,128)S(1)}, f32[80,128]{1,0:T(8,128)S(1)}, u32[]{:S(2)}, u32[]{:S(2)}) collective-permute-start(f32[80,128]{1,0:T(8,128)S(1)} %get-tuple-element.95), channel_id=1, source_target_pairs={{0,15},{1,0},{2,1},{3,2},{4,3},{5,4},{6,5},{7,6},{8,7},{9,8},{10,9... | collective-permute-start | bytes 122888 | tf_op jit(solution)/shard_map/ppermute | solution.py:395
  55.9 5.0 %collective-permute-start.14 = (f32[80,128]{1,0:T(8,128)S(1)}, f32[80,128]{1,0:T(8,128)S(1)}, u32[]{:S(2)}, u32[]{:S(2)}) collective-permute-start(f32[80,128]{1,0:T(8,128)S(1)} %get-tuple-element.101), channel_id=1, source_target_pairs={{0,496},{16,0},{32,16},{48,32},{64,48},{80,64},{96,80},{112,96},{1... | collective-permute-start | bytes 122888 | tf_op jit(solution)/shard_map/ppermute | solution.py:395
  59.7 3.9 %collective-permute-start.15 = (f32[80,128]{1,0:T(8,128)S(1)}, f32[80,128]{1,0:T(8,128)S(1)}, u32[]{:S(2)}, u32[]{:S(2)}) collective-permute-start(f32[80,128]{1,0:T(8,128)S(1)} %get-tuple-element.102), channel_id=1, source_target_pairs={{0,1},{1,2},{2,3},{3,4},{4,5},{5,6},{6,7},{7,8},{8,9},{9,10},{10,1... | collective-permute-start | bytes 122888 | tf_op jit(solution)/shard_map/ppermute | solution.py:395

commit v8 on v7

--- a/solution.py
+++ b/solution.py
@@ -128,10 +128,12 @@
             spread_ref[start : start + group, :] = select_ref[:owned, start : start + group].T
             row = table[k : k + 1, part]
             for i in range(2):
-                meet_ref[i * shared : (i + 1) * shared, start : start + group] = jnp.where(
+                meet_ref[2 * i * shared : (2 * i + 1) * shared, start : start + group] = jnp.where(
                     sends[:, i : i + 1] == row, 1.0, 0.0
                 ).astype(BF16)
-            meet_ref[2 * shared :, start : start + group] = select_ref[owned:, start : start + group]
+                meet_ref[(2 * i + 1) * shared : (2 * i + 2) * shared, start : start + group] = select_ref[
+                    owned + i * shared : owned + (i + 1) * shared, start : start + group
+                ]
             leave_ref[start : start + group, :] = meet_ref[:, start : start + group].T
     for have in have_weights:
         have()
@@ -178,6 +180,14 @@
     known_ref[...] = folded(dot(stacked(source_ref[...]), select_ref[: source_ref.shape[1], :]))
 
 
+def partway_kernel(known_ref, later_ref, first_ref, meet_ref, odd_ref, read_ref):
+    odd = odd_ref[:1, :] != 0
+    later, first = later_ref[...], first_ref[...]
+    pair = jnp.concatenate([jnp.where(odd, later, first), jnp.where(odd, first, later)], axis=1)
+    rows = meet_ref.shape[0] // 2
+    read_ref[...] = known_ref[...] + folded(dot(stacked(pair), meet_ref[:rows, :]))
+
+
 def step_kernel(first, final, *refs):
     refs = list(refs)
     known_ref = refs.pop(0)
@@ -195,12 +205,12 @@
     own = jnp.concatenate([ref[...] for ref in sent_before], axis=1)
     if first:
         section, slab = [ref[...] for ref in got]
-        arrivals = jnp.concatenate([slab, section], axis=1)
-        read = folded(dot(stacked(arrivals), meet_ref[2 * shared :, :]))
+        read = folded(dot(stacked(slab), meet_ref[shared : 2 * shared, :]))
+        read = read + folded(dot(stacked(section), meet_ref[3 * shared :, :]))
     else:
         back, up = arrived(got, odd)
         own = own + jnp.concatenate(back, axis=1)
-        read = folded(dot(stacked(jnp.concatenate(back + up, axis=1)), meet_ref[...]))
+        read = folded(dot(stacked(jnp.concatenate([back[1], up[1]], axis=1)), meet_ref[2 * shared :, :]))
     read = known_ref[...] + read
     for t in range(shapes):
         columns = slice(t * group, (t + 1) * group)
@@ -218,14 +228,15 @@
     shrink = 1.0 / scale_ref[:, :1]
     if final:
         leaving = folded(dot(result_ref[...], leave_ref[:, shared : 3 * shared])) * shrink
-        refs[8][...] = leaving[:, shared:]
-        refs[9][...] = leaving[:, :shared] - (SHIFT * shrink) * own[:, shared:]
+        refs[8][...] = leaving[:, :shared]
+        refs[9][...] = leaving[:, shared:] - (SHIFT * shrink) * own[:, shared:]
         return
     down_ref, sent_ref = refs[8:10]
     leaving = folded(dot(result_ref[...], leave_ref[...])) * shrink
-    down = [leaving[:, (2 + i) * shared : (3 + i) * shared] for i in range(2)]
-    down_ref[...] = leaving[:, 2 * shared :]
-    sent = leaving[:, : 2 * shared] - (SHIFT * shrink) * own
+    quarters = [leaving[:, i * shared : (i + 1) * shared] for i in range(4)]
+    down = quarters[1::2]
+    down_ref[...] = jnp.concatenate(down, axis=1)
+    sent = jnp.concatenate(quarters[::2], axis=1) - (SHIFT * shrink) * own
     sent_ref[...] = sent
     up = [sent[:, i * shared : (i + 1) * shared] for i in range(2)]
     parts = {
@@ -503,6 +514,11 @@
     for j in range(ITERS):
         first, final = j == 0, j == ITERS - 1
         outs = [shape(2 * dofs, 4 * elements, dtype=BF16)]
+        if not first:
+            along_gx = [got[STARTS.index(name)] for name in ("gx later", "gx first")]
+            known = call(
+                partway_kernel, shape(dofs, 4 * elements), known, *along_gx, meet, odd, flops=10**8, name=f"partway{j}"
+            )
         results = call(
             functools.partial(step_kernel, first, final),
             tuple(outs + ([part] * 2 if final else [both] * 2 + [part] * 4)),

time: 97.8 us -> 98.6 us (level)
    pallas_call x15 -> x18, Pallas kernels: 20.4 us -> 21.2 us  [call(): pl.pallas_call(kernel, out_shape=out_shape, in_specs=[pl.BlockSpec(memory...]
  transfers between devices with their start and end apart: 16 -> 16, of which waited for: 3 -> 3; matrix products, arithmetic and copies ran while one was open for 0% -> 0% of each run, Pallas kernels for 11% -> 12%
where the time goes in v8:
time: 98.6 us; the launch traced here: 98.2 us
  starting transfers between devices  40.7 us (41%)
  blocking collectives  32.2 us (33%)
  Pallas kernels  21.2 us (22%)
  waiting for transfers between devices  3.57 us (4%)
    all_to_all x2, blocking collectives, every(): lax.all_to_all(row.reshape(count, 1, 128), axis, 0, 0).reshape(count, 128)  32.2 us
    pallas_call x18, Pallas kernels, call(): pl.pallas_call(kernel, out_shape=out_shape, in_specs=[pl.BlockSpec(memory...  21.2 us
    ppermute x10, starting transfers between devices, passed_along(): return lax.ppermute(value, axis, pairs)  20.5 us
    ppermute x6, starting transfers between devices, exchange(): return lax.ppermute(value, axis, pairs)  20.2 us
    ppermute x10, waiting for transfers between devices, passed_along(): return lax.ppermute(value, axis, pairs)  3.55 us
  transfers between devices with their start and end apart: 16, of which 3 were waited for; matrix products, arithmetic and copies ran while one was open for 0% of the time, Pallas kernels for 12%

profile of v8, /device:TPU:1, one launch (start us, length us, event | category | flops | bytes accessed | tf_op | source)
XLA Modules:
  0.0 98.2 jit_solution(1900983983992202893)
XLA Ops:
  0.0 0.0 copy-start
  0.0 1.2 %first.1 = (f32[80,128]{1,0:T(8,128)S(1)}, f32[80,128]{1,0:T(8,128)S(1)}, s32[2,128]{1,0:T(2,128)S(1)}) custom-call(f32[80,768]{1,0:T(8,128)} %bitcast.17, s32[2,128]{1,0:T(2,128)} %bitcast.37), custom_call_target="tpu_custom_call" | custom-call | bytes 4194304 | tf_op jit(solution)/shard_map/first/pallas_call | solution.py:434
  1.3 3.5 %collective-permute-start = (f32[80,128]{1,0:T(8,128)S(1)}, f32[80,128]{1,0:T(8,128)S(1)}, u32[]{:S(2)}, u32[]{:S(2)}) collective-permute-start(f32[80,128]{1,0:T(8,128)S(1)} %get-tuple-element.59.refs_4_), channel_id=1, source_target_pairs={{0,1},{1,2},{2,3},{3,4},{4,5},{5,6},{6,7},{7,8},{8,9},{9,10},{10,1... | collective-permute-start | bytes 122888 | tf_op jit(solution)/shard_map/ppermute | solution.py:406
  4.7 3.1 %collective-permute-start.1 = (f32[80,128]{1,0:T(8,128)S(1)}, f32[80,128]{1,0:T(8,128)S(1)}, u32[]{:S(2)}, u32[]{:S(2)}) collective-permute-start(f32[80,128]{1,0:T(8,128)S(1)} %get-tuple-element.60.refs_3_), channel_id=1, source_target_pairs={{0,16},{16,32},{32,48},{48,64},{64,80},{80,96},{96,112},{112,128},... | collective-permute-start | bytes 122888 | tf_op jit(solution)/shard_map/ppermute | solution.py:406
  7.9 2.4 %tables.1 = (bf16[1024,2048]{1,0:T(8,128)(2,1)S(1)}, bf16[2048,768]{1,0:T(8,128)(2,1)S(1)}, bf16[512,2048]{1,0:T(8,128)(2,1)S(1)}, bf16[2048,512]{1,0:T(8,128)(2...) custom-call(s32[4,512]{1,0:T(4,128)} %bitcast.39, ...), custom_call_target="tpu_custom_call" | custom-call | flops 1000000000 | bytes 4194304 | tf_op jit(solution)/shard_map/tables/pallas_call | solution.py:434
  10.3 0.0 copy-done
  10.3 0.7 gather.1.refs_0_
  11.0 0.0 copy-start.1
  11.0 0.0 copy-start.2
  11.0 0.1 and_select_fusion
  11.1 1.6 %weights.1 = (bf16[2,640,960]{2,1,0:T(8,128)(2,1)S(1)}, f32[1,128]{1,0:T(1,128)S(1)}) custom-call(f32[2,192,192]{2,1,0:T(8,128)S(1)} %get-tuple-element.63.inverse_ref, f32[2,192,320]{2,1,0:T(8,128)S(1)} %get-tuple-element.64.lifting_ref, f32[2,320,320]{2,1,0:T(8,128)S(1)} %get-tuple-element.65.block_ref), custom_call_target="tpu_custom_call" | custom-call | flops 1000000000 | bytes 4194304 | tf_op jit(solution)/shard_map/weights/pallas_call | solution.py:434
  12.7 0.0 collective-permute-done.refs_1_.refs_12_
  12.8 0.7 collective-permute-done.1.refs_2_
  13.4 0.1 broadcast_in_dim.4.refs_11_.refs_7_.odd_ref.refs_12_.refs_13_
  13.5 0.0 copy-done.1
  13.5 0.0 copy-done.2
  13.5 1.7 %step0.1 = (bf16[160,2048]{1,0:T(8,128)(2,1)S(1)}, f32[80,256]{1,0:T(8,128)S(1)}, f32[80,256]{1,0:T(8,128)S(1)}, f32[80,128]{1,0:T(8,128)S(1)}, f32[80,128]{1,0:...) custom-call(f32[80,2048]{1,0:T(8,128)S(1)} %gather.1.refs_0_, ...), custom_call_target="tpu_custom_call" | custom-call | flops 1000000000 | bytes 4194304 | tf_op jit(solution)/shard_map/step0/pallas_call | solution.py:434
  15.2 5.4 %collective-permute-start.2 = (f32[80,128]{1,0:T(8,128)S(1)}, f32[80,128]{1,0:T(8,128)S(1)}, u32[]{:S(2)}, u32[]{:S(2)}) collective-permute-start(f32[80,128]{1,0:T(8,128)S(1)} %get-tuple-element.73), channel_id=1, source_target_pairs={{0,496},{16,32},{32,16},{48,64},{64,48},{80,96},{96,80},{112,128},... | collective-permute-start | bytes 122888 | tf_op jit(solution)/shard_map/ppermute | solution.py:416
  20.6 1.9 %collective-permute-start.3 = (f32[80,128]{1,0:T(8,128)S(1)}, f32[80,128]{1,0:T(8,128)S(1)}, u32[]{:S(2)}, u32[]{:S(2)}) collective-permute-start(f32[80,128]{1,0:T(8,128)S(1)} %get-tuple-element.74), channel_id=1, source_target_pairs={{0,16},{16,0},{32,48},{48,32},{64,80},{80,64},{96,112},{112,96},{1... | collective-permute-start | bytes 122888 | tf_op jit(solution)/shard_map/ppermute | solution.py:416
  22.6 0.3 collective-permute-start.4
  22.9 3.1 %collective-permute-start.5 = (f32[80,128]{1,0:T(8,128)S(1)}, f32[80,128]{1,0:T(8,128)S(1)}, u32[]{:S(2)}, u32[]{:S(2)}) collective-permute-start(f32[80,128]{1,0:T(8,128)S(1)} %get-tuple-element.76), channel_id=1, source_target_pairs={{0,15},{1,0},{2,1},{3,2},{4,3},{5,4},{6,5},{7,6},{8,7},{9,8},{10,9... | collective-permute-start | bytes 122888 | tf_op jit(solution)/shard_map/ppermute | solution.py:406
  26.0 1.8 %between0.1 = (f32[8,128]{1,0:T(8,128)S(1)}, f32[80,768]{1,0:T(8,128)S(1)}, f32[80,2048]{1,0:T(8,128)S(1)}) custom-call(bf16[160,2048]{1,0:T(8,128)(2,1)S(1)} %get-tuple-element.68.refs_0_, f32[80,768]{1,0:T(8,128)S(1)} %bitcast.19, f32[80,256]{1,0:T(8,128)S(1)} %get-tuple-element.69.refs_2_.refs_14_, ...), custom_call_target="tpu_custom_call" | custom-call | flops 1000000000 | bytes 4194304 | tf_op jit(solution)/shard_map/between0/pallas_call | solution.py:434
  27.7 0.0 collective-permute-done.2.later_ref.refs_1_.refs_2_
  27.7 0.0 collective-permute-done.3.first_ref.refs_2_.refs_3_
  27.8 0.3 partway1.1.refs_0_
  28.1 0.0 collective-permute-done.4.refs_3_.refs_4_.refs_13_
  28.1 0.0 collective-permute-done.5.refs_4_.refs_5_
  28.1 1.6 %step1.1 = (bf16[160,2048]{1,0:T(8,128)(2,1)S(1)}, f32[80,256]{1,0:T(8,128)S(1)}, f32[80,256]{1,0:T(8,128)S(1)}, f32[80,128]{1,0:T(8,128)S(1)}, f32[80,128]{1,0:...) custom-call(f32[80,2048]{1,0:T(8,128)S(1)} %partway1.1.refs_0_, ...), custom_call_target="tpu_custom_call" | custom-call | flops 1000000000 | bytes 4194304 | tf_op jit(solution)/shard_map/step1/pallas_call | solution.py:434
  29.7 4.0 %collective-permute-start.6 = (f32[80,128]{1,0:T(8,128)S(1)}, f32[80,128]{1,0:T(8,128)S(1)}, u32[]{:S(2)}, u32[]{:S(2)}) collective-permute-start(f32[80,128]{1,0:T(8,128)S(1)} %get-tuple-element.82), channel_id=1, source_target_pairs={{0,496},{16,32},{32,16},{48,64},{64,48},{80,96},{96,80},{112,128},... | collective-permute-start | bytes 122888 | tf_op jit(solution)/shard_map/ppermute | solution.py:416
  33.7 1.9 %collective-permute-start.7 = (f32[80,128]{1,0:T(8,128)S(1)}, f32[80,128]{1,0:T(8,128)S(1)}, u32[]{:S(2)}, u32[]{:S(2)}) collective-permute-start(f32[80,128]{1,0:T(8,128)S(1)} %get-tuple-element.83), channel_id=1, source_target_pairs={{0,16},{16,0},{32,48},{48,32},{64,80},{80,64},{96,112},{112,96},{1... | collective-permute-start | bytes 122888 | tf_op jit(solution)/shard_map/ppermute | solution.py:416
  35.7 0.0 collective-permute-start.8
  35.7 3.3 %collective-permute-start.9 = (f32[80,128]{1,0:T(8,128)S(1)}, f32[80,128]{1,0:T(8,128)S(1)}, u32[]{:S(2)}, u32[]{:S(2)}) collective-permute-start(f32[80,128]{1,0:T(8,128)S(1)} %get-tuple-element.85), channel_id=1, source_target_pairs={{0,15},{1,0},{2,1},{3,2},{4,3},{5,4},{6,5},{7,6},{8,7},{9,8},{10,9... | collective-permute-start | bytes 122888 | tf_op jit(solution)/shard_map/ppermute | solution.py:406
  39.0 1.8 %between1.1 = (f32[80,768]{1,0:T(8,128)S(1)}, f32[8,128]{1,0:T(8,128)S(1)}, f32[80,768]{1,0:T(8,128)S(1)}, f32[80,2048]{1,0:T(8,128)S(1)}) custom-call(bf16[160,2048]{1,0:T(8,128)(2,1)S(1)} %get-tuple-element.78.refs_0_, f32[80,768]{1,0:T(8,128)S(1)} %get-tuple-element.79.refs_1_, f32[80,128]{1,0:T(8,128)S(1)} %collective-permute-done.2.later_ref.refs_1_.refs_2_, ...), custom_call_target="tpu_custom_call" | custom-call | flops 1000000000 | bytes 4194304 | tf_op jit(solution)/shard_map/between1/pallas_call | solution.py:434
  40.8 0.0 collective-permute-done.6.later_ref.refs_1_.refs_2_
  40.8 0.0 collective-permute-done.7.first_ref.refs_2_.refs_3_
  40.8 0.3 partway2.1.refs_0_
  41.2 0.0 collective-permute-done.8.refs_3_.refs_4_.refs_15_
  41.2 0.0 collective-permute-done.9.refs_4_.refs_5_
  41.2 1.6 %step2.1 = (bf16[160,2048]{1,0:T(8,128)(2,1)S(1)}, f32[80,256]{1,0:T(8,128)S(1)}, f32[80,256]{1,0:T(8,128)S(1)}, f32[80,128]{1,0:T(8,128)S(1)}, f32[80,128]{1,0:...) custom-call(f32[80,2048]{1,0:T(8,128)S(1)} %partway2.1.refs_0_, ...), custom_call_target="tpu_custom_call" | custom-call | flops 1000000000 | bytes 4194304 | tf_op jit(solution)/shard_map/step2/pallas_call | solution.py:434
  42.8 4.8 %collective-permute-start.10 = (f32[80,128]{1,0:T(8,128)S(1)}, f32[80,128]{1,0:T(8,128)S(1)}, u32[]{:S(2)}, u32[]{:S(2)}) collective-permute-start(f32[80,128]{1,0:T(8,128)S(1)} %get-tuple-element.92), channel_id=1, source_target_pairs={{0,496},{16,32},{32,16},{48,64},{64,48},{80,96},{96,80},{112,128},... | collective-permute-start | bytes 122888 | tf_op jit(solution)/shard_map/ppermute | solution.py:416
  47.6 2.1 %collective-permute-start.11 = (f32[80,128]{1,0:T(8,128)S(1)}, f32[80,128]{1,0:T(8,128)S(1)}, u32[]{:S(2)}, u32[]{:S(2)}) collective-permute-start(f32[80,128]{1,0:T(8,128)S(1)} %get-tuple-element.93), channel_id=1, source_target_pairs={{0,16},{16,0},{32,48},{48,32},{64,80},{80,64},{96,112},{112,96},{1... | collective-permute-start | bytes 122888 | tf_op jit(solution)/shard_map/ppermute | solution.py:416
  49.7 0.0 collective-permute-start.12
  49.7 3.2 %collective-permute-start.13 = (f32[80,128]{1,0:T(8,128)S(1)}, f32[80,128]{1,0:T(8,128)S(1)}, u32[]{:S(2)}, u32[]{:S(2)}) collective-permute-start(f32[80,128]{1,0:T(8,128)S(1)} %get-tuple-element.95), channel_id=1, source_target_pairs={{0,15},{1,0},{2,1},{3,2},{4,3},{5,4},{6,5},{7,6},{8,7},{9,8},{10,9... | collective-permute-start | bytes 122888 | tf_op jit(solution)/shard_map/ppermute | solution.py:406
  53.0 1.8 %between2.1 = (f32[80,768]{1,0:T(8,128)S(1)}, f32[8,128]{1,0:T(8,128)S(1)}, f32[80,768]{1,0:T(8,128)S(1)}, f32[80,2048]{1,0:T(8,128)S(1)}) custom-call(bf16[160,2048]{1,0:T(8,128)(2,1)S(1)} %get-tuple-element.87.refs_0_, f32[80,768]{1,0:T(8,128)S(1)} %get-tuple-element.88.refs_1_, f32[80,128]{1,0:T(8,128)S(1)} %collective-permute-done.6.later_ref.refs_1_.refs_2_, ...), custom_call_target="tpu_custom_call" | custom-call | flops 1000000000 | bytes 4194304 | tf_op jit(solution)/shard_map/between2/pallas_call | solution.py:434
  54.8 0.0 collective-permute-done.10.later_ref.refs_1_.refs_2_
  54.8 0.0 collective-permute-done.11.first_ref.refs_2_.refs_3_
  54.8 0.3 partway3.1.refs_0_
  55.1 0.0 collective-permute-done.12.refs_3_.refs_4_.refs_17_
  55.2 0.0 collective-permute-done.13.refs_4_.refs_5_
  55.2 1.5 %step3.1 = (bf16[160,2048]{1,0:T(8,128)(2,1)S(1)}, f32[80,128]{1,0:T(8,128)S(1)}, f32[80,128]{1,0:T(8,128)S(1)}) custom-call(f32[80,2048]{1,0:T(8,128)S(1)} %partway3.1.refs_0_, f32[80,128]{1,0:T(8,128)S(1)} %collective-permute-done.10.later_ref.refs_1_.refs_2_, f32[80,128]{1,0:T(8,128)S(1)} %collective-permute-done.11.first_ref.refs_2_.refs_3_, ...), custom_call_target="tpu_custom_call" | custom-call | flops 1000000000 | bytes 4194304 | tf_op jit(solution)/shard_map/step3/pallas_call | solution.py:434
  56.7 3.9 %collective-permute-start.14 = (f32[80,128]{1,0:T(8,128)S(1)}, f32[80,128]{1,0:T(8,128)S(1)}, u32[]{:S(2)}, u32[]{:S(2)}) collective-permute-start(f32[80,128]{1,0:T(8,128)S(1)} %get-tuple-element.101), channel_id=1, source_target_pairs={{0,496},{16,0},{32,16},{48,32},{64,48},{80,64},{96,80},{112,96},{1... | collective-permute-start | bytes 122888 | tf_op jit(solution)/shard_map/ppermute | solution.py:406
  60.6 0.0 collective-permute-start.15
  60.6 1.0 %between3.1 = (f32[80,768]{1,0:T(8,128)S(1)}, f32[8,128]{1,0:T(8,128)S(1)}, f32[80,768]{1,0:T(8,128)S(1)}, f32[80,128]{1,0:T(8,128)S(1)}) custom-call(bf16[160,2048]{1,0:T(8,128)(2,1)S(1)} %get-tuple-element.97.refs_0_, f32[80,768]{1,0:T(8,128)S(1)} %get-tuple-element.98.refs_1_, f32[80,128]{1,0:T(8,128)S(1)} %collective-permute-done.10.later_ref.refs_1_.refs_2_, ...), custom_call_target="tpu_custom_call" | custom-call | flops 1000000000 | bytes 4194304 | tf_op jit(solution)/shard_map/between3/pallas_call | solution.py:434
  61.6 0.1 collective-permute-done.14.refs_1_
  61.7 2.8 %collective-permute-done.15.refs_2_ = f32[80,128]{1,0:T(8,128)S(1)} collective-permute-done((f32[80,128]{1,0:T(8,128)S(1)}, f32[80,128]{1,0:T(8,128)S(1)}, u32[]{:S(2)}, u32[]{:S(2)}) %collective-permute-start.15) | collective-permute-done | bytes 40992 | tf_op jit(solution)/shard_map/ppermute | solution.py:406
  64.5 0.4 last.1
  64.9 16.3 %all_to_all.10 = f32[16,1,128]{2,1,0:T(1,128)S(1)} all-to-all(f32[16,1,128]{2,1,0:T(1,128)S(1)} %bitcast.27), channel_id=1, replica_groups=mesh['gx'=32,'yz'=16] {'yz'}, dimensions={0} | all-to-all | bytes 16384 | tf_op jit(solution)/shard_map/all_to_all | solution.py:421
  81.2 15.9 %all_to_all.11 = f32[32,1,128]{2,1,0:T(1,128)S(1)} all-to-all(f32[32,1,128]{2,1,0:T(1,128)S(1)} %bitcast.26), channel_id=1, replica_groups=mesh['gx'=32,'yz'=16] {'gx'}, dimensions={0} | all-to-all | bytes 32768 | tf_op jit(solution)/shard_map/all_to_all | solution.py:421
  97.1 1.1 %solve.1 = f32[80,768]{1,0:T(8,128)} custom-call(f32[32,128]{1,0:T(8,128)S(1)} %bitcast.25, f32[1,128]{1,0:T(1,128)S(1)} %get-tuple-element.67.refs_10_.refs_6_.refs_11_.refs_12_.scale_ref, f32[80,768]{1,0:T(8,128)S(1)} %bitcast.24, f32[80,768]{1,0:T(8,128)S(1)} %get-tuple-element.90.refs_8_.refs_7_.refs_5_.refs_1_, ...), custom_call_target="tpu_custom_call" | custom-call | bytes 4194304 | tf_op jit(solution)/shard_map/solve/pallas_call | solution.py:434
  (1 shorter events, 0.0 us)
Async XLA Ops:
  0.0 10.3 %copy-start = (f32[1,1,80,768]{3,2,1,0:T(8,128)S(1)}, f32[1,1,80,768]{3,2,1,0:T(8,128)}, u32[]{:S(2)}) copy-start(f32[1,1,80,768]{3,2,1,0:T(8,128)} %param.8) | copy-start | bytes 737284
  1.3 11.5 %collective-permute-start = (f32[80,128]{1,0:T(8,128)S(1)}, f32[80,128]{1,0:T(8,128)S(1)}, u32[]{:S(2)}, u32[]{:S(2)}) collective-permute-start(f32[80,128]{1,0:T(8,128)S(1)} %get-tuple-element.59.refs_4_), channel_id=1, source_target_pairs={{0,1},{1,2},{2,3},{3,4},{4,5},{5,6},{6,7},{7,8},{8,9},{9,10},{10,1... | collective-permute-start | bytes 122888 | tf_op jit(solution)/shard_map/ppermute | solution.py:406
  4.7 8.7 %collective-permute-start.1 = (f32[80,128]{1,0:T(8,128)S(1)}, f32[80,128]{1,0:T(8,128)S(1)}, u32[]{:S(2)}, u32[]{:S(2)}) collective-permute-start(f32[80,128]{1,0:T(8,128)S(1)} %get-tuple-element.60.refs_3_), channel_id=1, source_target_pairs={{0,16},{16,32},{32,48},{48,64},{64,80},{80,96},{96,112},{112,128},... | collective-permute-start | bytes 122888 | tf_op jit(solution)/shard_map/ppermute | solution.py:406
  11.0 2.5 %copy-start.1 = (f32[1,1,512]{2,1,0:T(1,128)S(1)}, f32[1,1,512]{2,1,0:T(1,128)}, u32[]{:S(2)}) copy-start(f32[1,1,512]{2,1,0:T(1,128)} %param.11) | copy-start | bytes 6148
  11.0 2.5 %copy-start.2 = (f32[1,1,512]{2,1,0:T(1,128)S(1)}, f32[1,1,512]{2,1,0:T(1,128)}, u32[]{:S(2)}) copy-start(f32[1,1,512]{2,1,0:T(1,128)} %param.12) | copy-start | bytes 6148
  15.2 12.5 %collective-permute-start.2 = (f32[80,128]{1,0:T(8,128)S(1)}, f32[80,128]{1,0:T(8,128)S(1)}, u32[]{:S(2)}, u32[]{:S(2)}) collective-permute-start(f32[80,128]{1,0:T(8,128)S(1)} %get-tuple-element.73), channel_id=1, source_target_pairs={{0,496},{16,32},{32,16},{48,64},{64,48},{80,96},{96,80},{112,128},... | collective-permute-start | bytes 122888 | tf_op jit(solution)/shard_map/ppermute | solution.py:416
  20.6 7.1 %collective-permute-start.3 = (f32[80,128]{1,0:T(8,128)S(1)}, f32[80,128]{1,0:T(8,128)S(1)}, u32[]{:S(2)}, u32[]{:S(2)}) collective-permute-start(f32[80,128]{1,0:T(8,128)S(1)} %get-tuple-element.74), channel_id=1, source_target_pairs={{0,16},{16,0},{32,48},{48,32},{64,80},{80,64},{96,112},{112,96},{1... | collective-permute-start | bytes 122888 | tf_op jit(solution)/shard_map/ppermute | solution.py:416
  22.6 5.5 %collective-permute-start.4 = (f32[80,128]{1,0:T(8,128)S(1)}, f32[80,128]{1,0:T(8,128)S(1)}, u32[]{:S(2)}, u32[]{:S(2)}) collective-permute-start(f32[80,128]{1,0:T(8,128)S(1)} %get-tuple-element.75), channel_id=1, source_target_pairs={{0,1},{1,2},{2,3},{3,4},{4,5},{5,6},{6,7},{7,8},{8,9},{9,10},{10,1... | collective-permute-start | bytes 122888 | tf_op jit(solution)/shard_map/ppermute | solution.py:406
  22.9 5.2 %collective-permute-start.5 = (f32[80,128]{1,0:T(8,128)S(1)}, f32[80,128]{1,0:T(8,128)S(1)}, u32[]{:S(2)}, u32[]{:S(2)}) collective-permute-start(f32[80,128]{1,0:T(8,128)S(1)} %get-tuple-element.76), channel_id=1, source_target_pairs={{0,15},{1,0},{2,1},{3,2},{4,3},{5,4},{6,5},{7,6},{8,7},{9,8},{10,9... | collective-permute-start | bytes 122888 | tf_op jit(solution)/shard_map/ppermute | solution.py:406
  29.7 11.1 %collective-permute-start.6 = (f32[80,128]{1,0:T(8,128)S(1)}, f32[80,128]{1,0:T(8,128)S(1)}, u32[]{:S(2)}, u32[]{:S(2)}) collective-permute-start(f32[80,128]{1,0:T(8,128)S(1)} %get-tuple-element.82), channel_id=1, source_target_pairs={{0,496},{16,32},{32,16},{48,64},{64,48},{80,96},{96,80},{112,128},... | collective-permute-start | bytes 122888 | tf_op jit(solution)/shard_map/ppermute | solution.py:416
  33.7 7.1 %collective-permute-start.7 = (f32[80,128]{1,0:T(8,128)S(1)}, f32[80,128]{1,0:T(8,128)S(1)}, u32[]{:S(2)}, u32[]{:S(2)}) collective-permute-start(f32[80,128]{1,0:T(8,128)S(1)} %get-tuple-element.83), channel_id=1, source_target_pairs={{0,16},{16,0},{32,48},{48,32},{64,80},{80,64},{96,112},{112,96},{1... | collective-permute-start | bytes 122888 | tf_op jit(solution)/shard_map/ppermute | solution.py:416
  35.7 5.5 %collective-permute-start.8 = (f32[80,128]{1,0:T(8,128)S(1)}, f32[80,128]{1,0:T(8,128)S(1)}, u32[]{:S(2)}, u32[]{:S(2)}) collective-permute-start(f32[80,128]{1,0:T(8,128)S(1)} %get-tuple-element.84), channel_id=1, source_target_pairs={{0,1},{1,2},{2,3},{3,4},{4,5},{5,6},{6,7},{7,8},{8,9},{9,10},{10,1... | collective-permute-start | bytes 122888 | tf_op jit(solution)/shard_map/ppermute | solution.py:406
  35.7 5.5 %collective-permute-start.9 = (f32[80,128]{1,0:T(8,128)S(1)}, f32[80,128]{1,0:T(8,128)S(1)}, u32[]{:S(2)}, u32[]{:S(2)}) collective-permute-start(f32[80,128]{1,0:T(8,128)S(1)} %get-tuple-element.85), channel_id=1, source_target_pairs={{0,15},{1,0},{2,1},{3,2},{4,3},{5,4},{6,5},{7,6},{8,7},{9,8},{10,9... | collective-permute-start | bytes 122888 | tf_op jit(solution)/shard_map/ppermute | solution.py:406
  42.8 12.0 %collective-permute-start.10 = (f32[80,128]{1,0:T(8,128)S(1)}, f32[80,128]{1,0:T(8,128)S(1)}, u32[]{:S(2)}, u32[]{:S(2)}) collective-permute-start(f32[80,128]{1,0:T(8,128)S(1)} %get-tuple-element.92), channel_id=1, source_target_pairs={{0,496},{16,32},{32,16},{48,64},{64,48},{80,96},{96,80},{112,128},... | collective-permute-start | bytes 122888 | tf_op jit(solution)/shard_map/ppermute | solution.py:416
  47.6 7.2 %collective-permute-start.11 = (f32[80,128]{1,0:T(8,128)S(1)}, f32[80,128]{1,0:T(8,128)S(1)}, u32[]{:S(2)}, u32[]{:S(2)}) collective-permute-start(f32[80,128]{1,0:T(8,128)S(1)} %get-tuple-element.93), channel_id=1, source_target_pairs={{0,16},{16,0},{32,48},{48,32},{64,80},{80,64},{96,112},{112,96},{1... | collective-permute-start | bytes 122888 | tf_op jit(solution)/shard_map/ppermute | solution.py:416
  49.7 5.4 %collective-permute-start.12 = (f32[80,128]{1,0:T(8,128)S(1)}, f32[80,128]{1,0:T(8,128)S(1)}, u32[]{:S(2)}, u32[]{:S(2)}) collective-permute-start(f32[80,128]{1,0:T(8,128)S(1)} %get-tuple-element.94), channel_id=1, source_target_pairs={{0,1},{1,2},{2,3},{3,4},{4,5},{5,6},{6,7},{7,8},{8,9},{9,10},{10,1... | collective-permute-start | bytes 122888 | tf_op jit(solution)/shard_map/ppermute | solution.py:406
  49.7 5.4 %collective-permute-start.13 = (f32[80,128]{1,0:T(8,128)S(1)}, f32[80,128]{1,0:T(8,128)S(1)}, u32[]{:S(2)}, u32[]{:S(2)}) collective-permute-start(f32[80,128]{1,0:T(8,128)S(1)} %get-tuple-element.95), channel_id=1, source_target_pairs={{0,15},{1,0},{2,1},{3,2},{4,3},{5,4},{6,5},{7,6},{8,7},{9,8},{10,9... | collective-permute-start | bytes 122888 | tf_op jit(solution)/shard_map/ppermute | solution.py:406
  56.7 5.0 %collective-permute-start.14 = (f32[80,128]{1,0:T(8,128)S(1)}, f32[80,128]{1,0:T(8,128)S(1)}, u32[]{:S(2)}, u32[]{:S(2)}) collective-permute-start(f32[80,128]{1,0:T(8,128)S(1)} %get-tuple-element.101), channel_id=1, source_target_pairs={{0,496},{16,0},{32,16},{48,32},{64,48},{80,64},{96,80},{112,96},{1... | collective-permute-start | bytes 122888 | tf_op jit(solution)/shard_map/ppermute | solution.py:406
  60.6 3.9 %collective-permute-start.15 = (f32[80,128]{1,0:T(8,128)S(1)}, f32[80,128]{1,0:T(8,128)S(1)}, u32[]{:S(2)}, u32[]{:S(2)}) collective-permute-start(f32[80,128]{1,0:T(8,128)S(1)} %get-tuple-element.102), channel_id=1, source_target_pairs={{0,1},{1,2},{2,3},{3,4},{4,5},{5,6},{6,7},{7,8},{8,9},{9,10},{10,1... | collective-permute-start | bytes 122888 | tf_op jit(solution)/shard_map/ppermute | solution.py:406

commit v9 on v7

--- a/solution.py
+++ b/solution.py
@@ -13,7 +13,7 @@
 NORM_ROOM = 1024.0
 F32 = jnp.float32
 BF16 = jnp.bfloat16
-STARTS = ("gx later", "gx first", "yz up", "yz down")
+STARTS = ("gx later", "yz up", "gx first", "yz down")
 PAIRS = [(i, j) for j in range(ITERS + 1) for i in range(j + 1)]
 VMEM_BYTES = 20 * 1024 * 1024
 

time: 97.8 us -> 97.8 us (level)
  transfers between devices with their start and end apart: 16 -> 16, of which waited for: 3 -> 2; matrix products, arithmetic and copies ran while one was open for 0% -> 0% of each run, Pallas kernels for 11% -> 11%
where the time goes in v9:
time: 97.8 us; the launch traced here: 97.3 us
  starting transfers between devices  41.3 us (42%)
  blocking collectives  32.2 us (33%)
  Pallas kernels  20.4 us (21%)
  waiting for transfers between devices  2.94 us (3%)
    all_to_all x2, blocking collectives, every(): lax.all_to_all(row.reshape(count, 1, 128), axis, 0, 0).reshape(count, 128)  32.2 us
    ppermute x10, starting transfers between devices, passed_along(): return lax.ppermute(value, axis, pairs)  21.1 us
    pallas_call x15, Pallas kernels, call(): pl.pallas_call(kernel, out_shape=out_shape, in_specs=[pl.BlockSpec(memory...  20.4 us
    ppermute x6, starting transfers between devices, exchange(): return lax.ppermute(value, axis, pairs)  20.2 us
    ppermute x10, waiting for transfers between devices, passed_along(): return lax.ppermute(value, axis, pairs)  2.93 us
  transfers between devices with their start and end apart: 16, of which 2 were waited for; matrix products, arithmetic and copies ran while one was open for 0% of the time, Pallas kernels for 11%

profile of v9, /device:TPU:1, one launch (start us, length us, event | category | flops | bytes accessed | tf_op | source)
XLA Modules:
  0.0 97.3 jit_solution(9136482910579858073)
XLA Ops:
  0.0 0.0 copy-start
  0.0 1.2 %first.1 = (f32[80,128]{1,0:T(8,128)S(1)}, f32[80,128]{1,0:T(8,128)S(1)}, s32[2,128]{1,0:T(2,128)S(1)}) custom-call(f32[80,768]{1,0:T(8,128)} %bitcast.17, s32[2,128]{1,0:T(2,128)} %bitcast.37), custom_call_target="tpu_custom_call" | custom-call | bytes 4194304 | tf_op jit(solution)/shard_map/first/pallas_call | solution.py:423
  1.3 3.5 %collective-permute-start = (f32[80,128]{1,0:T(8,128)S(1)}, f32[80,128]{1,0:T(8,128)S(1)}, u32[]{:S(2)}, u32[]{:S(2)}) collective-permute-start(f32[80,128]{1,0:T(8,128)S(1)} %get-tuple-element.59.refs_4_), channel_id=1, source_target_pairs={{0,1},{1,2},{2,3},{3,4},{4,5},{5,6},{6,7},{7,8},{8,9},{9,10},{10,1... | collective-permute-start | bytes 122888 | tf_op jit(solution)/shard_map/ppermute | solution.py:395
  4.7 3.1 %collective-permute-start.1 = (f32[80,128]{1,0:T(8,128)S(1)}, f32[80,128]{1,0:T(8,128)S(1)}, u32[]{:S(2)}, u32[]{:S(2)}) collective-permute-start(f32[80,128]{1,0:T(8,128)S(1)} %get-tuple-element.60.refs_3_), channel_id=1, source_target_pairs={{0,16},{16,32},{32,48},{48,64},{64,80},{80,96},{96,112},{112,128},... | collective-permute-start | bytes 122888 | tf_op jit(solution)/shard_map/ppermute | solution.py:395
  7.9 2.3 %tables.1 = (bf16[1024,2048]{1,0:T(8,128)(2,1)S(1)}, bf16[2048,768]{1,0:T(8,128)(2,1)S(1)}, bf16[512,2048]{1,0:T(8,128)(2,1)S(1)}, bf16[2048,512]{1,0:T(8,128)(2...) custom-call(s32[4,512]{1,0:T(4,128)} %bitcast.39, ...), custom_call_target="tpu_custom_call" | custom-call | flops 1000000000 | bytes 4194304 | tf_op jit(solution)/shard_map/tables/pallas_call | solution.py:423
  10.2 0.0 copy-done
  10.2 0.7 gather.1.refs_0_
  10.9 0.0 copy-start.1
  10.9 0.0 copy-start.2
  10.9 0.1 and_select_fusion
  11.0 1.6 %weights.1 = (bf16[2,640,960]{2,1,0:T(8,128)(2,1)S(1)}, f32[1,128]{1,0:T(1,128)S(1)}) custom-call(f32[2,192,192]{2,1,0:T(8,128)S(1)} %get-tuple-element.63.inverse_ref, f32[2,192,320]{2,1,0:T(8,128)S(1)} %get-tuple-element.64.lifting_ref, f32[2,320,320]{2,1,0:T(8,128)S(1)} %get-tuple-element.65.block_ref), custom_call_target="tpu_custom_call" | custom-call | flops 1000000000 | bytes 4194304 | tf_op jit(solution)/shard_map/weights/pallas_call | solution.py:423
  12.6 0.0 collective-permute-done.refs_1_.refs_12_
  12.6 0.8 collective-permute-done.1.refs_2_
  13.4 0.1 broadcast_in_dim.4.refs_11_.refs_7_.refs_12_.refs_13_
  13.5 0.0 copy-done.1
  13.5 0.0 copy-done.2
  13.5 1.6 %step0.1 = (bf16[160,2048]{1,0:T(8,128)(2,1)S(1)}, f32[80,256]{1,0:T(8,128)S(1)}, f32[80,256]{1,0:T(8,128)S(1)}, f32[80,128]{1,0:T(8,128)S(1)}, f32[80,128]{1,0:...) custom-call(f32[80,2048]{1,0:T(8,128)S(1)} %gather.1.refs_0_, ...), custom_call_target="tpu_custom_call" | custom-call | flops 1000000000 | bytes 4194304 | tf_op jit(solution)/shard_map/step0/pallas_call | solution.py:423
  15.1 5.3 %collective-permute-start.2 = (f32[80,128]{1,0:T(8,128)S(1)}, f32[80,128]{1,0:T(8,128)S(1)}, u32[]{:S(2)}, u32[]{:S(2)}) collective-permute-start(f32[80,128]{1,0:T(8,128)S(1)} %get-tuple-element.73), channel_id=1, source_target_pairs={{0,496},{16,32},{32,16},{48,64},{64,48},{80,96},{96,80},{112,128},... | collective-permute-start | bytes 122888 | tf_op jit(solution)/shard_map/ppermute | solution.py:405
  20.4 0.3 collective-permute-start.3
  20.7 1.9 %collective-permute-start.4 = (f32[80,128]{1,0:T(8,128)S(1)}, f32[80,128]{1,0:T(8,128)S(1)}, u32[]{:S(2)}, u32[]{:S(2)}) collective-permute-start(f32[80,128]{1,0:T(8,128)S(1)} %get-tuple-element.75), channel_id=1, source_target_pairs={{0,16},{16,0},{32,48},{48,32},{64,80},{80,64},{96,112},{112,96},{1... | collective-permute-start | bytes 122888 | tf_op jit(solution)/shard_map/ppermute | solution.py:405
  22.6 3.1 %collective-permute-start.5 = (f32[80,128]{1,0:T(8,128)S(1)}, f32[80,128]{1,0:T(8,128)S(1)}, u32[]{:S(2)}, u32[]{:S(2)}) collective-permute-start(f32[80,128]{1,0:T(8,128)S(1)} %get-tuple-element.76), channel_id=1, source_target_pairs={{0,15},{1,0},{2,1},{3,2},{4,3},{5,4},{6,5},{7,6},{8,7},{9,8},{10,9... | collective-permute-start | bytes 122888 | tf_op jit(solution)/shard_map/ppermute | solution.py:395
  25.7 1.7 %between0.1 = (f32[8,128]{1,0:T(8,128)S(1)}, f32[80,768]{1,0:T(8,128)S(1)}, f32[80,2048]{1,0:T(8,128)S(1)}) custom-call(bf16[160,2048]{1,0:T(8,128)(2,1)S(1)} %get-tuple-element.68.refs_0_, f32[80,768]{1,0:T(8,128)S(1)} %bitcast.19, f32[80,256]{1,0:T(8,128)S(1)} %get-tuple-element.69.refs_2_.refs_14_, ...), custom_call_target="tpu_custom_call" | custom-call | flops 1000000000 | bytes 4194304 | tf_op jit(solution)/shard_map/between0/pallas_call | solution.py:423
  27.5 0.0 collective-permute-done.2.refs_1_.refs_2_
  27.5 0.0 collective-permute-done.3.refs_2_.refs_3_.refs_13_
  27.5 0.0 collective-permute-done.4.refs_3_.refs_4_
  27.5 0.0 collective-permute-done.5.refs_4_.refs_5_
  27.5 1.7 %step1.1 = (bf16[160,2048]{1,0:T(8,128)(2,1)S(1)}, f32[80,256]{1,0:T(8,128)S(1)}, f32[80,256]{1,0:T(8,128)S(1)}, f32[80,128]{1,0:T(8,128)S(1)}, f32[80,128]{1,0:...) custom-call(f32[80,2048]{1,0:T(8,128)S(1)} %get-tuple-element.72.refs_0_, ...), custom_call_target="tpu_custom_call" | custom-call | flops 1000000000 | bytes 4194304 | tf_op jit(solution)/shard_map/step1/pallas_call | solution.py:423
  29.3 4.1 %collective-permute-start.6 = (f32[80,128]{1,0:T(8,128)S(1)}, f32[80,128]{1,0:T(8,128)S(1)}, u32[]{:S(2)}, u32[]{:S(2)}) collective-permute-start(f32[80,128]{1,0:T(8,128)S(1)} %get-tuple-element.82), channel_id=1, source_target_pairs={{0,496},{16,32},{32,16},{48,64},{64,48},{80,96},{96,80},{112,128},... | collective-permute-start | bytes 122888 | tf_op jit(solution)/shard_map/ppermute | solution.py:405
  33.4 0.9 collective-permute-start.7
  34.3 1.9 %collective-permute-start.8 = (f32[80,128]{1,0:T(8,128)S(1)}, f32[80,128]{1,0:T(8,128)S(1)}, u32[]{:S(2)}, u32[]{:S(2)}) collective-permute-start(f32[80,128]{1,0:T(8,128)S(1)} %get-tuple-element.84), channel_id=1, source_target_pairs={{0,16},{16,0},{32,48},{48,32},{64,80},{80,64},{96,112},{112,96},{1... | collective-permute-start | bytes 122888 | tf_op jit(solution)/shard_map/ppermute | solution.py:405
  36.2 2.4 %collective-permute-start.9 = (f32[80,128]{1,0:T(8,128)S(1)}, f32[80,128]{1,0:T(8,128)S(1)}, u32[]{:S(2)}, u32[]{:S(2)}) collective-permute-start(f32[80,128]{1,0:T(8,128)S(1)} %get-tuple-element.85), channel_id=1, source_target_pairs={{0,15},{1,0},{2,1},{3,2},{4,3},{5,4},{6,5},{7,6},{8,7},{9,8},{10,9... | collective-permute-start | bytes 122888 | tf_op jit(solution)/shard_map/ppermute | solution.py:395
  38.6 1.8 %between1.1 = (f32[80,768]{1,0:T(8,128)S(1)}, f32[8,128]{1,0:T(8,128)S(1)}, f32[80,768]{1,0:T(8,128)S(1)}, f32[80,2048]{1,0:T(8,128)S(1)}) custom-call(bf16[160,2048]{1,0:T(8,128)(2,1)S(1)} %get-tuple-element.78.refs_0_, f32[80,768]{1,0:T(8,128)S(1)} %get-tuple-element.79.refs_1_, f32[80,128]{1,0:T(8,128)S(1)} %collective-permute-done.2.refs_1_.refs_2_, ...), custom_call_target="tpu_custom_call" | custom-call | flops 1000000000 | bytes 4194304 | tf_op jit(solution)/shard_map/between1/pallas_call | solution.py:423
  40.4 0.0 collective-permute-done.6.refs_1_.refs_2_
  40.4 0.0 collective-permute-done.7.refs_2_.refs_3_.refs_15_
  40.4 0.0 collective-permute-done.8.refs_3_.refs_4_
  40.4 0.0 collective-permute-done.9.refs_4_.refs_5_
  40.5 1.7 %step2.1 = (bf16[160,2048]{1,0:T(8,128)(2,1)S(1)}, f32[80,256]{1,0:T(8,128)S(1)}, f32[80,256]{1,0:T(8,128)S(1)}, f32[80,128]{1,0:T(8,128)S(1)}, f32[80,128]{1,0:...) custom-call(f32[80,2048]{1,0:T(8,128)S(1)} %get-tuple-element.81.refs_0_, ...), custom_call_target="tpu_custom_call" | custom-call | flops 1000000000 | bytes 4194304 | tf_op jit(solution)/shard_map/step2/pallas_call | solution.py:423
  42.2 4.8 %collective-permute-start.10 = (f32[80,128]{1,0:T(8,128)S(1)}, f32[80,128]{1,0:T(8,128)S(1)}, u32[]{:S(2)}, u32[]{:S(2)}) collective-permute-start(f32[80,128]{1,0:T(8,128)S(1)} %get-tuple-element.92), channel_id=1, source_target_pairs={{0,496},{16,32},{32,16},{48,64},{64,48},{80,96},{96,80},{112,128},... | collective-permute-start | bytes 122888 | tf_op jit(solution)/shard_map/ppermute | solution.py:405
  47.0 0.4 collective-permute-start.11
  47.4 2.1 %collective-permute-start.12 = (f32[80,128]{1,0:T(8,128)S(1)}, f32[80,128]{1,0:T(8,128)S(1)}, u32[]{:S(2)}, u32[]{:S(2)}) collective-permute-start(f32[80,128]{1,0:T(8,128)S(1)} %get-tuple-element.94), channel_id=1, source_target_pairs={{0,16},{16,0},{32,48},{48,32},{64,80},{80,64},{96,112},{112,96},{1... | collective-permute-start | bytes 122888 | tf_op jit(solution)/shard_map/ppermute | solution.py:405
  49.5 2.8 %collective-permute-start.13 = (f32[80,128]{1,0:T(8,128)S(1)}, f32[80,128]{1,0:T(8,128)S(1)}, u32[]{:S(2)}, u32[]{:S(2)}) collective-permute-start(f32[80,128]{1,0:T(8,128)S(1)} %get-tuple-element.95), channel_id=1, source_target_pairs={{0,15},{1,0},{2,1},{3,2},{4,3},{5,4},{6,5},{7,6},{8,7},{9,8},{10,9... | collective-permute-start | bytes 122888 | tf_op jit(solution)/shard_map/ppermute | solution.py:395
  52.3 1.8 %between2.1 = (f32[80,768]{1,0:T(8,128)S(1)}, f32[8,128]{1,0:T(8,128)S(1)}, f32[80,768]{1,0:T(8,128)S(1)}, f32[80,2048]{1,0:T(8,128)S(1)}) custom-call(bf16[160,2048]{1,0:T(8,128)(2,1)S(1)} %get-tuple-element.87.refs_0_, f32[80,768]{1,0:T(8,128)S(1)} %get-tuple-element.88.refs_1_, f32[80,128]{1,0:T(8,128)S(1)} %collective-permute-done.6.refs_1_.refs_2_, ...), custom_call_target="tpu_custom_call" | custom-call | flops 1000000000 | bytes 4194304 | tf_op jit(solution)/shard_map/between2/pallas_call | solution.py:423
  54.1 0.0 collective-permute-done.10.refs_1_.refs_2_
  54.1 0.0 collective-permute-done.11.refs_2_.refs_3_.refs_17_
  54.1 0.0 collective-permute-done.12.refs_3_.refs_4_
  54.1 0.0 collective-permute-done.13.refs_4_.refs_5_
  54.1 1.6 %step3.1 = (bf16[160,2048]{1,0:T(8,128)(2,1)S(1)}, f32[80,128]{1,0:T(8,128)S(1)}, f32[80,128]{1,0:T(8,128)S(1)}) custom-call(f32[80,2048]{1,0:T(8,128)S(1)} %get-tuple-element.91.refs_0_, f32[80,128]{1,0:T(8,128)S(1)} %collective-permute-done.10.refs_1_.refs_2_, f32[80,128]{1,0:T(8,128)S(1)} %collective-permute-done.11.refs_2_.refs_3_.refs_17_, ...), custom_call_target="tpu_custom_call" | custom-call | flops 1000000000 | bytes 4194304 | tf_op jit(solution)/shard_map/step3/pallas_call | solution.py:423
  55.8 3.9 %collective-permute-start.14 = (f32[80,128]{1,0:T(8,128)S(1)}, f32[80,128]{1,0:T(8,128)S(1)}, u32[]{:S(2)}, u32[]{:S(2)}) collective-permute-start(f32[80,128]{1,0:T(8,128)S(1)} %get-tuple-element.101), channel_id=1, source_target_pairs={{0,496},{16,0},{32,16},{48,32},{64,48},{80,64},{96,80},{112,96},{1... | collective-permute-start | bytes 122888 | tf_op jit(solution)/shard_map/ppermute | solution.py:395
  59.7 0.8 collective-permute-start.15
  60.5 1.0 %between3.1 = (f32[80,768]{1,0:T(8,128)S(1)}, f32[8,128]{1,0:T(8,128)S(1)}, f32[80,768]{1,0:T(8,128)S(1)}, f32[80,128]{1,0:T(8,128)S(1)}) custom-call(bf16[160,2048]{1,0:T(8,128)(2,1)S(1)} %get-tuple-element.97.refs_0_, f32[80,768]{1,0:T(8,128)S(1)} %get-tuple-element.98.refs_1_, f32[80,128]{1,0:T(8,128)S(1)} %collective-permute-done.10.refs_1_.refs_2_, ...), custom_call_target="tpu_custom_call" | custom-call | flops 1000000000 | bytes 4194304 | tf_op jit(solution)/shard_map/between3/pallas_call | solution.py:423
  61.5 0.0 collective-permute-done.14.refs_1_
  61.5 2.1 %collective-permute-done.15.refs_2_ = f32[80,128]{1,0:T(8,128)S(1)} collective-permute-done((f32[80,128]{1,0:T(8,128)S(1)}, f32[80,128]{1,0:T(8,128)S(1)}, u32[]{:S(2)}, u32[]{:S(2)}) %collective-permute-start.15) | collective-permute-done | bytes 40992 | tf_op jit(solution)/shard_map/ppermute | solution.py:395
  63.6 0.4 last.1
  64.0 16.0 %all_to_all.10 = f32[16,1,128]{2,1,0:T(1,128)S(1)} all-to-all(f32[16,1,128]{2,1,0:T(1,128)S(1)} %bitcast.27), channel_id=1, replica_groups=mesh['gx'=32,'yz'=16] {'yz'}, dimensions={0} | all-to-all | bytes 16384 | tf_op jit(solution)/shard_map/all_to_all | solution.py:410
  80.1 16.2 %all_to_all.11 = f32[32,1,128]{2,1,0:T(1,128)S(1)} all-to-all(f32[32,1,128]{2,1,0:T(1,128)S(1)} %bitcast.26), channel_id=1, replica_groups=mesh['gx'=32,'yz'=16] {'gx'}, dimensions={0} | all-to-all | bytes 32768 | tf_op jit(solution)/shard_map/all_to_all | solution.py:410
  96.3 1.1 %solve.1 = f32[80,768]{1,0:T(8,128)} custom-call(f32[32,128]{1,0:T(8,128)S(1)} %bitcast.25, f32[1,128]{1,0:T(1,128)S(1)} %get-tuple-element.67.refs_10_.refs_6_.refs_11_.refs_12_.scale_ref, f32[80,768]{1,0:T(8,128)S(1)} %bitcast.24, f32[80,768]{1,0:T(8,128)S(1)} %get-tuple-element.90.refs_8_.refs_7_.refs_5_.refs_1_, ...), custom_call_target="tpu_custom_call" | custom-call | bytes 4194304 | tf_op jit(solution)/shard_map/solve/pallas_call | solution.py:423
  (1 shorter events, 0.0 us)
Async XLA Ops:
  0.0 10.2 %copy-start = (f32[1,1,80,768]{3,2,1,0:T(8,128)S(1)}, f32[1,1,80,768]{3,2,1,0:T(8,128)}, u32[]{:S(2)}) copy-start(f32[1,1,80,768]{3,2,1,0:T(8,128)} %param.8) | copy-start | bytes 737284
  1.3 11.4 %collective-permute-start = (f32[80,128]{1,0:T(8,128)S(1)}, f32[80,128]{1,0:T(8,128)S(1)}, u32[]{:S(2)}, u32[]{:S(2)}) collective-permute-start(f32[80,128]{1,0:T(8,128)S(1)} %get-tuple-element.59.refs_4_), channel_id=1, source_target_pairs={{0,1},{1,2},{2,3},{3,4},{4,5},{5,6},{6,7},{7,8},{8,9},{9,10},{10,1... | collective-permute-start | bytes 122888 | tf_op jit(solution)/shard_map/ppermute | solution.py:395
  4.7 8.7 %collective-permute-start.1 = (f32[80,128]{1,0:T(8,128)S(1)}, f32[80,128]{1,0:T(8,128)S(1)}, u32[]{:S(2)}, u32[]{:S(2)}) collective-permute-start(f32[80,128]{1,0:T(8,128)S(1)} %get-tuple-element.60.refs_3_), channel_id=1, source_target_pairs={{0,16},{16,32},{32,48},{48,64},{64,80},{80,96},{96,112},{112,128},... | collective-permute-start | bytes 122888 | tf_op jit(solution)/shard_map/ppermute | solution.py:395
  10.9 2.6 %copy-start.1 = (f32[1,1,512]{2,1,0:T(1,128)S(1)}, f32[1,1,512]{2,1,0:T(1,128)}, u32[]{:S(2)}) copy-start(f32[1,1,512]{2,1,0:T(1,128)} %param.11) | copy-start | bytes 6148
  10.9 2.6 %copy-start.2 = (f32[1,1,512]{2,1,0:T(1,128)S(1)}, f32[1,1,512]{2,1,0:T(1,128)}, u32[]{:S(2)}) copy-start(f32[1,1,512]{2,1,0:T(1,128)} %param.12) | copy-start | bytes 6148
  15.1 12.4 %collective-permute-start.2 = (f32[80,128]{1,0:T(8,128)S(1)}, f32[80,128]{1,0:T(8,128)S(1)}, u32[]{:S(2)}, u32[]{:S(2)}) collective-permute-start(f32[80,128]{1,0:T(8,128)S(1)} %get-tuple-element.73), channel_id=1, source_target_pairs={{0,496},{16,32},{32,16},{48,64},{64,48},{80,96},{96,80},{112,128},... | collective-permute-start | bytes 122888 | tf_op jit(solution)/shard_map/ppermute | solution.py:405
  20.4 7.1 %collective-permute-start.3 = (f32[80,128]{1,0:T(8,128)S(1)}, f32[80,128]{1,0:T(8,128)S(1)}, u32[]{:S(2)}, u32[]{:S(2)}) collective-permute-start(f32[80,128]{1,0:T(8,128)S(1)} %get-tuple-element.74), channel_id=1, source_target_pairs={{0,1},{1,2},{2,3},{3,4},{4,5},{5,6},{6,7},{7,8},{8,9},{9,10},{10,1... | collective-permute-start | bytes 122888 | tf_op jit(solution)/shard_map/ppermute | solution.py:395
  20.7 6.8 %collective-permute-start.4 = (f32[80,128]{1,0:T(8,128)S(1)}, f32[80,128]{1,0:T(8,128)S(1)}, u32[]{:S(2)}, u32[]{:S(2)}) collective-permute-start(f32[80,128]{1,0:T(8,128)S(1)} %get-tuple-element.75), channel_id=1, source_target_pairs={{0,16},{16,0},{32,48},{48,32},{64,80},{80,64},{96,112},{112,96},{1... | collective-permute-start | bytes 122888 | tf_op jit(solution)/shard_map/ppermute | solution.py:405
  22.6 4.9 %collective-permute-start.5 = (f32[80,128]{1,0:T(8,128)S(1)}, f32[80,128]{1,0:T(8,128)S(1)}, u32[]{:S(2)}, u32[]{:S(2)}) collective-permute-start(f32[80,128]{1,0:T(8,128)S(1)} %get-tuple-element.76), channel_id=1, source_target_pairs={{0,15},{1,0},{2,1},{3,2},{4,3},{5,4},{6,5},{7,6},{8,7},{9,8},{10,9... | collective-permute-start | bytes 122888 | tf_op jit(solution)/shard_map/ppermute | solution.py:395
  29.3 11.1 %collective-permute-start.6 = (f32[80,128]{1,0:T(8,128)S(1)}, f32[80,128]{1,0:T(8,128)S(1)}, u32[]{:S(2)}, u32[]{:S(2)}) collective-permute-start(f32[80,128]{1,0:T(8,128)S(1)} %get-tuple-element.82), channel_id=1, source_target_pairs={{0,496},{16,32},{32,16},{48,64},{64,48},{80,96},{96,80},{112,128},... | collective-permute-start | bytes 122888 | tf_op jit(solution)/shard_map/ppermute | solution.py:405
  33.4 7.0 %collective-permute-start.7 = (f32[80,128]{1,0:T(8,128)S(1)}, f32[80,128]{1,0:T(8,128)S(1)}, u32[]{:S(2)}, u32[]{:S(2)}) collective-permute-start(f32[80,128]{1,0:T(8,128)S(1)} %get-tuple-element.83), channel_id=1, source_target_pairs={{0,1},{1,2},{2,3},{3,4},{4,5},{5,6},{6,7},{7,8},{8,9},{9,10},{10,1... | collective-permute-start | bytes 122888 | tf_op jit(solution)/shard_map/ppermute | solution.py:395
  34.3 6.1 %collective-permute-start.8 = (f32[80,128]{1,0:T(8,128)S(1)}, f32[80,128]{1,0:T(8,128)S(1)}, u32[]{:S(2)}, u32[]{:S(2)}) collective-permute-start(f32[80,128]{1,0:T(8,128)S(1)} %get-tuple-element.84), channel_id=1, source_target_pairs={{0,16},{16,0},{32,48},{48,32},{64,80},{80,64},{96,112},{112,96},{1... | collective-permute-start | bytes 122888 | tf_op jit(solution)/shard_map/ppermute | solution.py:405
  36.2 4.2 %collective-permute-start.9 = (f32[80,128]{1,0:T(8,128)S(1)}, f32[80,128]{1,0:T(8,128)S(1)}, u32[]{:S(2)}, u32[]{:S(2)}) collective-permute-start(f32[80,128]{1,0:T(8,128)S(1)} %get-tuple-element.85), channel_id=1, source_target_pairs={{0,15},{1,0},{2,1},{3,2},{4,3},{5,4},{6,5},{7,6},{8,7},{9,8},{10,9... | collective-permute-start | bytes 122888 | tf_op jit(solution)/shard_map/ppermute | solution.py:395
  42.2 11.9 %collective-permute-start.10 = (f32[80,128]{1,0:T(8,128)S(1)}, f32[80,128]{1,0:T(8,128)S(1)}, u32[]{:S(2)}, u32[]{:S(2)}) collective-permute-start(f32[80,128]{1,0:T(8,128)S(1)} %get-tuple-element.92), channel_id=1, source_target_pairs={{0,496},{16,32},{32,16},{48,64},{64,48},{80,96},{96,80},{112,128},... | collective-permute-start | bytes 122888 | tf_op jit(solution)/shard_map/ppermute | solution.py:405
  47.0 7.1 %collective-permute-start.11 = (f32[80,128]{1,0:T(8,128)S(1)}, f32[80,128]{1,0:T(8,128)S(1)}, u32[]{:S(2)}, u32[]{:S(2)}) collective-permute-start(f32[80,128]{1,0:T(8,128)S(1)} %get-tuple-element.93), channel_id=1, source_target_pairs={{0,1},{1,2},{2,3},{3,4},{4,5},{5,6},{6,7},{7,8},{8,9},{9,10},{10,1... | collective-permute-start | bytes 122888 | tf_op jit(solution)/shard_map/ppermute | solution.py:395
  47.4 6.7 %collective-permute-start.12 = (f32[80,128]{1,0:T(8,128)S(1)}, f32[80,128]{1,0:T(8,128)S(1)}, u32[]{:S(2)}, u32[]{:S(2)}) collective-permute-start(f32[80,128]{1,0:T(8,128)S(1)} %get-tuple-element.94), channel_id=1, source_target_pairs={{0,16},{16,0},{32,48},{48,32},{64,80},{80,64},{96,112},{112,96},{1... | collective-permute-start | bytes 122888 | tf_op jit(solution)/shard_map/ppermute | solution.py:405
  49.5 4.6 %collective-permute-start.13 = (f32[80,128]{1,0:T(8,128)S(1)}, f32[80,128]{1,0:T(8,128)S(1)}, u32[]{:S(2)}, u32[]{:S(2)}) collective-permute-start(f32[80,128]{1,0:T(8,128)S(1)} %get-tuple-element.95), channel_id=1, source_target_pairs={{0,15},{1,0},{2,1},{3,2},{4,3},{5,4},{6,5},{7,6},{8,7},{9,8},{10,9... | collective-permute-start | bytes 122888 | tf_op jit(solution)/shard_map/ppermute | solution.py:395
  55.8 5.7 %collective-permute-start.14 = (f32[80,128]{1,0:T(8,128)S(1)}, f32[80,128]{1,0:T(8,128)S(1)}, u32[]{:S(2)}, u32[]{:S(2)}) collective-permute-start(f32[80,128]{1,0:T(8,128)S(1)} %get-tuple-element.101), channel_id=1, source_target_pairs={{0,496},{16,0},{32,16},{48,32},{64,48},{80,64},{96,80},{112,96},{1... | collective-permute-start | bytes 122888 | tf_op jit(solution)/shard_map/ppermute | solution.py:395
  59.7 3.9 %collective-permute-start.15 = (f32[80,128]{1,0:T(8,128)S(1)}, f32[80,128]{1,0:T(8,128)S(1)}, u32[]{:S(2)}, u32[]{:S(2)}) collective-permute-start(f32[80,128]{1,0:T(8,128)S(1)} %get-tuple-element.102), channel_id=1, source_target_pairs={{0,1},{1,2},{2,3},{3,4},{4,5},{5,6},{6,7},{7,8},{8,9},{9,10},{10,1... | collective-permute-start | bytes 122888 | tf_op jit(solution)/shard_map/ppermute | solution.py:395
